TPU v7x, 32 devices: a whole 2x2x4 slice. The times are simulated.
32 devices in a mesh: rows: 4 (over x, core), heads: 8 (over z, y).
Axes of the slice: x: 2, y: 2, z: 4, core: 2. Of those that a mesh axis runs over, the one named last changes fastest.
Arguments:
- tokens: bfloat16 [24576, 1024], P(('rows', 'heads')), may hold values from -6 to 6
- cotangent: bfloat16 [24576, 1024], P(('rows', 'heads')), may hold values from -6 to 6
- domain: int32 [12], P('rows'), may hold values from 0 to 3
- group_weight: float32 [4], replicated, may hold values from 0.25 to 4
- gain_attn: bfloat16 [1024], replicated, may hold values from 0.5 to 1.5
- w_query: bfloat16 [1024, 1024], P(None, 'heads'), may hold values from -0.25 to 0.25
- w_query_rope: bfloat16 [1024, 512], P(None, 'heads'), may hold values from -0.25 to 0.25
- w_latent: bfloat16 [1024, 512], replicated, may hold values from -0.1875 to 0.1875
- w_key_rope: bfloat16 [1024, 32], replicated, may hold values from -0.1875 to 0.1875
- w_key_up: bfloat16 [256, 1024], P(None, 'heads'), may hold values from -0.375 to 0.375
- w_value_up: bfloat16 [256, 1024], P(None, 'heads'), may hold values from -0.375 to 0.375
- w_out: bfloat16 [1024, 1024], P('heads'), may hold values from -0.75 to 0.75
- gain_mlp: bfloat16 [1024], replicated, may hold values from 0.5 to 1.5
- w_gate: bfloat16 [1024, 2816], P(None, 'heads'), may hold values from -0.1875 to 0.1875
- w_up: bfloat16 [1024, 2816], P(None, 'heads'), may hold values from -0.1875 to 0.1875
- w_down: bfloat16 [2816, 1024], P('heads'), may hold values from -0.109375 to 0.109375
Outputs:
- block_output: bfloat16 [24576, 1024], P(('rows', 'heads'))
- grad_tokens: float32 [24576, 1024], P(('rows', 'heads'))
- grad_gain_attn: float32 [1024], P(('rows', 'heads'))
- grad_query: float32 [1024, 1024], P('rows', 'heads')
- grad_query_rope: float32 [1024, 512], P('rows', 'heads')
- grad_latent: float32 [1024, 512], P(('rows', 'heads'))
- grad_key_rope: float32 [1024, 32], P(('rows', 'heads'))
- grad_key_up: float32 [256, 1024], P('rows', 'heads')
- grad_value_up: float32 [256, 1024], P('rows', 'heads')
- grad_out: float32 [1024, 1024], P('heads', 'rows')
- grad_gain_mlp: float32 [1024], P(('rows', 'heads'))
- grad_gate: float32 [1024, 2816], P('rows', 'heads')
- grad_up: float32 [1024, 2816], P('rows', 'heads')
- grad_down: float32 [2816, 1024], P('heads', 'rows')
All inputs are finite; a program needn't handle non-finite values.
Results may differ from a plain program's by a relative error of at most 0.018.
Values may be sent and summed in bfloat16 or wider, within the bound.
A program may use at most 256 MiB of HBM per device.

v0:
```python
import jax
import jax.numpy as jnp
from jax import lax
from jax.sharding import PartitionSpec as P

D = 1024
HEADS = 16
HD = 64
LGROUPS = 2
LAT = 256
RD = 32
LEN = 2048


EPS = 1e-05
THETA = 10000.0
NEG_LARGE = -1e30


def rms_scale(values):
    return lax.rsqrt(jnp.mean(values * values, axis=-1, keepdims=True) + EPS)


def rotary(row_count, seq_len, half_dim):
    positions = (jnp.arange(row_count) % seq_len).astype(jnp.float32)
    frequency = THETA ** (-jnp.arange(half_dim).astype(jnp.float32) / half_dim)
    angles = positions[:, None] * frequency[None, :]
    return (jnp.cos(angles), jnp.sin(angles))


def rotate(values, cosine, sine_table):
    half_dim = values.shape[-1] // 2
    front_half = values[..., :half_dim]
    back_half = values[..., half_dim:]
    return jnp.concatenate(
        [
            front_half * cosine - back_half * sine_table,
            back_half * cosine + front_half * sine_table,
        ],
        axis=-1,
    )


def round_trip(values):
    return lax.optimization_barrier(values.astype(jnp.bfloat16)).astype(jnp.float32)


def norm_backward(source, scale_rows, gain, grad_normed):
    scaled = source * scale_rows
    weighted = grad_normed * gain
    grad_source = scale_rows * (
        weighted - scaled * jnp.mean(weighted * scaled, axis=-1, keepdims=True)
    )
    return (grad_source, jnp.sum(grad_normed * scaled, axis=0))


def silu_grads(grad_inner, gate_act, up_act):
    sigmoid_gate = jax.nn.sigmoid(gate_act)
    grad_gate = grad_inner * up_act * sigmoid_gate * (1.0 + gate_act * (1.0 - sigmoid_gate))
    grad_upper = grad_inner * gate_act * sigmoid_gate
    return (grad_gate.astype(jnp.bfloat16), grad_upper.astype(jnp.bfloat16))


def block_scores(query_block, rope_block, key_seq, key_rope_seq, offset, score_scale):
    scores = jnp.einsum("qhd,khd->hqk", query_block, key_seq, preferred_element_type=jnp.float32)
    scores = scores + jnp.einsum(
        "qhr,kr->hqk", rope_block, key_rope_seq, preferred_element_type=jnp.float32
    )
    scores = scores * score_scale
    rows_at = offset + jnp.arange(query_block.shape[0])
    cols_at = jnp.arange(key_seq.shape[0])
    return jnp.where((cols_at[None, :] <= rows_at[:, None])[None], scores, NEG_LARGE)


def attend_forward(query_heads, query_rope, key_heads, value_heads, key_rope, score_scale):
    row_count, heads_here = (query_heads.shape[0], query_heads.shape[1])
    seq_count = row_count // LEN
    block_rows = min(512, LEN)
    blocks = LEN // block_rows

    def attend_one_block(block_index):
        seq_start = block_index // blocks * LEN
        offset = block_index % blocks * block_rows
        query_block = lax.dynamic_slice_in_dim(query_heads, seq_start + offset, block_rows, 0)
        rope_block = lax.dynamic_slice_in_dim(query_rope, seq_start + offset, block_rows, 0)
        key_seq = lax.dynamic_slice_in_dim(key_heads, seq_start, LEN, 0)
        value_seq = lax.dynamic_slice_in_dim(value_heads, seq_start, LEN, 0)
        key_rope_seq = lax.dynamic_slice_in_dim(key_rope, seq_start, LEN, 0)
        scores = block_scores(query_block, rope_block, key_seq, key_rope_seq, offset, score_scale)
        row_max = jnp.max(scores, axis=-1, keepdims=True)
        exp_terms = jnp.exp(scores - row_max)
        row_total = jnp.sum(exp_terms, axis=-1, keepdims=True)
        attention = (exp_terms / row_total).astype(jnp.bfloat16)
        output = jnp.einsum(
            "hqk,khd->qhd", attention, value_seq, preferred_element_type=jnp.float32
        )
        return (output.astype(jnp.bfloat16), (row_max + jnp.log(row_total))[..., 0])

    outputs, log_totals = lax.map(attend_one_block, jnp.arange(seq_count * blocks))
    return (
        outputs.reshape(row_count, heads_here, -1),
        log_totals.transpose(0, 2, 1).reshape(row_count, heads_here),
    )


def attend_backward(
    query_heads, query_rope, key_heads, value_heads, key_rope, log_totals, grad_mixed, score_scale
):
    row_count, heads_here = (query_heads.shape[0], query_heads.shape[1])
    head_dim = query_heads.shape[2]
    rope_dim = query_rope.shape[2]
    seq_count = row_count // LEN
    block_rows = min(512, LEN)
    blocks = LEN // block_rows

    def one_seq(seq_index):
        seq_start = seq_index * LEN
        key_seq = lax.dynamic_slice_in_dim(key_heads, seq_start, LEN, 0)
        value_seq = lax.dynamic_slice_in_dim(value_heads, seq_start, LEN, 0)
        key_rope_seq = lax.dynamic_slice_in_dim(key_rope, seq_start, LEN, 0)

        def one_one_block(totals, block_index):
            grad_keys, grad_values, grad_key_rope = totals
            offset = block_index * block_rows
            begin_row = seq_start + offset
            query_block = lax.dynamic_slice_in_dim(query_heads, begin_row, block_rows, 0)
            rope_block = lax.dynamic_slice_in_dim(query_rope, begin_row, block_rows, 0)
            log_block = lax.dynamic_slice_in_dim(log_totals, begin_row, block_rows, 0)
            grad_block = lax.dynamic_slice_in_dim(grad_mixed, begin_row, block_rows, 0)
            scores = block_scores(
                query_block, rope_block, key_seq, key_rope_seq, offset, score_scale
            )
            attention = jnp.exp(scores - log_block.T[:, :, None])
            grad_attention = jnp.einsum(
                "qhd,khd->hqk", grad_block, value_seq, preferred_element_type=jnp.float32
            )
            row_inner = jnp.sum(grad_attention * attention, axis=-1, keepdims=True)
            grad_scores = (attention * (grad_attention - row_inner)).astype(jnp.bfloat16)
            grad_query = (
                jnp.einsum("hqk,khd->qhd", grad_scores, key_seq, preferred_element_type=jnp.float32)
                * score_scale
            )
            grad_query_rope = (
                jnp.einsum(
                    "hqk,kr->qhr", grad_scores, key_rope_seq, preferred_element_type=jnp.float32
                )
                * score_scale
            )
            grad_keys = (
                grad_keys
                + jnp.einsum(
                    "hqk,qhd->khd", grad_scores, query_block, preferred_element_type=jnp.float32
                )
                * score_scale
            )
            grad_key_rope = (
                grad_key_rope
                + jnp.einsum(
                    "hqk,qhr->khr", grad_scores, rope_block, preferred_element_type=jnp.float32
                )
                * score_scale
            )
            grad_values = grad_values + jnp.einsum(
                "hqk,qhd->khd",
                attention.astype(jnp.bfloat16),
                grad_block,
                preferred_element_type=jnp.float32,
            )
            return ((grad_keys, grad_values, grad_key_rope), (grad_query, grad_query_rope))

        initial = (
            jnp.zeros((LEN, heads_here, head_dim), jnp.float32),
            jnp.zeros((LEN, heads_here, head_dim), jnp.float32),
            jnp.zeros((LEN, heads_here, rope_dim), jnp.float32),
        )
        totals, (grad_query, grad_query_rope) = lax.scan(one_one_block, initial, jnp.arange(blocks))
        return (
            totals[0],
            totals[1],
            totals[2],
            grad_query.reshape(LEN, heads_here, head_dim),
            grad_query_rope.reshape(LEN, heads_here, rope_dim),
        )

    results = lax.map(one_seq, jnp.arange(seq_count))
    return tuple((result.reshape((row_count,) + result.shape[2:]) for result in results))


def on_device(
    tokens,
    cotangent,
    domain,
    group_weight,
    gain_attn,
    w_query,
    w_query_rope,
    w_latent,
    w_key_rope,
    w_key_up,
    w_value_up,
    w_out,
    gain_mlp,
    w_gate,
    w_up,
    w_down,
):
    heads_here = w_query.shape[1] // HD
    head_first = lax.axis_index("heads") * heads_here
    group_index = head_first // (HEADS // LGROUPS)
    local_rows = tokens.shape[0]
    score_scale = (HD + RD) ** (-0.5)
    source = tokens.astype(jnp.float32)
    scale_attn = rms_scale(source)
    gain_one = gain_attn.astype(jnp.float32)
    normed = (source * scale_attn * gain_one).astype(jnp.bfloat16)
    gathered = lax.all_gather(normed, "heads", axis=0, tiled=True)
    total_rows = gathered.shape[0]
    latent_weight = lax.dynamic_slice_in_dim(w_latent, group_index * LAT, LAT, 1)
    project_weight = jnp.concatenate([w_query, w_query_rope, latent_weight, w_key_rope], axis=1)
    projected = jnp.dot(gathered, project_weight, preferred_element_type=jnp.float32)
    cut_query = heads_here * HD
    cut_rope = cut_query + heads_here * RD
    cut_latent = cut_rope + LAT
    cosine, sine_table = rotary(total_rows, LEN, RD // 2)
    head_cosine = cosine[:, None, :]
    head_sine = sine_table[:, None, :]
    query_heads = projected[:, :cut_query].astype(jnp.bfloat16).reshape(total_rows, heads_here, HD)
    query_rope = rotate(
        projected[:, cut_query:cut_rope].reshape(total_rows, heads_here, RD), head_cosine, head_sine
    ).astype(jnp.bfloat16)
    latent = projected[:, cut_rope:cut_latent].astype(jnp.bfloat16)
    key_rope = rotate(projected[:, cut_latent:], cosine, sine_table).astype(jnp.bfloat16)
    up_weight = jnp.concatenate(
        [w_key_up.reshape(LAT, heads_here, HD), w_value_up.reshape(LAT, heads_here, HD)], axis=2
    )
    keys_values = jnp.dot(
        latent, up_weight.reshape(LAT, heads_here * 2 * HD), preferred_element_type=jnp.float32
    )
    keys_values = keys_values.astype(jnp.bfloat16).reshape(total_rows, heads_here, 2 * HD)
    key_heads = keys_values[:, :, :HD]
    value_heads = keys_values[:, :, HD:]
    mixed_heads, log_totals = attend_forward(
        query_heads, query_rope, key_heads, value_heads, key_rope, score_scale
    )
    mixed_flat = mixed_heads.reshape(total_rows, heads_here * HD)
    hidden = source + lax.psum_scatter(
        jnp.dot(mixed_flat, w_out, preferred_element_type=jnp.float32),
        "heads",
        scatter_dimension=0,
        tiled=True,
    )
    scale_mlp = rms_scale(hidden)
    gain_two = gain_mlp.astype(jnp.float32)
    normed_mlp = (hidden * scale_mlp * gain_two).astype(jnp.bfloat16)
    width_here = w_gate.shape[1]
    gathered_mlp = lax.all_gather(normed_mlp, "heads", axis=0, tiled=True)
    gate_up_weight = jnp.concatenate([w_gate, w_up], axis=1)
    gate_up = jnp.dot(gathered_mlp, gate_up_weight, preferred_element_type=jnp.float32)
    gate_act = gate_up[:, :width_here]
    up_act = gate_up[:, width_here:]
    inner_act = (jax.nn.silu(gate_act) * up_act).astype(jnp.bfloat16)
    mlp_local = lax.psum_scatter(
        jnp.dot(inner_act, w_down, preferred_element_type=jnp.float32).astype(jnp.bfloat16),
        "heads",
        scatter_dimension=0,
        tiled=True,
    ).astype(jnp.float32)
    block_output = (hidden + mlp_local).astype(jnp.bfloat16)
    seq_weights = jnp.sum(
        (domain[:, None] == jnp.arange(group_weight.shape[0])[None, :]).astype(jnp.float32)
        * group_weight[None, :],
        axis=1,
    )
    token_seq = (lax.axis_index("heads") * local_rows + jnp.arange(local_rows)) // LEN
    token_weight = jnp.sum(
        (token_seq[:, None] == jnp.arange(domain.shape[0])[None, :]).astype(jnp.float32)
        * seq_weights[None, :],
        axis=1,
    )
    grad_output = cotangent.astype(jnp.float32) * token_weight[:, None]
    grad_branch = grad_output.astype(jnp.bfloat16)
    grad_rows = lax.all_gather(grad_branch, "heads", axis=0, tiled=True)
    grad_inner = jnp.einsum("td,fd->tf", grad_rows, w_down, preferred_element_type=jnp.float32)
    grad_down_t = jnp.einsum("td,tf->df", grad_rows, inner_act, preferred_element_type=jnp.float32)
    grad_gate_rows, grad_up_rows = silu_grads(grad_inner, gate_act, up_act)
    grad_gate_up = jnp.concatenate([grad_gate_rows, grad_up_rows], axis=1)
    gate_up_grads = jnp.einsum(
        "td,tf->df", gathered_mlp, grad_gate_up, preferred_element_type=jnp.float32
    )
    grad_gate_w = gate_up_grads[:, :width_here]
    grad_up_w = gate_up_grads[:, width_here:]
    grad_normed_mlp = lax.psum_scatter(
        jnp.einsum("tf,df->td", grad_gate_up, gate_up_weight, preferred_element_type=jnp.float32),
        "heads",
        scatter_dimension=0,
        tiled=True,
    )
    grad_hidden_part, grad_gain_two = norm_backward(hidden, scale_mlp, gain_two, grad_normed_mlp)
    grad_hidden = grad_output + grad_hidden_part
    grad_attn_rows = lax.all_gather(grad_hidden.astype(jnp.bfloat16), "heads", axis=0, tiled=True)
    grad_mixed = jnp.einsum("td,ed->te", grad_attn_rows, w_out, preferred_element_type=jnp.float32)
    grad_mixed = grad_mixed.astype(jnp.bfloat16).reshape(total_rows, heads_here, HD)
    grad_out_t = jnp.einsum(
        "td,te->de", grad_attn_rows, mixed_flat, preferred_element_type=jnp.float32
    )
    grad_keys, grad_values, grad_key_copies, grad_query, grad_query_rope = attend_backward(
        query_heads,
        query_rope,
        key_heads,
        value_heads,
        key_rope,
        log_totals,
        grad_mixed,
        score_scale,
    )
    grad_query_back = rotate(round_trip(grad_query_rope), head_cosine, -head_sine).astype(
        jnp.bfloat16
    )
    grad_key_back = rotate(round_trip(grad_key_copies), head_cosine, -head_sine).astype(
        jnp.bfloat16
    )
    grad_kv = jnp.concatenate(
        [grad_keys.astype(jnp.bfloat16), grad_values.astype(jnp.bfloat16)], axis=2
    )
    grad_latent_heads = jnp.einsum(
        "thj,chj->thc", grad_kv, up_weight, preferred_element_type=jnp.float32
    ).astype(jnp.bfloat16)
    grad_up_weight = jnp.einsum("tc,thj->chj", latent, grad_kv, preferred_element_type=jnp.float32)
    grad_key_up_w = grad_up_weight[:, :, :HD].reshape(LAT, heads_here * HD)
    grad_value_up_w = grad_up_weight[:, :, HD:].reshape(LAT, heads_here * HD)
    grad_project = jnp.concatenate(
        [
            grad_query.astype(jnp.bfloat16).reshape(total_rows, heads_here * HD),
            grad_query_back.reshape(total_rows, heads_here * RD),
            grad_latent_heads.reshape(total_rows, heads_here * LAT),
            grad_key_back.reshape(total_rows, heads_here * RD),
        ],
        axis=1,
    )
    repeat_weight = jnp.concatenate(
        [
            w_query,
            w_query_rope,
            jnp.tile(latent_weight, (1, heads_here)),
            jnp.tile(w_key_rope, (1, heads_here)),
        ],
        axis=1,
    )
    weight_all = jnp.einsum("td,tc->dc", gathered, grad_project, preferred_element_type=jnp.float32)
    cut_back_rope = heads_here * (HD + RD)
    cut_back_latent = cut_back_rope + heads_here * LAT
    grad_query_w = weight_all[:, :cut_query]
    grad_query_rope_w = weight_all[:, cut_query:cut_back_rope]
    grad_latent_part = jnp.sum(
        weight_all[:, cut_back_rope:cut_back_latent].reshape(D, heads_here, LAT), axis=1
    )
    grad_key_rope_w = jnp.sum(weight_all[:, cut_back_latent:].reshape(D, heads_here, RD), axis=1)
    group_mask = (jnp.arange(LGROUPS) == group_index).astype(jnp.float32)
    grad_latent_full = (grad_latent_part[:, None, :] * group_mask[None, :, None]).reshape(
        D, LGROUPS * LAT
    )
    grad_normed = lax.psum_scatter(
        jnp.einsum(
            "tc,dc->td", grad_project, repeat_weight, preferred_element_type=jnp.float32
        ).astype(jnp.bfloat16),
        "heads",
        scatter_dimension=0,
        tiled=True,
    ).astype(jnp.float32)
    grad_source_part, grad_gain_one = norm_backward(source, scale_attn, gain_one, grad_normed)
    grad_tokens = grad_hidden + grad_source_part
    (
        grad_query_s,
        grad_query_rope_s,
        grad_key_up_s,
        grad_value_up_s,
        grad_gate_s,
        grad_up_s,
        grad_out_s,
        grad_down_s,
    ) = (
        lax.psum_scatter(
            grad_query_w.astype(jnp.bfloat16), "rows", scatter_dimension=0, tiled=True
        ).astype(jnp.float32),
        lax.psum_scatter(
            grad_query_rope_w.astype(jnp.bfloat16), "rows", scatter_dimension=0, tiled=True
        ).astype(jnp.float32),
        lax.psum_scatter(
            grad_key_up_w.astype(jnp.bfloat16), "rows", scatter_dimension=0, tiled=True
        ).astype(jnp.float32),
        lax.psum_scatter(
            grad_value_up_w.astype(jnp.bfloat16), "rows", scatter_dimension=0, tiled=True
        ).astype(jnp.float32),
        lax.psum_scatter(
            grad_gate_w.astype(jnp.bfloat16), "rows", scatter_dimension=0, tiled=True
        ).astype(jnp.float32),
        lax.psum_scatter(
            grad_up_w.astype(jnp.bfloat16), "rows", scatter_dimension=0, tiled=True
        ).astype(jnp.float32),
        lax.psum_scatter(
            grad_out_t.astype(jnp.bfloat16), "rows", scatter_dimension=0, tiled=True
        ).astype(jnp.float32),
        lax.psum_scatter(
            grad_down_t.astype(jnp.bfloat16), "rows", scatter_dimension=0, tiled=True
        ).astype(jnp.float32),
    )
    grad_latent_s, grad_key_rope_s, grad_gain_attn_s, grad_gain_mlp_s = (
        lax.psum_scatter(grad_latent_full, ("rows", "heads"), scatter_dimension=0, tiled=True),
        lax.psum_scatter(grad_key_rope_w, ("rows", "heads"), scatter_dimension=0, tiled=True),
        lax.psum_scatter(grad_gain_one, ("rows", "heads"), scatter_dimension=0, tiled=True),
        lax.psum_scatter(grad_gain_two, ("rows", "heads"), scatter_dimension=0, tiled=True),
    )
    return (
        block_output,
        grad_tokens,
        grad_gain_attn_s,
        grad_query_s,
        grad_query_rope_s,
        grad_latent_s,
        grad_key_rope_s,
        grad_key_up_s,
        grad_value_up_s,
        grad_out_s.T,
        grad_gain_mlp_s,
        grad_gate_s,
        grad_up_s,
        grad_down_s.T,
    )


def solution(mesh):
    in_specs = (
        P(("rows", "heads"), None),
        P(("rows", "heads"), None),
        P("rows"),
        P(),
        P(),
        P(None, "heads"),
        P(None, "heads"),
        P(),
        P(),
        P(None, "heads"),
        P(None, "heads"),
        P("heads", None),
        P(),
        P(None, "heads"),
        P(None, "heads"),
        P("heads", None),
    )
    out_specs = (
        P(("rows", "heads"), None),
        P(("rows", "heads"), None),
        P(("rows", "heads")),
        P("rows", "heads"),
        P("rows", "heads"),
        P(("rows", "heads"), None),
        P(("rows", "heads"), None),
        P("rows", "heads"),
        P("rows", "heads"),
        P("heads", "rows"),
        P(("rows", "heads")),
        P("rows", "heads"),
        P("rows", "heads"),
        P("heads", "rows"),
    )
    return jax.shard_map(
        on_device, mesh=mesh, in_specs=in_specs, out_specs=out_specs, check_vma=False
    )
```

profile of v0, /device:TPU:0, one launch (start us, length us, event | category | flops | bytes accessed | tf_op | source)
XLA Modules:
  0.0 3113.8 jit_solution(13107538641954501714)
XLA Ops:
  14.9 177.8 %all-gather.5.cloned.1.call-done = bf16[6144,1024]{1,0:T(8,128)(2,1)} async-done(((bf16[768,1024]{1,0:T(8,128)(2,1)}), bf16[6144,1024]{1,0:T(8,128)(2,1)}) %all-gather.5.cloned.1.call-update) | async-done | bytes 12582928 | tf_op jit(solution)/shard_map/all_gather | solution.py:216
  192.8 12.3 fusion.111
  210.7 3.8 fusion.87
  215.5 186.2 %while.51 = (s32[]{:T(128)}, bf16[12,512,2,64]{1,3,2,0:T(8,128)(2,1)}, f32[12,2,512]{2,1,0:T(2,128)}, s32[12]{0:T(128)S(1)}, bf16[6144,2,64]{0,2,1:T(8,128)(2,1)...) while((s32[]{:T(128)}, ...), condition=%wide.region_4.5_spmd, body=%wide.region_1.4_spmd.sunk | while | flops 691076608 | bytes 45584892 | solution.py:99
  407.1 10.1 fusion.113
  418.0 401.3 %reduce-scatter.17.cloned.1.call-done = f32[768,1024]{1,0:T(8,128)} async-done(((f32[6144,1024]{1,0:T(8,128)}), f32[768,1024]{1,0:T(8,128)}) %reduce-scatter.17.cloned.1.call-update) | async-done | bytes 3145744 | tf_op jit(solution)/shard_map/reduce_scatter | solution.py:246
  828.7 171.9 %all-gather.7.cloned.1.call-done = bf16[6144,1024]{1,0:T(8,128)(2,1)} async-done(((bf16[768,1024]{1,0:T(8,128)(2,1)}), bf16[6144,1024]{1,0:T(8,128)(2,1)}) %all-gather.7.cloned.1.call-update) | async-done | bytes 12582928 | tf_op jit(solution)/shard_map/all_gather | solution.py:256
  1000.5 15.9 fusion.114
  1016.4 160.8 %all-gather.9.cloned.1.call-done = bf16[6144,1024]{1,0:T(8,128)(2,1)} async-done(((bf16[768,1024]{1,0:T(8,128)(2,1)}), bf16[6144,1024]{1,0:T(8,128)(2,1)}) %all-gather.9.cloned.1.call-update) | async-done | bytes 12582928 | tf_op jit(solution)/shard_map/all_gather | solution.py:282
  1177.2 20.7 multiply_convert_fusion.2
  1197.9 18.9 fusion.54
  1216.9 12.1 convolution_convert_fusion.1
  1229.0 389.8 %reduce-scatter.21.cloned.1.call-done = f32[768,1024]{1,0:T(8,128)} async-done(((f32[6144,1024]{1,0:T(8,128)}), f32[768,1024]{1,0:T(8,128)}) %reduce-scatter.21.cloned.1.call-update) | async-done | bytes 3145744 | tf_op jit(solution)/shard_map/reduce_scatter | solution.py:292
  1618.9 4.3 multiply_reduce_fusion.1
  1623.2 205.7 %reduce-scatter.19.cloned.1.call-done = bf16[768,1024]{1,0:T(8,128)(2,1)} async-done(((bf16[6144,1024]{1,0:T(8,128)(2,1)}), bf16[768,1024]{1,0:T(8,128)(2,1)}) %reduce-scatter.19.cloned.1.call-update) | async-done | bytes 1572880 | tf_op jit(solution)/shard_map/reduce_scatter | solution.py:262
  1828.8 5.6 fusion.106
  1834.5 14.9 fusion.70
  1851.5 11.4 convolution_convert_fusion.5
  1863.0 147.1 %all-gather.11.cloned.1.call-done = bf16[6144,1024]{1,0:T(8,128)(2,1)} async-done(((bf16[768,1024]{1,0:T(8,128)(2,1)}), bf16[6144,1024]{1,0:T(8,128)(2,1)}) %all-gather.11.cloned.1.call-update) | async-done | bytes 12582928 | tf_op jit(solution)/shard_map/all_gather | solution.py:300
  2010.2 10.0 convolution_convert_fusion.4
  2020.2 469.1 %while.53 = (s32[]{:T(128)}, bf16[3,2048,2,64]{1,3,2,0:T(8,128)(2,1)}, bf16[3,2048,2,64]{1,3,2,0:T(8,128)(2,1)}, bf16[3,2048,2,32]{1,3,2,0:T(8,128)(2,1)}, bf16[...) while((s32[]{:T(128)}, ...), condition=%wide.region_16.17_spmd, body=%wide.region_12.16_spmd.sunk | while | flops 1768652288 | bytes 193750048 | solution.py:185
  2025.8 138.7 %while.54 = (s32[]{:T(128)}, f32[2048,2,64]{0,2,1:T(8,128)S(1)}, f32[2048,2,64]{0,2,1:T(8,128)S(1)}, f32[2048,2,32]{0,2,1:T(8,128)S(1)}, bf16[4,512,2,64]{1,3,2,...) while((s32[]{:T(128)}, f32[2048,2,64]{0,2,1:T(8,128)S(1)}, ...), condition=%wide.region_15.15_spmd.clone, body=%wide.region_13.14_spmd.clone.sunk | while | flops 1768652288 | bytes 154952144 | solution.py:176
  2037.5 5.5 multiply_reduce_fusion.5
  2043.1 8.8 multiply_convert_fusion.6
  2072.4 5.5 multiply_reduce_fusion.5
  2077.9 8.7 multiply_convert_fusion.6
  2107.0 5.5 multiply_reduce_fusion.5
  2112.5 8.6 multiply_convert_fusion.6
  2141.6 5.5 multiply_reduce_fusion.5
  2147.1 8.6 multiply_convert_fusion.6
  2182.2 138.5 %while.54 = (s32[]{:T(128)}, f32[2048,2,64]{0,2,1:T(8,128)S(1)}, f32[2048,2,64]{0,2,1:T(8,128)S(1)}, f32[2048,2,32]{0,2,1:T(8,128)S(1)}, bf16[4,512,2,64]{1,3,2,...) while((s32[]{:T(128)}, f32[2048,2,64]{0,2,1:T(8,128)S(1)}, ...), condition=%wide.region_15.15_spmd.clone, body=%wide.region_13.14_spmd.clone.sunk | while | flops 1768652288 | bytes 154952144 | solution.py:176
  2193.9 5.5 multiply_reduce_fusion.5
  2199.4 8.6 multiply_convert_fusion.6
  2228.5 5.5 multiply_reduce_fusion.5
  2234.1 8.6 multiply_convert_fusion.6
  2263.2 5.5 multiply_reduce_fusion.5
  2268.7 8.6 multiply_convert_fusion.6
  2297.8 5.5 multiply_reduce_fusion.5
  2303.3 8.6 multiply_convert_fusion.6
  2338.3 138.4 %while.54 = (s32[]{:T(128)}, f32[2048,2,64]{0,2,1:T(8,128)S(1)}, f32[2048,2,64]{0,2,1:T(8,128)S(1)}, f32[2048,2,32]{0,2,1:T(8,128)S(1)}, bf16[4,512,2,64]{1,3,2,...) while((s32[]{:T(128)}, f32[2048,2,64]{0,2,1:T(8,128)S(1)}, ...), condition=%wide.region_15.15_spmd.clone, body=%wide.region_13.14_spmd.clone.sunk | while | flops 1768652288 | bytes 154952144 | solution.py:176
  2350.1 5.5 multiply_reduce_fusion.5
  2355.6 8.6 multiply_convert_fusion.6
  2384.7 5.5 multiply_reduce_fusion.5
  2390.2 8.6 multiply_convert_fusion.6
  2419.3 5.5 multiply_reduce_fusion.5
  2424.8 8.6 multiply_convert_fusion.6
  2453.9 5.5 multiply_reduce_fusion.5
  2459.4 8.6 multiply_convert_fusion.6
  2489.3 4.2 copy.172
  2496.5 6.3 pad_maximum_fusion.4
  2502.7 4.7 copy.179
  2507.4 3.9 fusion.67
  2512.1 6.3 convolution_convert_fusion.2
  2518.4 6.2 copy.188
  2526.1 6.3 reshape.338
  2538.8 19.2 fusion.112
  2559.7 7.2 convolution_convert_fusion.6
  2571.4 18.6 convolution_convert_fusion
  2610.1 12.7 reduce-scatter.25.cloned.1.call-done
  2624.4 209.2 %reduce-scatter.23.cloned.1.call-done = bf16[768,1024]{1,0:T(8,128)(2,1)} async-done(((bf16[6144,1024]{1,0:T(8,128)(2,1)}), bf16[768,1024]{1,0:T(8,128)(2,1)}) %reduce-scatter.23.cloned.1.call-update) | async-done | bytes 1572880 | tf_op jit(solution)/shard_map/reduce_scatter | solution.py:362
  2836.1 39.6 %all-reduce.2 = (f32[1024]{0:T(1024)S(1)}, f32[1024]{0:T(1024)S(1)}) all-reduce(f32[1024]{0:T(1024)S(1)} %get-tuple-element.513, f32[1024]{0:T(1024)S(1)} %copy-done.47), channel_id=6, replica_groups=mesh['rows'=4,'heads'=8] {'rows','heads'}, use_global_device_ids=true, to_apply=%region_20.21.clone | all-reduce | flops 2048 | bytes 16384
  2876.9 5.0 fusion.61
  2881.9 87.4 %reduce-scatter.43.cloned.1.call-done = f32[32,32]{1,0:T(8,128)} async-done(((f32[1024,32]{1,0:T(8,128)}), f32[32,32]{1,0:T(8,128)}) %reduce-scatter.43.cloned.1.call-update) | async-done | bytes 4112
  2969.3 137.2 %reduce-scatter.29.cloned.1.call-done = f32[32,512]{1,0:T(8,128)} async-done(((f32[1024,512]{1,0:T(8,128)}), f32[32,512]{1,0:T(8,128)}) %reduce-scatter.29.cloned.1.call-update) | async-done | bytes 65552 | tf_op jit(solution)/shard_map/reduce_scatter | solution.py:408
  (642 shorter events, 515.7 us)
Async XLA Ops:
  7.2 7.7 copy-start
  7.2 185.6 %all-gather.5.cloned.1.call-start = ((), (), s32[]{:S(2)}) async-start(), calls=%async_computation.14 | async-start | bytes 14155776 | tf_op jit(solution)/shard_map/all_gather | solution.py:216
  8.0 5.6 copy-start.45
  8.0 5.8 copy-start.46
  9.8 4.5 copy-start.40
  13.5 179.3 %copy-start.50 = (bf16[1024,128]{1,0:T(8,128)(2,1)S(1)}, bf16[1024,128]{1,0:T(8,128)(2,1)}, u32[]{:S(2)}) copy-start(bf16[1024,128]{1,0:T(8,128)(2,1)} %param.27) | copy-start | bytes 786436
  13.5 805.8 %reduce-scatter.17.cloned.1.call-start = ((), (), s32[]{:S(2)}) async-start(), calls=%async_computation.15 | async-start | bytes 28311552 | tf_op jit(solution)/shard_map/reduce_scatter | solution.py:246
  14.5 190.5 %copy-start.38 = (bf16[1024,64]{1,0:T(8,128)(2,1)}, bf16[1024,64]{1,0:T(8,128)(2,1)S(1)}, u32[]{:S(2)}) copy-start(bf16[1024,64]{1,0:T(8,128)(2,1)S(1)} %copy.160) | copy-start | bytes 393220
  14.9 190.1 %copy-start.19 = (bf16[1024,256]{1,0:T(8,128)(2,1)}, bf16[1024,256]{1,0:T(8,128)(2,1)S(1)}, u32[]{:S(2)}) copy-start(bf16[1024,256]{1,0:T(8,128)(2,1)S(1)} %constant_dynamic-slice_fusion.3) | copy-start | bytes 1572868
  401.7 5.4 copy-start.35
  417.3 402.0 %copy-start.8 = (bf16[768,1024]{1,0:T(8,128)(2,1)S(1)}, bf16[768,1024]{1,0:T(8,128)(2,1)}, u32[]{:S(2)}) copy-start(bf16[768,1024]{1,0:T(8,128)(2,1)} %param.22) | copy-start | bytes 4718596
  417.3 583.2 %all-gather.7.cloned.1.call-start = ((), (), s32[]{:S(2)}) async-start(), calls=%async_computation.16 | async-start | bytes 14155776 | tf_op jit(solution)/shard_map/all_gather | solution.py:256
  824.8 352.4 %all-gather.9.cloned.1.call-start = ((), (), s32[]{:S(2)}) async-start(), calls=%async_computation.18 | async-start | bytes 14155776 | tf_op jit(solution)/shard_map/all_gather | solution.py:282
  826.7 792.1 %reduce-scatter.21.cloned.1.call-start = ((), (), s32[]{:S(2)}) async-start(), calls=%async_computation.19 | async-start | bytes 28311552 | tf_op jit(solution)/shard_map/reduce_scatter | solution.py:292
  828.7 348.6 %copy-start.49 = (bf16[352,1024]{1,0:T(8,128)(2,1)S(1)}, bf16[352,1024]{1,0:T(8,128)(2,1)}, u32[]{:S(2)}) copy-start(bf16[352,1024]{1,0:T(8,128)(2,1)} %param.37) | copy-start | bytes 2162692
  1216.8 612.0 %reduce-scatter.19.cloned.1.call-start = ((), (), s32[]{:S(2)}) async-start(), calls=%async_computation.17 | async-start | bytes 14155776 | tf_op jit(solution)/shard_map/reduce_scatter | solution.py:262
  1229.0 781.2 %all-gather.11.cloned.1.call-start = ((), (), s32[]{:S(2)}) async-start(), calls=%async_computation.20 | async-start | bytes 14155776 | tf_op jit(solution)/shard_map/all_gather | solution.py:300
  1834.5 764.8 %reduce-scatter.37.cloned.1.call-start = ((), (), s32[]{:S(2)}) async-start(), calls=%async_computation.28 | async-start | bytes 901120 | tf_op jit(solution)/shard_map/reduce_scatter | solution.py:394
  1850.7 750.4 %reduce-scatter.39.cloned.1.call-start = ((), (), s32[]{:S(2)}) async-start(), calls=%async_computation.29 | async-start | bytes 901120 | tf_op jit(solution)/shard_map/reduce_scatter | solution.py:397
  1851.4 751.3 %reduce-scatter.41.cloned.1.call-start = ((), (), s32[]{:S(2)}) async-start(), calls=%async_computation.30 | async-start | bytes 901120 | tf_op jit(solution)/shard_map/reduce_scatter | solution.py:403
  1863.0 741.4 %reduce-scatter.33.cloned.1.call-start = ((), (), s32[]{:S(2)}) async-start(), calls=%async_computation.26 | async-start | bytes 81920 | tf_op jit(solution)/shard_map/reduce_scatter | solution.py:391
  2043.1 12.5 copy-start.11
  2077.9 12.4 copy-start.11
  2112.5 12.3 copy-start.11
  2147.1 12.3 copy-start.11
  2167.2 6.4 copy-start.5
  2170.8 4.3 copy-start.23
  2170.8 4.3 copy-start.26
  2199.4 12.3 copy-start.11
  2234.1 12.3 copy-start.11
  2268.7 12.3 copy-start.11
  2303.3 12.3 copy-start.11
  2323.3 6.4 copy-start.5
  2327.0 4.3 copy-start.23
  2327.0 4.3 copy-start.26
  2355.6 12.3 copy-start.11
  2390.2 12.3 copy-start.11
  2424.8 12.3 copy-start.11
  2459.4 12.3 copy-start.11
  2479.5 6.4 copy-start.5
  2483.1 4.4 copy-start.23
  2483.1 4.4 copy-start.26
  2507.4 4.7 copy-start.30
  2512.1 93.7 %reduce-scatter.31.cloned.1.call-start = ((), (), s32[]{:S(2)}) async-start(), calls=%async_computation.25 | async-start | bytes 81920 | tf_op jit(solution)/shard_map/reduce_scatter | solution.py:388
  2518.4 6.3 copy-start.31
  2526.1 9.7 copy-start.18
  2526.1 9.7 copy-start.28
  2535.8 71.3 %reduce-scatter.27.cloned.1.call-start = ((), (), s32[]{:S(2)}) async-start(), calls=%async_computation.23 | async-start | bytes 163840 | tf_op jit(solution)/shard_map/reduce_scatter | solution.py:385
  2538.8 19.2 copy-start.32
  2538.8 20.9 copy-start.14
  2559.6 7.4 copy-start.37
  2559.6 8.2 copy-start.20
  2559.7 48.8 %reduce-scatter.35.cloned.1.call-start = ((), (), s32[]{:S(2)}) async-start(), calls=%async_computation.27 | async-start | bytes 327680 | tf_op jit(solution)/shard_map/reduce_scatter | solution.py:400
  2566.9 4.5 copy-start.22
  2566.9 4.5 copy-start.39
  2567.0 55.8 %reduce-scatter.25.cloned.1.call-start = ((), (), s32[]{:S(2)}) async-start(), calls=%async_computation.22 | async-start | bytes 327680 | tf_op jit(solution)/shard_map/reduce_scatter | solution.py:382
  2571.3 262.2 %reduce-scatter.23.cloned.1.call-start = ((), (), s32[]{:S(2)}) async-start(), calls=%async_computation.21 | async-start | bytes 14155776 | tf_op jit(solution)/shard_map/reduce_scatter | solution.py:362
  2590.0 379.3 %reduce-scatter.43.cloned.1.call-start = ((), (), s32[]{:S(2)}) async-start(), calls=%async_computation.31 | async-start | bytes 540672
  2597.6 508.9 %reduce-scatter.29.cloned.1.call-start = ((), (), s32[]{:S(2)}) async-start(), calls=%async_computation.24 | async-start | bytes 2162688 | tf_op jit(solution)/shard_map/reduce_scatter | solution.py:408
  2599.2 234.4 %copy-start.9 = (bf16[768,1024]{1,0:T(8,128)(2,1)S(1)}, bf16[768,1024]{1,0:T(8,128)(2,1)}, u32[]{:S(2)}) copy-start(bf16[768,1024]{1,0:T(8,128)(2,1)} %param.22) | copy-start | bytes 4718596
  2599.2 234.4 %copy-start.42 = (f32[1024]{0:T(1024)S(1)}, f32[1024]{0:T(1024)}, u32[]{:S(2)}) copy-start(f32[1024]{0:T(1024)} %copy-done.41) | copy-start | bytes 12292
  2599.2 234.4 %copy-start.44 = (f32[768]{0:T(1024)S(1)}, f32[768]{0:T(1024)}, u32[]{:S(2)}) copy-start(f32[768]{0:T(1024)} %copy-done.43) | copy-start | bytes 9220
  2599.2 236.9 %copy-start.47 = (f32[1024]{0:T(1024)S(1)}, f32[1024]{0:T(1024)}, u32[]{:S(2)}) copy-start(f32[1024]{0:T(1024)} %get-tuple-element.511) | copy-start | bytes 12292
  2876.9 229.6 %copy-start.1 = (bf16[1024,512]{1,0:T(8,128)(2,1)S(1)}, bf16[1024,512]{1,0:T(8,128)(2,1)}, u32[]{:S(2)}) copy-start(bf16[1024,512]{1,0:T(8,128)(2,1)} %param.29) | copy-start | bytes 3145732
  (72 other events, 191.3 us)
Sparse Core Ops, SparseCore 0:
  13.6 179.1 all-gather.4
  417.4 401.8 reduce-scatter.16
  825.0 175.5 all-gather.6
  1002.6 174.6 all-gather.8
  1217.0 401.8 reduce-scatter.20
  1622.3 206.4 reduce-scatter.18
  1834.6 175.5 all-gather.10
  2012.7 21.0 reduce-scatter.36
  2036.5 22.8 reduce-scatter.38
  2061.7 22.8 reduce-scatter.40
  2512.2 17.9 reduce-scatter.32
  2535.9 17.9 reduce-scatter.30
  2559.7 18.1 reduce-scatter.26
  2580.2 20.0 reduce-scatter.34
  2602.7 19.9 reduce-scatter.24
  2626.2 207.2 reduce-scatter.22
  2836.2 133.0 reduce-scatter.42
  2972.1 134.3 reduce-scatter.28
where the time goes:
time: 3130 us; the launch traced here: 3110 us
  waiting for transfers between devices  2100 us (67%)
  matrix products  565 us (18%)
  other arithmetic  199 us (6%)
  local copies, waits for them, and re-layouts  148 us (5%)
  loops' own time  44.1 us (1%)
  blocking collectives  39.6 us (1%)
    reduce_scatter x1, waiting for transfers between devices, on_device(): lax.psum_scatter(jnp.dot(mixed_flat, w_out, preferred_element_type=jnp.fl...  401 us
    reduce_scatter x1, waiting for transfers between devices, on_device(): lax.psum_scatter(jnp.einsum('tf,df->td', grad_gate_up, gate_up_weight, pr...  390 us
    reduce_scatter x1, waiting for transfers between devices, on_device(): lax.psum_scatter(jnp.einsum('tc,dc->td', grad_project, repeat_weight, pre...  209 us
    reduce_scatter x1, waiting for transfers between devices, on_device(): lax.psum_scatter(jnp.dot(inner_act, w_down, preferred_element_type=jnp.fl...  206 us
    all_gather x1, waiting for transfers between devices, on_device(): gathered = lax.all_gather(normed, 'heads', axis=0, tiled=True)  178 us
    all_gather x1, waiting for transfers between devices, on_device(): gathered_mlp = lax.all_gather(normed_mlp, 'heads', axis=0, tiled=True)  172 us
    all_gather x1, waiting for transfers between devices, on_device(): grad_rows = lax.all_gather(grad_branch, 'heads', axis=0, tiled=True)  161 us
    all_gather x1, waiting for transfers between devices, on_device(): lax.all_gather(grad_hidden.astype(jnp.bfloat16), 'heads', axis=0, tiled=T...  147 us
  transfers between devices with their start and end apart: 18, of which 11 were waited for; matrix products, arithmetic and copies ran while one was open for 21% of the time, Pallas kernels for 0%

commit v1 on v0

v1 whole, which is shorter than its diff:
```python
import functools
import math

import jax
import jax.numpy as jnp
from jax import lax
from jax.experimental import pallas as pl
from jax.experimental.pallas import tpu as pltpu
from jax.sharding import PartitionSpec as P

D = 1024
HEADS = 16
HD = 64
LGROUPS = 2
LAT = 256
RD = 32
LEN = 2048
EPS = 1e-05
THETA = 10000.0
NEG_LARGE = -1e30
LANES = 128
PAIR = 2
LOG2E = math.log2(math.e)
LN2 = math.log(2.0)
SCALE = (HD + RD) ** (-0.5)

bf16 = jnp.bfloat16
f32 = jnp.float32


def dot_nn(a, b):
    return jnp.dot(a, b, preferred_element_type=f32)


def dot_nt(a, b):
    return lax.dot_general(a, b, (((1,), (1,)), ((), ())), preferred_element_type=f32)


def dot_tn(a, b):
    return lax.dot_general(a, b, (((0,), (0,)), ((), ())), preferred_element_type=f32)


def rms_scale(values):
    return lax.rsqrt(jnp.mean(values * values, axis=-1, keepdims=True) + EPS)


def norm_backward(source, scale_rows, gain, grad_normed):
    scaled = source * scale_rows
    weighted = grad_normed * gain
    grad_source = scale_rows * (
        weighted - scaled * jnp.mean(weighted * scaled, axis=-1, keepdims=True)
    )
    return (grad_source, jnp.sum(grad_normed * scaled, axis=0))


def attend_forward_kernel(
    block, own, halo, place_ref, q_ref, latent_ref, rope_ref, up_ref, mixed_ref, log_ref, key_s, value_s
):
    total = halo + own

    def prepare(index, _):
        rows = pl.ds(pl.multiple_of(index * block, block), block)
        latent = latent_ref[rows, :]
        lane = lax.broadcasted_iota(jnp.int32, (block, LANES), 1)
        for e in range(PAIR):
            both = dot_nn(latent, up_ref[:, e * LANES : (e + 1) * LANES]).astype(bf16)
            key_s[e, rows, :] = jnp.where(lane < HD, both, rope_ref[rows, :])
            value_s[e, index] = both[:, HD:].T
        return 0

    lax.fori_loop(halo - place_ref[0], total, prepare, 0)
    keep = lax.broadcasted_iota(jnp.int32, (block, block), 0) <= lax.broadcasted_iota(
        jnp.int32, (block, block), 1
    )
    for j in range(own):
        at = halo + j
        cols = slice(j * block, (j + 1) * block)
        queries = [q_ref[cols, e * LANES : (e + 1) * LANES].T for e in range(PAIR)]
        state = []
        for e in range(PAIR):
            scores = dot_nn(key_s[e, at * block : (at + 1) * block, :], queries[e])
            scores = jnp.where(keep, scores, NEG_LARGE)
            top = jnp.max(scores, axis=0, keepdims=True)
            terms = jnp.exp2(scores - top)
            sums = jnp.sum(terms, axis=0, keepdims=True)
            state += [top, sums, dot_nn(value_s[e, at], terms.astype(bf16))]

        def step(index, held):
            rows = pl.ds(pl.multiple_of(index * block, block), block)
            out = []
            for e in range(PAIR):
                top, sums, mixed = held[3 * e : 3 * e + 3]
                scores = dot_nn(key_s[e, rows, :], queries[e])
                higher = jnp.maximum(top, jnp.max(scores, axis=0, keepdims=True))
                shrink = jnp.exp2(top - higher)
                terms = jnp.exp2(scores - higher)
                sums = sums * shrink + jnp.sum(terms, axis=0, keepdims=True)
                mixed = mixed * shrink + dot_nn(value_s[e, index], terms.astype(bf16))
                out += [higher, sums, mixed]
            return tuple(out)

        state = lax.fori_loop(at - place_ref[j], at, step, tuple(state))
        for e in range(PAIR):
            top, sums, mixed = state[3 * e : 3 * e + 3]
            mixed_ref[e * HD : (e + 1) * HD, cols] = (mixed / sums).astype(bf16)
            log_ref[e, :, cols] = top + jnp.log2(sums)


def attend_forward(places, queries, window, up_weight, block, own, halo):
    rows, wide = own * block, (halo + own) * block
    steps = HEADS // LGROUPS // PAIR
    return pl.pallas_call(
        functools.partial(attend_forward_kernel, block, own, halo),
        grid_spec=pltpu.PrefetchScalarGridSpec(
            num_scalar_prefetch=1,
            grid=(HEADS // PAIR,),
            in_specs=[
                pl.BlockSpec((rows, PAIR * LANES), lambda h, p: (0, h)),
                pl.BlockSpec((wide, LAT), lambda h, p: (0, h // steps)),
                pl.BlockSpec((wide, LANES), lambda h, p: (0, LGROUPS * LAT // LANES)),
                pl.BlockSpec((LAT, PAIR * LANES), lambda h, p: (0, h)),
            ],
            out_specs=[
                pl.BlockSpec((PAIR * HD, rows), lambda h, p: (h, 0)),
                pl.BlockSpec((PAIR, 1, rows), lambda h, p: (h, 0, 0)),
            ],
            scratch_shapes=[
                pltpu.VMEM((PAIR, wide, LANES), bf16),
                pltpu.VMEM((PAIR, halo + own, HD, block), bf16),
            ],
        ),
        out_shape=[
            jax.ShapeDtypeStruct((HEADS * HD, rows), bf16),
            jax.ShapeDtypeStruct((HEADS, 1, rows), f32),
        ],
        compiler_params=pltpu.CompilerParams(vmem_limit_bytes=48 << 20),
        name="attend_forward",
    )(places, queries, window, window, up_weight)


def attend_backward_kernel(
    block, own, halo, steps, place_ref, q_ref, latent_ref, rope_ref, up_ref, mixed_ref, log_ref,
    grad_ref, cos_ref, low_ref, high_ref, dq_ref, dlatent_ref, drope_ref, dup_ref,
    key_s, key_t_s, value_s, dkey_s, dvalue_s,
):
    h = pl.program_id(0)
    total = halo + own
    first = halo - place_ref[0]

    @pl.when(h == 0)
    def _():
        drope_ref[...] = jnp.zeros_like(drope_ref)

    @pl.when(h % steps == 0)
    def _():
        dlatent_ref[...] = jnp.zeros_like(dlatent_ref)

    lane = lax.broadcasted_iota(jnp.int32, (block, LANES), 1)

    def prepare(index, _):
        rows = pl.ds(pl.multiple_of(index * block, block), block)
        latent = latent_ref[rows, :]
        for e in range(PAIR):
            both = dot_nn(latent, up_ref[:, e * LANES : (e + 1) * LANES]).astype(bf16)
            keys = jnp.where(lane < HD, both, rope_ref[rows, :])
            key_s[e, rows, :] = keys
            key_t_s[e, index] = keys.T
            value_s[e, rows, :] = both[:, HD:]
            dkey_s[e, rows, :] = jnp.zeros((block, LANES), f32)
            dvalue_s[e, rows, :] = jnp.zeros((block, LANES), f32)
        return 0

    lax.fori_loop(first, total, prepare, 0)
    keep = lax.broadcasted_iota(jnp.int32, (block, block), 0) <= lax.broadcasted_iota(
        jnp.int32, (block, block), 1
    )
    for j in range(own):
        at = halo + j
        cols = slice(j * block, (j + 1) * block)
        queries = [q_ref[cols, e * LANES : (e + 1) * LANES] for e in range(PAIR)]
        queries_t = [q.T for q in queries]
        grads_t = [grad_ref[e * HD : (e + 1) * HD, cols] for e in range(PAIR)]
        grads = [jnp.concatenate([jnp.zeros((block, HD), bf16), g.T], axis=1) for g in grads_t]
        logs = [log_ref[e, :, cols] for e in range(PAIR)]
        inner = [
            jnp.sum(
                grads_t[e].astype(f32) * mixed_ref[e * HD : (e + 1) * HD, cols].astype(f32),
                axis=0,
                keepdims=True,
            )
            for e in range(PAIR)
        ]

        def tile(index, held, masked):
            rows = pl.ds(pl.multiple_of(index * block, block), block)
            out = []
            for e in range(PAIR):
                scores = dot_nn(key_s[e, rows, :], queries_t[e])
                if masked:
                    scores = jnp.where(keep, scores, NEG_LARGE)
                probs = jnp.exp2(scores - logs[e])
                grad_probs = dot_nn(value_s[e, rows, :], grads_t[e])
                grad_scores = (probs * (grad_probs - inner[e])).astype(bf16)
                dvalue_s[e, rows, :] += dot_nn(probs.astype(bf16), grads[e])
                dkey_s[e, rows, :] += dot_nn(grad_scores, queries[e])
                out.append(held[e] + dot_nn(key_t_s[e, index], grad_scores))
            return tuple(out)

        held = tile(at, tuple(jnp.zeros((LANES, block), f32) for _ in range(PAIR)), True)
        held = lax.fori_loop(
            at - place_ref[j], at, lambda index, held: tile(index, held, False), held
        )
        for e in range(PAIR):
            grad = held[e].T * SCALE
            grad = (
                grad * cos_ref[cols, :]
                + pltpu.roll(grad, RD // 2, 1) * low_ref[cols, :]
                + pltpu.roll(grad, LANES - RD // 2, 1) * high_ref[cols, :]
            )
            dq_ref[cols, e * LANES : (e + 1) * LANES] = grad.astype(bf16)
    dup_ref[...] = jnp.zeros_like(dup_ref)

    def finish(index, _):
        rows = pl.ds(pl.multiple_of(index * block, block), block)
        latent_t = latent_ref[rows, :].T
        grad_latent = None
        grad_rope = None
        for e in range(PAIR):
            grad_key = dkey_s[e, rows, :] * LN2
            both = jnp.where(lane < HD, grad_key, dvalue_s[e, rows, :]).astype(bf16)
            part = dot_nt(both, up_ref[:, e * LANES : (e + 1) * LANES])
            grad_latent = part if grad_latent is None else grad_latent + part
            grad_rope = grad_key if grad_rope is None else grad_rope + grad_key
            dup_ref[:, e * LANES : (e + 1) * LANES] += dot_nn(latent_t, both)
        dlatent_ref[rows, :] += grad_latent
        drope_ref[rows, :] += grad_rope
        return 0

    lax.fori_loop(first, total, finish, 0)


def attend_backward(
    places, queries, window, up_weight, mixed, logs, grad_mixed, cos_t, low_t, high_t, block, own, halo
):
    rows, wide = own * block, (halo + own) * block
    steps = HEADS // LGROUPS // PAIR
    table = pl.BlockSpec((rows, LANES), lambda h, p: (0, 0))
    return pl.pallas_call(
        functools.partial(attend_backward_kernel, block, own, halo, steps),
        grid_spec=pltpu.PrefetchScalarGridSpec(
            num_scalar_prefetch=1,
            grid=(HEADS // PAIR,),
            in_specs=[
                pl.BlockSpec((rows, PAIR * LANES), lambda h, p: (0, h)),
                pl.BlockSpec((wide, LAT), lambda h, p: (0, h // steps)),
                pl.BlockSpec((wide, LANES), lambda h, p: (0, LGROUPS * LAT // LANES)),
                pl.BlockSpec((LAT, PAIR * LANES), lambda h, p: (0, h)),
                pl.BlockSpec((PAIR * HD, rows), lambda h, p: (h, 0)),
                pl.BlockSpec((PAIR, 1, rows), lambda h, p: (h, 0, 0)),
                pl.BlockSpec((PAIR * HD, rows), lambda h, p: (h, 0)),
                table,
                table,
                table,
            ],
            out_specs=[
                pl.BlockSpec((rows, PAIR * LANES), lambda h, p: (0, h)),
                pl.BlockSpec((wide, LAT), lambda h, p: (0, h // steps)),
                pl.BlockSpec((wide, LANES), lambda h, p: (0, 0)),
                pl.BlockSpec((LAT, PAIR * LANES), lambda h, p: (0, h)),
            ],
            scratch_shapes=[
                pltpu.VMEM((PAIR, wide, LANES), bf16),
                pltpu.VMEM((PAIR, halo + own, LANES, block), bf16),
                pltpu.VMEM((PAIR, wide, HD), bf16),
                pltpu.VMEM((PAIR, wide, LANES), f32),
                pltpu.VMEM((PAIR, wide, LANES), f32),
            ],
        ),
        out_shape=[
            jax.ShapeDtypeStruct((rows, HEADS * LANES), bf16),
            jax.ShapeDtypeStruct((wide, LGROUPS * LAT), f32),
            jax.ShapeDtypeStruct((wide, LANES), f32),
            jax.ShapeDtypeStruct((LAT, HEADS * LANES), f32),
        ],
        compiler_params=pltpu.CompilerParams(vmem_limit_bytes=56 << 20),
        name="attend_backward",
    )(places, queries, window, window, up_weight, mixed, logs, grad_mixed, cos_t, low_t, high_t)


def project_kernel(normed_ref, weight_ref, cos_ref, sin_ref, out_ref):
    raw = dot_nn(normed_ref[...], weight_ref[...])
    for e in range(PAIR):
        part = raw[:, e * LANES : (e + 1) * LANES]
        part = part * cos_ref[...] + pltpu.roll(part, LANES - RD, 1) * sin_ref[...]
        out_ref[:, e * LANES : (e + 1) * LANES] = part.astype(bf16)


def project_queries(normed, weight, cos_t, sin_t):
    rows = normed.shape[0]
    table = pl.BlockSpec((rows, LANES), lambda h: (0, 0))
    return pl.pallas_call(
        project_kernel,
        grid=(HEADS // PAIR,),
        in_specs=[
            pl.BlockSpec((rows, D), lambda h: (0, 0)),
            pl.BlockSpec((D, PAIR * LANES), lambda h: (0, h)),
            table,
            table,
        ],
        out_specs=pl.BlockSpec((rows, PAIR * LANES), lambda h: (0, h)),
        out_shape=jax.ShapeDtypeStruct((rows, HEADS * LANES), bf16),
        compiler_params=pltpu.CompilerParams(vmem_limit_bytes=40 << 20),
        name="project_queries",
    )(normed, weight, cos_t, sin_t)


def feed_kernel(cuts, shards, units, normed_ref, grad_ref, weight_ref, out_ref, dnormed_ref, dweight_ref):
    def whole(which):
        return jnp.concatenate(
            [
                jnp.concatenate(
                    [weight_ref[q, t, which * units : (which + 1) * units, :] for q in range(cuts)],
                    axis=1,
                )
                for t in range(shards)
            ],
            axis=0,
        )

    def put(which, grad):
        wide = D // cuts
        for t in range(shards):
            for q in range(cuts):
                dweight_ref[q, t, which * units : (which + 1) * units, :] = grad[
                    t * units : (t + 1) * units, q * wide : (q + 1) * wide
                ].astype(bf16)

    @pl.when(pl.program_id(0) == 0)
    def _():
        out_ref[...] = jnp.zeros_like(out_ref)
        dnormed_ref[...] = jnp.zeros_like(dnormed_ref)

    normed = normed_ref[...]
    grad = grad_ref[...]
    w_gate, w_up, w_down = whole(0), whole(1), whole(2)
    gate = dot_nt(w_gate, normed)
    upper = dot_nt(w_up, normed)
    grad_inner = dot_nt(w_down, grad)
    sig = jax.nn.sigmoid(gate)
    silu = gate * sig
    inner = (silu * upper).astype(bf16)
    grad_gate = (grad_inner * upper * sig * (1.0 + gate * (1.0 - sig))).astype(bf16)
    grad_upper = (grad_inner * silu).astype(bf16)
    out_ref[...] += dot_tn(inner, w_down)
    dnormed_ref[...] += dot_tn(grad_gate, w_gate)
    dnormed_ref[...] += dot_tn(grad_upper, w_up)
    put(0, dot_nn(grad_gate, normed))
    put(1, dot_nn(grad_upper, normed))
    put(2, dot_nn(inner, grad))


def feed_forward_both(normed, grad, weights, units):
    rows = normed.shape[0]
    cuts, pieces, tall, wide = weights.shape
    shards = max(1, min(pieces, 704 // units))
    once = pl.Buffered(1)
    return pl.pallas_call(
        functools.partial(feed_kernel, cuts, shards, units),
        grid=(pieces // shards,),
        in_specs=[
            pl.BlockSpec((rows, D), lambda f: (0, 0), pipeline_mode=once),
            pl.BlockSpec((rows, D), lambda f: (0, 0), pipeline_mode=once),
            pl.BlockSpec((cuts, shards, tall, wide), lambda f: (0, f, 0, 0)),
        ],
        out_specs=[
            pl.BlockSpec((rows, D), lambda f: (0, 0), pipeline_mode=once),
            pl.BlockSpec((rows, D), lambda f: (0, 0), pipeline_mode=once),
            pl.BlockSpec((cuts, shards, 3 * units, wide), lambda f: (0, f, 0, 0)),
        ],
        out_shape=[
            jax.ShapeDtypeStruct((rows, D), f32),
            jax.ShapeDtypeStruct((rows, D), f32),
            jax.ShapeDtypeStruct((cuts, pieces, 3 * units, wide), bf16),
        ],
        compiler_params=pltpu.CompilerParams(vmem_limit_bytes=60 << 20),
        name="feed_forward_both",
    )(normed, grad, weights)


def bits_of(size):
    return size.bit_length() - 1


def bit_pairs(size, bit):
    return [(i, i ^ (1 << bit)) for i in range(size)]


def gather_all(piece, shape):
    lead = []
    for axis in ("heads", "rows"):
        for bit in range(bits_of(shape[axis])):
            other = lax.ppermute(piece, axis, bit_pairs(shape[axis], bit))
            upper = (lax.axis_index(axis) >> bit) & 1
            piece = jnp.stack(
                [jnp.where(upper == 1, other, piece), jnp.where(upper == 1, piece, other)]
            )
            lead.append((axis, bit))
    tail = len(piece.shape) - len(lead)
    lead = lead[::-1]
    wanted = [("rows", b) for b in reversed(range(bits_of(shape["rows"])))]
    wanted += [("heads", b) for b in reversed(range(bits_of(shape["heads"])))]
    order = [lead.index(w) for w in wanted] + [len(lead) + i for i in range(tail)]
    whole = piece.transpose(order)
    return whole.reshape((shape["rows"], shape["heads"]) + whole.shape[len(lead) :])


def scatter_all(parts, shape):
    row_bits, head_bits = bits_of(shape["rows"]), bits_of(shape["heads"])
    tails = [part.shape[2:] for part in parts]
    lead = [("rows", b) for b in reversed(range(row_bits))]
    lead += [("heads", b) for b in reversed(range(head_bits))]
    parts = [part.reshape((2,) * len(lead) + tail) for part, tail in zip(parts, tails)]
    for axis, count in (("rows", row_bits), ("heads", head_bits)):
        for bit in range(count):
            at = lead.index((axis, bit))
            upper = (lax.axis_index(axis) >> bit) & 1
            sent = [lax.dynamic_index_in_dim(part, 1 - upper, at, keepdims=False) for part in parts]
            kept = [lax.dynamic_index_in_dim(part, upper, at, keepdims=False) for part in parts]
            got = [lax.ppermute(part, axis, bit_pairs(shape[axis], bit)) for part in sent]
            parts = [
                (a.astype(f32) + b.astype(f32)).astype(part.dtype)
                for a, b, part in zip(kept, got, parts)
            ]
            lead.pop(at)
    return parts


def lane_table(rows, entries):
    columns = []
    for width, value in entries:
        columns.append(
            jnp.full((rows, width), value, f32) if isinstance(value, float) else value
        )
    return jnp.concatenate(columns, axis=1)


def on_device(
    shape,
    tokens,
    cotangent,
    domain,
    group_weight,
    gain_attn,
    w_query,
    w_query_rope,
    w_latent,
    w_key_rope,
    w_key_up,
    w_value_up,
    w_out,
    gain_mlp,
    w_gate,
    w_up,
    w_down,
):
    n_rows, n_heads = shape["rows"], shape["heads"]
    row_at, head_at = lax.axis_index("rows"), lax.axis_index("heads")
    local = tokens.shape[0]
    block = math.gcd(local, LEN)
    own, halo = local // block, LEN // block - 1
    heads_here = w_query.shape[1] // HD
    units = w_gate.shape[1]
    cut = D // n_rows

    half = RD // 2
    rope_here = w_query_rope.reshape(D, heads_here, RD)
    query_here = jnp.concatenate(
        [
            w_query.reshape(D, heads_here, HD),
            rope_here,
            -rope_here[:, :, half:],
            rope_here[:, :, :half],
        ],
        axis=2,
    ).reshape(D, heads_here * LANES)
    up_here = jnp.concatenate(
        [w_key_up.reshape(LAT, heads_here, HD), w_value_up.reshape(LAT, heads_here, HD)], axis=2
    ).reshape(LAT, heads_here * LANES)
    small = jnp.concatenate([query_here, up_here], axis=0)
    tall = small.shape[0]
    small_piece = lax.dynamic_slice_in_dim(small, row_at * (tall // n_rows), tall // n_rows, 0)
    small_all = gather_all(small_piece, shape).transpose(0, 2, 1, 3).reshape(tall, HEADS * LANES)
    query_weight, up_weight = small_all[:D], small_all[D:]

    def part_of(weight):
        return lax.dynamic_slice_in_dim(weight, row_at * cut, cut, 1)

    large = jnp.concatenate(
        [part_of(w_gate.T), part_of(w_up.T), part_of(w_down), part_of(w_out)], axis=0
    )
    large_all = lax.all_gather(large, ("rows", "heads"), axis=0, tiled=True)
    large_all = large_all.reshape(n_rows, n_heads, large.shape[0], cut)
    out_weight = large_all[:, :, 3 * units :].transpose(1, 2, 0, 3).reshape(HEADS * HD, D)

    start = head_at * local
    positions = ((start + jnp.arange(local)) % LEN).astype(f32)
    frequency = THETA ** (-jnp.arange(half).astype(f32) / half)
    angles = positions[:, None] * frequency[None, :]
    cos, sin = jnp.cos(angles), jnp.sin(angles)
    places = ((start // block + jnp.arange(own)) % (LEN // block)).astype(jnp.int32)
    front = SCALE * LOG2E
    query_cos = lane_table(local, [(HD, front), (0, front * cos), (0, front * cos), (RD, 0.0)])
    query_sin = lane_table(local, [(HD, 0.0), (0, front * sin), (0, front * sin), (RD, 0.0)])
    key_cos = lane_table(local, [(HD, 0.0), (0, cos), (0, cos), (RD, 0.0)])
    key_sin = lane_table(local, [(HD, 0.0), (0, sin), (0, sin), (RD, 0.0)])
    back_cos = lane_table(local, [(HD, 1.0), (0, cos), (0, cos), (RD, 0.0)])
    back_low = lane_table(local, [(HD + half, 0.0), (0, -sin), (RD, 0.0)])
    back_high = lane_table(local, [(HD, 0.0), (0, sin), (half + RD, 0.0)])

    source = tokens.astype(f32)
    scale_attn = rms_scale(source)
    gain_one = gain_attn.astype(f32)
    normed = (source * scale_attn * gain_one).astype(bf16)
    blank = jnp.zeros((D, HD), bf16)
    latent_weight = jnp.concatenate(
        [w_latent, blank, w_key_rope, -w_key_rope[:, half:], w_key_rope[:, :half]], axis=1
    )
    raw = dot_nn(normed, latent_weight)
    raw_rope = raw[:, LGROUPS * LAT :]
    key_rope = raw_rope * key_cos + jnp.roll(raw_rope, -RD, axis=1) * key_sin
    latent = jnp.concatenate([raw[:, : LGROUPS * LAT], key_rope], axis=1).astype(bf16)

    def halo_pairs(k):
        back = -(-k // own)
        needs = [i for i in range(n_heads) if (i * local % LEN) // block >= k]
        return [(i - back, i) for i in needs]

    def halo_rows(k):
        at = own - 1 - (k - 1) % own
        return slice(at * block, (at + 1) * block)

    pieces = [
        lax.ppermute(latent[halo_rows(k)], "heads", halo_pairs(k)) for k in range(halo, 0, -1)
    ]
    window = jnp.concatenate(pieces + [latent], axis=0)
    queries = project_queries(normed, query_weight, query_cos, query_sin)
    mixed, logs = attend_forward(places, queries, window, up_weight, block, own, halo)

    hidden = source + dot_tn(mixed, out_weight)
    scale_mlp = rms_scale(hidden)
    gain_two = gain_mlp.astype(f32)
    normed_mlp = (hidden * scale_mlp * gain_two).astype(bf16)
    seq_weights = jnp.sum(
        (domain[:, None] == jnp.arange(group_weight.shape[0])[None, :]).astype(f32)
        * group_weight[None, :],
        axis=1,
    )
    token_seq = (start + jnp.arange(local)) // LEN
    token_weight = jnp.sum(
        (token_seq[:, None] == jnp.arange(domain.shape[0])[None, :]).astype(f32)
        * seq_weights[None, :],
        axis=1,
    )
    grad_output = cotangent.astype(f32) * token_weight[:, None]
    direct = cut % LANES == 0
    feed_weights = large_all
    if not direct:
        feed_weights = large_all[:, :, : 3 * units].transpose(1, 2, 0, 3)
        feed_weights = feed_weights.reshape(1, n_heads, 3 * units, D)
    feed_out, grad_normed_mlp, grad_feed = feed_forward_both(
        normed_mlp, grad_output.astype(bf16), feed_weights, units
    )
    if not direct:
        grad_feed = grad_feed.reshape(n_heads, 3 * units, n_rows, cut).transpose(2, 0, 1, 3)
    block_output = (hidden + feed_out).astype(bf16)
    grad_hidden_part, grad_gain_two = norm_backward(hidden, scale_mlp, gain_two, grad_normed_mlp)
    grad_hidden = grad_output + grad_hidden_part
    grad_hidden_low = grad_hidden.astype(bf16)
    own_feed = lax.psum_scatter(
        grad_feed.reshape((n_rows * n_heads,) + grad_feed.shape[2:]),
        ("rows", "heads"),
        scatter_dimension=0,
        tiled=True,
    )[0].astype(f32)

    grad_mixed = dot_nt(out_weight, grad_hidden_low).astype(bf16)
    grad_out_weight = dot_nn(mixed, grad_hidden_low).astype(bf16)
    own_out = lax.psum_scatter(
        grad_out_weight.reshape(n_heads, HEADS * HD // n_heads, n_rows, cut)
        .transpose(2, 0, 1, 3)
        .reshape(n_rows * n_heads, HEADS * HD // n_heads, cut),
        ("rows", "heads"),
        scatter_dimension=0,
        tiled=True,
    )[0].astype(f32)
    grad_query, grad_latent, grad_rope, grad_up_weight = attend_backward(
        places, queries, window, up_weight, mixed, logs, grad_mixed, back_cos, back_low, back_high,
        block, own, halo,
    )
    grad_window = jnp.concatenate([grad_latent, grad_rope], axis=1).astype(bf16)
    own_blocks = [
        grad_window[(halo + j) * block : (halo + j + 1) * block].astype(f32) for j in range(own)
    ]
    for k in range(1, halo + 1):
        got = lax.ppermute(
            grad_window[(halo - k) * block : (halo - k + 1) * block],
            "heads",
            [(b, a) for a, b in halo_pairs(k)],
        )
        at = own - 1 - (k - 1) % own
        own_blocks[at] = own_blocks[at] + got.astype(f32)
    grad_own = jnp.concatenate(own_blocks, axis=0)
    grad_rope_own = grad_own[:, LGROUPS * LAT :]
    grad_rope_own = (
        grad_rope_own * (key_cos)
        + jnp.roll(grad_rope_own, half, axis=1) * back_low
        + jnp.roll(grad_rope_own, -half, axis=1) * back_high
    )
    grad_own = jnp.concatenate([grad_own[:, : LGROUPS * LAT], grad_rope_own], axis=1).astype(bf16)

    grad_normed = dot_nt(grad_query, query_weight) + dot_nt(grad_own, latent_weight)
    grad_source_part, grad_gain_one = norm_backward(source, scale_attn, gain_one, grad_normed)
    grad_tokens = grad_hidden + grad_source_part
    grad_query_weight = dot_tn(normed, grad_query)
    grad_latent_weight = dot_tn(normed, grad_own)
    grad_small = jnp.concatenate([grad_query_weight, grad_up_weight], axis=0).astype(bf16)
    grad_small = jnp.concatenate(
        [
            grad_query_weight.astype(bf16).reshape(n_rows, D // n_rows, n_heads, heads_here * LANES),
            grad_up_weight.astype(bf16).reshape(n_rows, LAT // n_rows, n_heads, heads_here * LANES),
        ],
        axis=1,
    ).transpose(0, 2, 1, 3)
    at = LGROUPS * LAT
    grad_latent_weight = jnp.concatenate(
        [
            grad_latent_weight[:, :at],
            grad_gain_one[:, None],
            grad_gain_two[:, None],
            jnp.zeros((D, HD - 2), f32),
            grad_latent_weight[:, at + HD :],
        ],
        axis=1,
    ).astype(bf16)
    own_small, own_latent = scatter_all(
        [grad_small, grad_latent_weight.reshape(n_rows, n_heads, D // (n_rows * n_heads), at + LANES)],
        shape,
    )
    own_small = own_small.astype(f32)
    own_latent = own_latent.astype(f32)
    own_query = own_small[: D // n_rows].reshape(D // n_rows, heads_here, LANES)
    own_up = own_small[D // n_rows :].reshape(LAT // n_rows, heads_here, LANES)
    return (
        block_output,
        grad_tokens,
        own_latent[:, at],
        own_query[:, :, :HD].reshape(D // n_rows, heads_here * HD),
        own_query[:, :, HD : HD + RD].reshape(D // n_rows, heads_here * RD),
        own_latent[:, :at],
        own_latent[:, at + HD : at + HD + RD],
        own_up[:, :, :HD].reshape(LAT // n_rows, heads_here * HD),
        own_up[:, :, HD:].reshape(LAT // n_rows, heads_here * HD),
        own_out,
        own_latent[:, at + 1],
        own_feed[:units].T,
        own_feed[units : 2 * units].T,
        own_feed[2 * units :],
    )


def solution(mesh):
    in_specs = (
        P(("rows", "heads"), None),
        P(("rows", "heads"), None),
        P("rows"),
        P(),
        P(),
        P(None, "heads"),
        P(None, "heads"),
        P(),
        P(),
        P(None, "heads"),
        P(None, "heads"),
        P("heads", None),
        P(),
        P(None, "heads"),
        P(None, "heads"),
        P("heads", None),
    )
    out_specs = (
        P(("rows", "heads"), None),
        P(("rows", "heads"), None),
        P(("rows", "heads")),
        P("rows", "heads"),
        P("rows", "heads"),
        P(("rows", "heads"), None),
        P(("rows", "heads"), None),
        P("rows", "heads"),
        P("rows", "heads"),
        P("heads", "rows"),
        P(("rows", "heads")),
        P("rows", "heads"),
        P("rows", "heads"),
        P("heads", "rows"),
    )
    return jax.shard_map(
        functools.partial(on_device, dict(mesh.shape)),
        mesh=mesh,
        in_specs=in_specs,
        out_specs=out_specs,
        check_vma=False,
    )
```

time: 3130 us -> 828 us (0.26)
  waiting for transfers between devices: 2100 us -> 413 us
  matrix products: 565 us -> 27.4 us
  Pallas kernels: 0 us -> 157 us
  other arithmetic: 199 us -> 55.6 us
  starting transfers between devices: 0.75 us -> 76.1 us
  local copies, waits for them, and re-layouts: 148 us -> 74.6 us
  loops' own time: 44.1 us -> 0 us
  blocking collectives: 39.6 us -> 0 us
    reduce_scatter x13 -> x2, waiting for transfers between devices: 1360 us -> 22.6 us  [the longest x1 22.5 us: on_device(): lax.psum_scatter(grad_feed.reshape((n_rows * n_heads,) + grad_feed.shape[...]
    all_gather x4 -> x1, waiting for transfers between devices: 658 us -> 0.01 us  [on_device(): large_all = lax.all_gather(large, ('rows', 'heads'), axis=0, tiled=True)]
    dot_general x146 -> x8, matrix products: 561 us -> 27.4 us  [the longest x3 12.6 us: dot_nt(): lax.dot_general(a, b, (((1,), (1,)), ((), ())), preferred_element_type=f32)]
    ppermute x0 -> x29, waiting for transfers between devices: none -> 390 us  [the longest x7 177 us: on_device(): lax.ppermute(grad_window[(halo - k) * block:(halo - k + 1) * block], 'hea...]
    pallas_call x0 -> x4, Pallas kernels: none -> 157 us  [the longest x1 56.3 us: attend_backward(): pl.pallas_call(functools.partial(attend_backward_kernel, block, own, halo...]
    convert_element_type x27 -> x19, other arithmetic: 125 us -> 16.9 us  [the longest x8 8.12 us: scatter_all(): (a.astype(f32) + b.astype(f32)).astype(part.dtype)]
    unnamed x19 -> x3, waiting for transfers between devices: 88.4 us -> 0.71 us
    ppermute x0 -> x29, starting transfers between devices: none -> 76 us  [the longest x10 43.9 us: scatter_all(): lax.ppermute(part, axis, bit_pairs(shape[axis], bit))]
  transfers between devices with their start and end apart: 18 -> 32, of which waited for: 11 -> 18; matrix products, arithmetic and copies ran while one was open for 21% -> 13% of each run, Pallas kernels for 0% -> 13%
where the time goes in v1:
time: 828 us; the launch traced here: 820 us
  waiting for transfers between devices  413 us (50%)
  Pallas kernels  157 us (19%)
  starting transfers between devices  76.1 us (9%)
  local copies, waits for them, and re-layouts  74.6 us (9%)
  other arithmetic  55.6 us (7%)
  matrix products  27.4 us (3%)
  between operations  15.5 us (2%)
    ppermute x7, waiting for transfers between devices, on_device(): lax.ppermute(grad_window[(halo - k) * block:(halo - k + 1) * block], 'hea...  177 us
    ppermute x5, waiting for transfers between devices, gather_all(): other = lax.ppermute(piece, axis, bit_pairs(shape[axis], bit))  89.4 us
    ppermute x10, waiting for transfers between devices, scatter_all(): lax.ppermute(part, axis, bit_pairs(shape[axis], bit))  88.4 us
    pallas_call x1, Pallas kernels, attend_backward(): pl.pallas_call(functools.partial(attend_backward_kernel, block, own, halo...  56.3 us
    pallas_call x1, Pallas kernels, feed_forward_both(): pl.pallas_call(functools.partial(feed_kernel, cuts, shards, units), grid=...  50.2 us
    pallas_call x1, Pallas kernels, attend_forward(): pl.pallas_call(functools.partial(attend_forward_kernel, block, own, halo)...  44.9 us
    ppermute x10, starting transfers between devices, scatter_all(): lax.ppermute(part, axis, bit_pairs(shape[axis], bit))  43.9 us
    ppermute x7, waiting for transfers between devices, on_device(): lax.ppermute(latent[halo_rows(k)], 'heads', halo_pairs(k))  35.5 us
  transfers between devices with their start and end apart: 32, of which 18 were waited for; matrix products, arithmetic and copies ran while one was open for 13% of the time, Pallas kernels for 13%

profile of v1, /device:TPU:0, one launch (start us, length us, event | category | flops | bytes accessed | tf_op | source)
XLA Modules:
  0.0 819.8 jit_solution(5489110028825581597)
XLA Ops:
  12.3 3.0 collective-permute-start
  15.4 4.2 collective-permute-done
  19.7 1.9 collective-permute-start.1
  21.5 16.1 %collective-permute-done.1 = bf16[2,320,256]{2,1,0:T(8,128)(2,1)S(1)} collective-permute-done((bf16[2,320,256]{2,1,0:T(8,128)(2,1)S(1)}, bf16[2,320,256]{2,1,0:T(8,128)(2,1)S(1)}, u32[]{:S(2)}, u32[]{:S(2)}) %collective-permute-start.1) | collective-permute-done | bytes 327712 | tf_op jit(solution)/shard_map/ppermute | solution.py:402
  38.6 3.9 collective-permute-start.2
  44.5 2.3 concatenate.87
  46.8 37.6 %collective-permute-done.2 = bf16[2,2,320,256]{3,2,1,0:T(8,128)(2,1)} collective-permute-done((bf16[2,2,320,256]{3,2,1,0:T(8,128)(2,1)}, bf16[2,2,320,256]{3,2,1,0:T(8,128)(2,1)}, u32[]{:S(2)}, u32[]{:S(2)}) %collective-permute-start.2) | collective-permute-done | bytes 655392 | tf_op jit(solution)/shard_map/ppermute | solution.py:402
  93.7 1.7 select_bitcast_fusion.3
  95.4 1.7 pad_maximum_fusion.2
  99.3 3.0 fusion.38
  104.7 3.8 collective-permute-start.8
  108.4 2.6 collective-permute-start.6
  111.1 2.0 collective-permute-start.7
  119.1 18.7 %collective-permute-done.6 = bf16[256,640]{1,0:T(8,128)(2,1)} collective-permute-done((bf16[256,640]{1,0:T(8,128)(2,1)}, bf16[256,640]{1,0:T(8,128)(2,1)}, u32[]{:S(2)}, u32[]{:S(2)}) %collective-permute-start.6) | collective-permute-done | bytes 327712 | tf_op jit(solution)/shard_map/ppermute | solution.py:543
  140.2 11.4 %collective-permute-done.7 = bf16[256,640]{1,0:T(8,128)(2,1)} collective-permute-done((bf16[256,640]{1,0:T(8,128)(2,1)}, bf16[256,640]{1,0:T(8,128)(2,1)}, u32[]{:S(2)}, u32[]{:S(2)}) %collective-permute-start.7) | collective-permute-done | bytes 327712 | tf_op jit(solution)/shard_map/ppermute | solution.py:543
  154.2 5.4 collective-permute-done.11
  159.9 31.5 %collective-permute-done.4 = bf16[2,2,2,2,320,256]{5,4,3,2,1,0:T(8,128)(2,1)} collective-permute-done((bf16[2,2,2,2,320,256]{5,4,3,2,1,0:T(8,128)(2,1)}, bf16[2,2,2,2,320,256]{5,4,3,2,1,0:T(8,128)(2,1)}, u32[]{:S(2)}, u32[]{:S(2)}) %collective-permute-start.4) | collective-permute-done | bytes 2621472 | tf_op jit(solution)/shard_map/ppermute | solution.py:402
  191.3 2.2 select_bitcast_fusion.1
  194.0 3.0 copy.99
  197.1 2.3 copy.120
  199.9 1.7 copy-done.15
  201.8 1.7 copy-done.5
  203.4 6.1 project_queries.1.q_ref
  209.5 44.9 %attend_forward.1 = (bf16[1024,768]{1,0:T(8,128)(2,1)S(1)}, f32[16,1,768]{2,1,0:T(1,128)S(1)}) custom-call(s32[3]{0:T(128)S(1)} %and_select_fusion.place_ref, bf16[768,2048]{1,0:T(8,128)(2,1)S(1)} %project_queries.1.q_ref, bf16[2560,640]{1,0:T(8,128)(2,1)} %copy-done.12, bf16[2560,640]{1,0:T(8,128)(2,1)} %copy-done.12, bf16[256,2048]{1,0:T(8,128)(2,1)S(1)} %slice.225.up_ref), custom_call_target="tpu_custom_call" | custom-call | tf_op jit(solution)/shard_map/attend_forward/pallas_call | solution.py:112
  256.2 3.1 slice_bitcast_fusion
  259.4 4.4 copy.107
  263.8 5.2 multiply_reduce_fusion.2
  268.9 3.4 multiply_convert_fusion.normed_ref
  272.3 50.2 %feed_forward_both.1 = (f32[768,1024]{1,0:T(8,128)}, f32[768,1024]{1,0:T(8,128)}, bf16[4,8,1056,256]{3,2,1,0:T(8,128)(2,1)}) custom-call(bf16[768,1024]{1,0:T(8,128)(2,1)} %multiply_convert_fusion.normed_ref, bf16[768,1024]{1,0:T(8,128)(2,1)} %fusion.12.grad_ref, bf16[4,8,1184,256]{3,2,1,0:T(8,128)(2,1)} %bitcast.143), custom_call_target="tpu_custom_call" | custom-call | tf_op jit(solution)/shard_map/feed_forward_both/pallas_call | solution.py:367
  322.5 3.8 multiply_reduce_fusion
  326.7 4.3 multiply_add_fusion
  331.1 1.7 copy-done.20
  332.7 3.1 convolution_convert_fusion.1
  335.8 4.7 reshape.220
  340.5 3.3 copy.116
  344.6 5.6 fusion.22.grad_ref
  350.2 56.3 %attend_backward.1 = (bf16[768,2048]{1,0:T(8,128)(2,1)}, f32[2560,512]{1,0:T(8,128)}, f32[2560,128]{1,0:T(8,128)}, f32[256,2048]{1,0:T(8,128)}) custom-call(s32[3]{0:T(128)} %copy-done.11, bf16[768,2048]{1,0:T(8,128)(2,1)} %copy-done.2, bf16[2560,640]{1,0:T(8,128)(2,1)} %copy-done.12, bf16[2560,640]{1,0:T(8,128)(2,1)} %copy-done.12, ...), custom_call_target="tpu_custom_call" | custom-call | tf_op jit(solution)/shard_map/attend_backward/pallas_call | solution.py:248
  406.5 2.9 convert.51
  414.9 3.7 convolution_convert_fusion
  420.1 3.0 copy.112
  429.1 119.5 %collective-permute-done.12 = bf16[256,640]{1,0:T(8,128)(2,1)} collective-permute-done((bf16[256,640]{1,0:T(8,128)(2,1)}, bf16[256,640]{1,0:T(8,128)(2,1)}, u32[]{:S(2)}, u32[]{:S(2)}) %collective-permute-start.12) | collective-permute-done | bytes 327712 | tf_op jit(solution)/shard_map/ppermute | solution.py:605
  549.9 35.5 %collective-permute-done.13 = bf16[256,640]{1,0:T(8,128)(2,1)} collective-permute-done((bf16[256,640]{1,0:T(8,128)(2,1)}, bf16[256,640]{1,0:T(8,128)(2,1)}, u32[]{:S(2)}, u32[]{:S(2)}) %collective-permute-start.13) | collective-permute-done | bytes 327712 | tf_op jit(solution)/shard_map/ppermute | solution.py:605
  586.3 3.1 pad_maximum_fusion.1
  589.4 1.7 dynamic-slice_bitcast_fusion
  591.1 8.4 %collective-permute-done.15 = bf16[256,640]{1,0:T(8,128)(2,1)} collective-permute-done((bf16[256,640]{1,0:T(8,128)(2,1)}, bf16[256,640]{1,0:T(8,128)(2,1)}, u32[]{:S(2)}, u32[]{:S(2)}) %collective-permute-start.15) | collective-permute-done | bytes 327712 | tf_op jit(solution)/shard_map/ppermute | solution.py:605
  599.5 13.3 %collective-permute-done.17 = bf16[256,640]{1,0:T(8,128)(2,1)S(1)} collective-permute-done((bf16[256,640]{1,0:T(8,128)(2,1)}, bf16[256,640]{1,0:T(8,128)(2,1)S(1)}, u32[]{:S(2)}, u32[]{:S(2)}) %collective-permute-start.17) | collective-permute-done | bytes 327712 | tf_op jit(solution)/shard_map/ppermute | solution.py:605
  612.8 1.9 convert_add_fusion.9
  623.3 5.5 fusion.10
  630.6 2.8 concatenate.106
  634.3 2.5 collective-permute-done.19
  638.1 3.6 fusion
  647.1 52.4 %collective-permute-done.20 = bf16[2,2,2,32,640]{4,3,0,1,2:T(8,128)(2,1)S(1)} collective-permute-done((bf16[2,2,2,32,640]{4,3,0,1,2:T(8,128)(2,1)}, bf16[2,2,2,32,640]{4,3,0,1,2:T(8,128)(2,1)S(1)}, u32[]{:S(2)}, u32[]{:S(2)}) %collective-permute-start.20) | collective-permute-done | bytes 327712 | tf_op jit(solution)/shard_map/ppermute | solution.py:429
  700.9 7.2 collective-permute-done.21
  708.1 3.9 collective-permute-start.22
  712.0 1.7 fusion.13
  713.9 2.5 fusion.9
  716.5 30.2 %collective-permute-start.23 = (bf16[32,640]{1,0:T(8,128)(2,1)S(1)}, bf16[32,640]{1,0:T(8,128)(2,1)S(1)}, u32[]{:S(2)}, u32[]{:S(2)}) collective-permute-start(bf16[32,640]{1,0:T(8,128)(2,1)S(1)} %dynamic-slice_bitcast_fusion.11), channel_id=1, source_target_pairs={{0,4},{1,5},{2,6},{3,7},{4,0},{5,1},{6,2},{7,3},{8,12},{9,13},{10,... | collective-permute-start | bytes 122888 | tf_op jit(solution)/shard_map/ppermute | solution.py:429
  746.9 2.2 collective-permute-start.27
  749.1 2.3 collective-permute-done.23
  753.5 20.5 %collective-permute-done.27 = bf16[2,320,256]{2,1,0:T(8,128)(2,1)S(1)} collective-permute-done((bf16[2,320,256]{2,1,0:T(8,128)(2,1)S(1)}, bf16[2,320,256]{2,1,0:T(8,128)(2,1)S(1)}, u32[]{:S(2)}, u32[]{:S(2)}) %collective-permute-start.27) | collective-permute-done | bytes 327712 | tf_op jit(solution)/shard_map/ppermute | solution.py:429
  774.0 5.4 collective-permute-start.28
  779.5 1.5 bitcast_convert_fusion
  781.0 3.5 collective-permute-done.28
  788.3 22.5 %reduce-scatter.5.cloned.1.call-done = bf16[1,1056,256]{2,1,0:T(8,128)(2,1)} async-done(((bf16[32,1056,256]{2,1,0:T(8,128)(2,1)}), bf16[1,1056,256]{2,1,0:T(8,128)(2,1)}) %reduce-scatter.5.cloned.1.call-update) | async-done | bytes 540688 | tf_op jit(solution)/shard_map/reduce_scatter | solution.py:579
  (297 shorter events, 79.4 us)
Async XLA Ops:
  7.2 4.4 copy-start.49
  7.2 4.5 copy-start.50
  7.2 249.0 %all-gather.2.cloned.1.call-start = ((), (), s32[]{:S(2)}) async-start(), calls=%async_computation.2 | async-start | bytes 20004864 | tf_op jit(solution)/shard_map/all_gather | solution.py:501
  11.1 768.4 %reduce-scatter.3.cloned.1.call-start = ((), (), s32[]{:S(2)}) async-start(), calls=%async_computation.3 | async-start | bytes 2162688 | tf_op jit(solution)/shard_map/reduce_scatter | solution.py:588
  11.4 31.1 %copy-start.58 = (bf16[1024]{0:T(1024)(128)(2,1)S(1)}, bf16[1024]{0:T(1024)(128)(2,1)}, u32[]{:S(2)}) copy-start(bf16[1024]{0:T(1024)(128)(2,1)} %param.20) | copy-start | bytes 6148
  11.4 31.1 %copy-start.47 = (bf16[1024,32]{0,1:T(8,128)(2,1)S(1)}, bf16[1024,32]{0,1:T(8,128)(2,1)}, u32[]{:S(2)}) copy-start(bf16[1024,32]{0,1:T(8,128)(2,1)} %param.24) | copy-start | bytes 196612
  11.9 32.6 %copy-start.45 = (bf16[1024,512]{1,0:T(8,128)(2,1)S(1)}, bf16[1024,512]{1,0:T(8,128)(2,1)}, u32[]{:S(2)}) copy-start(bf16[1024,512]{1,0:T(8,128)(2,1)} %param.23) | copy-start | bytes 3145732
  12.3 7.2 collective-permute-start
  19.7 18.0 %collective-permute-start.1 = (bf16[2,320,256]{2,1,0:T(8,128)(2,1)S(1)}, bf16[2,320,256]{2,1,0:T(8,128)(2,1)S(1)}, u32[]{:S(2)}, u32[]{:S(2)}) collective-permute-start(bf16[2,320,256]{2,1,0:T(8,128)(2,1)S(1)} %pad_maximum_fusion.14), channel_id=1, source_target_pairs={{0,2},{1,3},{2,0},{3,1},{4,6},{5,7},{6,4},{7,5},{8,10},{9,11},{10,... | collective-permute-start | bytes 983048 | tf_op jit(solution)/shard_map/ppermute | solution.py:402
  38.6 45.8 %collective-permute-start.2 = (bf16[2,2,320,256]{3,2,1,0:T(8,128)(2,1)}, bf16[2,2,320,256]{3,2,1,0:T(8,128)(2,1)}, u32[]{:S(2)}, u32[]{:S(2)}) collective-permute-start(bf16[2,2,320,256]{3,2,1,0:T(8,128)(2,1)} %pad_maximum_fusion.7), channel_id=1, source_target_pairs={{0,4},{1,5},{2,6},{3,7},{4,0},{5,1},{6,2},{7,3},{8,12},{9,13},{10,... | collective-permute-start | bytes 1966088 | tf_op jit(solution)/shard_map/ppermute | solution.py:402
  46.8 40.9 %copy-start.42 = (bf16[1024,640]{1,0:T(8,128)(2,1)}, bf16[1024,640]{1,0:T(8,128)(2,1)S(1)}, u32[]{:S(2)}) copy-start(bf16[1024,640]{1,0:T(8,128)(2,1)S(1)} %concatenate.87) | copy-start | bytes 3932164
  46.8 40.0 %copy-start.17 = (bf16[768,1024]{1,0:T(8,128)(2,1)S(1)}, bf16[768,1024]{1,0:T(8,128)(2,1)}, u32[]{:S(2)}) copy-start(bf16[768,1024]{1,0:T(8,128)(2,1)} %param.16) | copy-start | bytes 4718596
  86.8 6.9 collective-permute-start.3
  92.0 7.1 copy-start.53
  92.1 7.1 copy-start.56
  97.2 5.1 copy-start.23
  97.2 94.2 %collective-permute-start.4 = (bf16[2,2,2,2,320,256]{5,4,3,2,1,0:T(8,128)(2,1)}, bf16[2,2,2,2,320,256]{5,4,3,2,1,0:T(8,128)(2,1)}, u32[]{:S(2)}, u32[]{:S(2)}) collective-permute-start(bf16[2,2,2,2,320,256]{5,4,3,2,1,0:T(8,128)(2,1)} %pad_maximum_fusion.2), channel_id=1, source_target_pairs={{0,16},{8,24},{16,0},{24,8},{1,17},{9,25},{17,1},{25,9},{2,18},{10... | collective-permute-start | bytes 7864328 | tf_op jit(solution)/shard_map/ppermute | solution.py:402
  99.3 13.9 %copy-start.64 = (f32[4]{0:T(128)S(1)}, f32[4]{0:T(128)}, u32[]{:S(2)}) copy-start(f32[4]{0:T(128)} %param.19) | copy-start | bytes 52
  99.3 13.9 %copy-start.65 = (s32[3]{0:T(128)S(1)}, s32[3]{0:T(128)}, u32[]{:S(2)}) copy-start(s32[3]{0:T(128)} %param.18) | copy-start | bytes 40
  99.3 14.1 %copy-start.25 = (bf16[768,1024]{1,0:T(8,128)(2,1)S(1)}, bf16[768,1024]{1,0:T(8,128)(2,1)}, u32[]{:S(2)}) copy-start(bf16[768,1024]{1,0:T(8,128)(2,1)} %param.17) | copy-start | bytes 4718596
  102.3 12.6 %copy-start.38 = (bf16[768,128]{1,0:T(8,128)(2,1)}, bf16[768,128]{1,0:T(8,128)(2,1)S(1)}, u32[]{:S(2)}) copy-start(bf16[768,128]{1,0:T(8,128)(2,1)S(1)} %get-tuple-element.111) | copy-start | bytes 589828
  102.3 12.6 %copy-start.54 = (f32[128]{0:T(128)S(1)}, f32[128]{0:T(128)}, u32[]{:S(2)}) copy-start(f32[128]{0:T(128)} %copy-done.53) | copy-start | bytes 1540
  103.3 13.4 %collective-permute-start.5 = (bf16[256,640]{1,0:T(8,128)(2,1)}, bf16[256,640]{1,0:T(8,128)(2,1)}, u32[]{:S(2)}, u32[]{:S(2)}) collective-permute-start(bf16[256,640]{1,0:T(8,128)(2,1)} %get-tuple-element.106), channel_id=1, source_target_pairs={{2,5},{10,13},{18,21},{26,29}} | collective-permute-start | bytes 983048 | tf_op jit(solution)/shard_map/ppermute | solution.py:543
  104.7 49.4 %collective-permute-start.8 = (bf16[256,640]{1,0:T(8,128)(2,1)}, bf16[256,640]{1,0:T(8,128)(2,1)S(1)}, u32[]{:S(2)}, u32[]{:S(2)}) collective-permute-start(bf16[256,640]{1,0:T(8,128)(2,1)} %get-tuple-element.106), channel_id=1, source_target_pairs={{0,2},{2,4},{3,5},{5,7},{8,10},{10,12},{11,13},{13,15},{16,18},{18... | collective-permute-start | bytes 983048 | tf_op jit(solution)/shard_map/ppermute | solution.py:543
  108.4 29.4 %collective-permute-start.6 = (bf16[256,640]{1,0:T(8,128)(2,1)}, bf16[256,640]{1,0:T(8,128)(2,1)}, u32[]{:S(2)}, u32[]{:S(2)}) collective-permute-start(bf16[256,640]{1,0:T(8,128)(2,1)} %get-tuple-element.107), channel_id=1, source_target_pairs={{0,2},{3,5},{8,10},{11,13},{16,18},{19,21},{24,26},{27,29}} | collective-permute-start | bytes 983048 | tf_op jit(solution)/shard_map/ppermute | solution.py:543
  111.1 40.5 %collective-permute-start.7 = (bf16[256,640]{1,0:T(8,128)(2,1)}, bf16[256,640]{1,0:T(8,128)(2,1)}, u32[]{:S(2)}, u32[]{:S(2)}) collective-permute-start(bf16[256,640]{1,0:T(8,128)(2,1)} %get-tuple-element.105), channel_id=1, source_target_pairs={{0,2},{3,5},{5,7},{8,10},{11,13},{13,15},{16,18},{19,21},{21,23},{... | collective-permute-start | bytes 983048 | tf_op jit(solution)/shard_map/ppermute | solution.py:543
  114.9 44.8 %copy-start.39 = (bf16[768,128]{1,0:T(8,128)(2,1)S(1)}, bf16[768,128]{1,0:T(8,128)(2,1)}, u32[]{:S(2)}) copy-start(bf16[768,128]{1,0:T(8,128)(2,1)} %copy-done.38) | copy-start | bytes 589828
  116.6 43.1 %copy-start.24 = (bf16[768,512]{1,0:T(8,128)(2,1)S(1)}, bf16[768,512]{1,0:T(8,128)(2,1)}, u32[]{:S(2)}) copy-start(bf16[768,512]{1,0:T(8,128)(2,1)} %slice.375) | copy-start | bytes 2359300
  116.7 92.8 %copy-start.11 = (s32[3]{0:T(128)}, s32[3]{0:T(128)S(1)}, u32[]{:S(2)}) copy-start(s32[3]{0:T(128)S(1)} %and_select_fusion.place_ref) | copy-start | bytes 40
  116.7 37.4 %collective-permute-start.9 = (bf16[256,640]{1,0:T(8,128)(2,1)}, bf16[256,640]{1,0:T(8,128)(2,1)S(1)}, u32[]{:S(2)}, u32[]{:S(2)}) collective-permute-start(bf16[256,640]{1,0:T(8,128)(2,1)} %get-tuple-element.107), channel_id=1, source_target_pairs={{0,1},{1,2},{3,4},{4,5},{6,7},{8,9},{9,10},{11,12},{12,13},{14,15}... | collective-permute-start | bytes 983048 | tf_op jit(solution)/shard_map/ppermute | solution.py:543
  137.8 16.3 %collective-permute-start.10 = (bf16[256,640]{1,0:T(8,128)(2,1)}, bf16[256,640]{1,0:T(8,128)(2,1)S(1)}, u32[]{:S(2)}, u32[]{:S(2)}) collective-permute-start(bf16[256,640]{1,0:T(8,128)(2,1)} %get-tuple-element.105), channel_id=1, source_target_pairs={{0,1},{1,2},{3,4},{4,5},{5,6},{6,7},{8,9},{9,10},{11,12},{12,13},{... | collective-permute-start | bytes 983048 | tf_op jit(solution)/shard_map/ppermute | solution.py:543
  151.6 8.1 collective-permute-start.11
  159.9 33.7 %copy-start.12 = (bf16[2560,640]{1,0:T(8,128)(2,1)}, bf16[2560,640]{1,0:T(8,128)(2,1)S(1)}, u32[]{:S(2)}) copy-start(bf16[2560,640]{1,0:T(8,128)(2,1)S(1)} %fusion.27.latent_ref.rope_ref) | copy-start | bytes 9830404
  201.7 7.8 copy-start.3
  209.5 44.9 %copy-start.2 = (bf16[768,2048]{1,0:T(8,128)(2,1)}, bf16[768,2048]{1,0:T(8,128)(2,1)S(1)}, u32[]{:S(2)}) copy-start(bf16[768,2048]{1,0:T(8,128)(2,1)S(1)} %project_queries.1.q_ref) | copy-start | bytes 9437188
  259.4 4.4 copy-start.9
  259.4 4.4 copy-start.18
  343.8 467.1 %reduce-scatter.5.cloned.1.call-start = ((), (), s32[]{:S(2)}) async-start(), calls=%async_computation.4 | async-start | bytes 17842176 | tf_op jit(solution)/shard_map/reduce_scatter | solution.py:579
  409.5 5.4 copy-start.6
  409.5 5.4 copy-start.62
  412.1 136.5 %collective-permute-start.12 = (bf16[256,640]{1,0:T(8,128)(2,1)}, bf16[256,640]{1,0:T(8,128)(2,1)}, u32[]{:S(2)}, u32[]{:S(2)}) collective-permute-start(bf16[256,640]{1,0:T(8,128)(2,1)} %get-tuple-element.85), channel_id=1, source_target_pairs={{1,0},{2,1},{4,3},{5,4},{7,6},{9,8},{10,9},{12,11},{13,12},{15,14}... | collective-permute-start | bytes 983048 | tf_op jit(solution)/shard_map/ppermute | solution.py:605
  413.6 171.9 %collective-permute-start.13 = (bf16[256,640]{1,0:T(8,128)(2,1)}, bf16[256,640]{1,0:T(8,128)(2,1)}, u32[]{:S(2)}, u32[]{:S(2)}) collective-permute-start(bf16[256,640]{1,0:T(8,128)(2,1)} %get-tuple-element.86), channel_id=1, source_target_pairs={{2,0},{5,3},{10,8},{13,11},{18,16},{21,19},{26,24},{29,27}} | collective-permute-start | bytes 983048 | tf_op jit(solution)/shard_map/ppermute | solution.py:605
  424.8 166.3 %collective-permute-start.14 = (bf16[256,640]{1,0:T(8,128)(2,1)}, bf16[256,640]{1,0:T(8,128)(2,1)}, u32[]{:S(2)}, u32[]{:S(2)}) collective-permute-start(bf16[256,640]{1,0:T(8,128)(2,1)} %get-tuple-element.87), channel_id=1, source_target_pairs={{1,0},{2,1},{4,3},{5,4},{6,5},{7,6},{9,8},{10,9},{12,11},{13,12},{... | collective-permute-start | bytes 983048 | tf_op jit(solution)/shard_map/ppermute | solution.py:605
  426.1 173.4 %collective-permute-start.15 = (bf16[256,640]{1,0:T(8,128)(2,1)}, bf16[256,640]{1,0:T(8,128)(2,1)}, u32[]{:S(2)}, u32[]{:S(2)}) collective-permute-start(bf16[256,640]{1,0:T(8,128)(2,1)} %get-tuple-element.88), channel_id=1, source_target_pairs={{2,0},{5,3},{7,5},{10,8},{13,11},{15,13},{18,16},{21,19},{23,21},{... | collective-permute-start | bytes 983048 | tf_op jit(solution)/shard_map/ppermute | solution.py:605
  427.4 172.1 %collective-permute-start.16 = (bf16[256,640]{1,0:T(8,128)(2,1)}, bf16[256,640]{1,0:T(8,128)(2,1)}, u32[]{:S(2)}, u32[]{:S(2)}) collective-permute-start(bf16[256,640]{1,0:T(8,128)(2,1)} %get-tuple-element.89), channel_id=1, source_target_pairs={{1,0},{2,1},{3,2},{4,3},{5,4},{6,5},{7,6},{9,8},{10,9},{11,10},{12... | collective-permute-start | bytes 983048 | tf_op jit(solution)/shard_map/ppermute | solution.py:605
  548.6 64.1 %collective-permute-start.17 = (bf16[256,640]{1,0:T(8,128)(2,1)}, bf16[256,640]{1,0:T(8,128)(2,1)S(1)}, u32[]{:S(2)}, u32[]{:S(2)}) collective-permute-start(bf16[256,640]{1,0:T(8,128)(2,1)} %get-tuple-element.91), channel_id=1, source_target_pairs={{2,0},{4,2},{5,3},{7,5},{10,8},{12,10},{13,11},{15,13},{18,16},{20... | collective-permute-start | bytes 983048 | tf_op jit(solution)/shard_map/ppermute | solution.py:605
  585.4 27.3 %collective-permute-start.18 = (bf16[256,640]{1,0:T(8,128)(2,1)}, bf16[256,640]{1,0:T(8,128)(2,1)S(1)}, u32[]{:S(2)}, u32[]{:S(2)}) collective-permute-start(bf16[256,640]{1,0:T(8,128)(2,1)} %get-tuple-element.90), channel_id=1, source_target_pairs={{5,2},{13,10},{21,18},{29,26}} | collective-permute-start | bytes 983048 | tf_op jit(solution)/shard_map/ppermute | solution.py:605
  589.4 25.8 %copy-start.16 = (bf16[4,320,8,256]{3,1,2,0:T(8,128)(2,1)}, bf16[4,320,8,256]{3,1,2,0:T(8,128)(2,1)S(1)}, u32[]{:S(2)}) copy-start(bf16[4,320,8,256]{3,1,2,0:T(8,128)(2,1)S(1)} %pad_maximum_fusion.1) | copy-start | bytes 15728644
  589.4 23.4 %copy-start.14 = (bf16[2560,512]{1,0:T(8,128)(2,1)S(1)}, bf16[2560,512]{1,0:T(8,128)(2,1)}, u32[]{:S(2)}) copy-start(bf16[2560,512]{1,0:T(8,128)(2,1)} %copy-done.13) | copy-start | bytes 7864324
  589.4 23.3 %copy-start.28 = (bf16[2560,128]{1,0:T(8,128)(2,1)S(1)}, bf16[2560,128]{1,0:T(8,128)(2,1)}, u32[]{:S(2)}) copy-start(bf16[2560,128]{1,0:T(8,128)(2,1)} %copy-done.27) | copy-start | bytes 1966084
  591.1 47.0 %collective-permute-start.24 = (bf16[2,2,2,2,320,256]{5,4,3,2,1,0:T(8,128)(2,1)}, bf16[2,2,2,2,320,256]{5,4,3,2,1,0:T(8,128)(2,1)}, u32[]{:S(2)}, u32[]{:S(2)}) collective-permute-start(bf16[2,2,2,2,320,256]{5,4,3,2,1,0:T(8,128)(2,1)} %dynamic-slice_bitcast_fusion), channel_id=1, source_target_pairs={{0,8},{8,0},{16,24},{24,16},{1,9},{9,1},{17,25},{25,17},{2,10},{10... | collective-permute-start | bytes 7864328 | tf_op jit(solution)/shard_map/ppermute | solution.py:429
  634.3 2.5 collective-permute-start.19
  638.1 7.3 copy-start.35
  644.3 67.7 %collective-permute-start.25 = (bf16[2,2,2,320,256]{4,3,2,1,0:T(8,128)(2,1)}, bf16[2,2,2,320,256]{4,3,2,1,0:T(8,128)(2,1)S(1)}, u32[]{:S(2)}, u32[]{:S(2)}) collective-permute-start(bf16[2,2,2,320,256]{4,3,2,1,0:T(8,128)(2,1)} %dynamic-slice_bitcast_fusion.1), channel_id=1, source_target_pairs={{0,16},{8,24},{16,0},{24,8},{1,17},{9,25},{17,1},{25,9},{2,18},{10... | collective-permute-start | bytes 3932168 | tf_op jit(solution)/shard_map/ppermute | solution.py:429
  646.2 53.3 %collective-permute-start.20 = (bf16[2,2,2,32,640]{4,3,0,1,2:T(8,128)(2,1)}, bf16[2,2,2,32,640]{4,3,0,1,2:T(8,128)(2,1)S(1)}, u32[]{:S(2)}, u32[]{:S(2)}) collective-permute-start(bf16[2,2,2,32,640]{4,3,0,1,2:T(8,128)(2,1)} %dynamic-slice_bitcast_fusion.5), channel_id=1, source_target_pairs={{0,16},{8,24},{16,0},{24,8},{1,17},{9,25},{17,1},{25,9},{2,18},{10... | collective-permute-start | bytes 983048 | tf_op jit(solution)/shard_map/ppermute | solution.py:429
  699.5 14.4 %copy-start.34 = (f32[768,1024]{1,0:T(8,128)S(1)}, f32[768,1024]{1,0:T(8,128)}, u32[]{:S(2)}) copy-start(f32[768,1024]{1,0:T(8,128)} %get-tuple-element.130) | copy-start | bytes 9437188
  700.8 13.1 %copy-start.21 = (f32[768,1024]{1,0:T(8,128)S(1)}, f32[768,1024]{1,0:T(8,128)}, u32[]{:S(2)}) copy-start(f32[768,1024]{1,0:T(8,128)} %copy-done.20) | copy-start | bytes 9437188
  700.8 7.3 collective-permute-start.21
  708.1 8.3 %collective-permute-start.22 = (bf16[2,32,640]{2,1,0:T(8,128)(2,1)S(1)}, bf16[2,32,640]{2,1,0:T(8,128)(2,1)S(1)}, u32[]{:S(2)}, u32[]{:S(2)}) collective-permute-start(bf16[2,32,640]{2,1,0:T(8,128)(2,1)S(1)} %dynamic-slice_bitcast_fusion.10), channel_id=1, source_target_pairs={{0,2},{1,3},{2,0},{3,1},{4,6},{5,7},{6,4},{7,5},{8,10},{9,11},{10,... | collective-permute-start | bytes 245768 | tf_op jit(solution)/shard_map/ppermute | solution.py:429
  713.8 32.9 %collective-permute-start.26 = (bf16[2,2,320,256]{3,2,1,0:T(8,128)(2,1)S(1)}, bf16[2,2,320,256]{3,2,1,0:T(8,128)(2,1)S(1)}, u32[]{:S(2)}, u32[]{:S(2)}) collective-permute-start(bf16[2,2,320,256]{3,2,1,0:T(8,128)(2,1)S(1)} %dynamic-slice_bitcast_fusion.2), channel_id=1, source_target_pairs={{0,1},{1,0},{2,3},{3,2},{4,5},{5,4},{6,7},{7,6},{8,9},{9,8},{10,11... | collective-permute-start | bytes 1966088 | tf_op jit(solution)/shard_map/ppermute | solution.py:429
  716.5 35.0 %collective-permute-start.23 = (bf16[32,640]{1,0:T(8,128)(2,1)S(1)}, bf16[32,640]{1,0:T(8,128)(2,1)S(1)}, u32[]{:S(2)}, u32[]{:S(2)}) collective-permute-start(bf16[32,640]{1,0:T(8,128)(2,1)S(1)} %dynamic-slice_bitcast_fusion.11), channel_id=1, source_target_pairs={{0,4},{1,5},{2,6},{3,7},{4,0},{5,1},{6,2},{7,3},{8,12},{9,13},{10,... | collective-permute-start | bytes 122888 | tf_op jit(solution)/shard_map/ppermute | solution.py:429
  746.9 27.0 %collective-permute-start.27 = (bf16[2,320,256]{2,1,0:T(8,128)(2,1)S(1)}, bf16[2,320,256]{2,1,0:T(8,128)(2,1)S(1)}, u32[]{:S(2)}, u32[]{:S(2)}) collective-permute-start(bf16[2,320,256]{2,1,0:T(8,128)(2,1)S(1)} %dynamic-slice_bitcast_fusion.4), channel_id=1, source_target_pairs={{0,2},{1,3},{2,0},{3,1},{4,6},{5,7},{6,4},{7,5},{8,10},{9,11},{10,... | collective-permute-start | bytes 983048 | tf_op jit(solution)/shard_map/ppermute | solution.py:429
  774.0 10.5 %collective-permute-start.28 = (bf16[320,256]{1,0:T(8,128)(2,1)S(1)}, bf16[320,256]{1,0:T(8,128)(2,1)S(1)}, u32[]{:S(2)}, u32[]{:S(2)}) collective-permute-start(bf16[320,256]{1,0:T(8,128)(2,1)S(1)} %dynamic-slice_bitcast_fusion.8), channel_id=1, source_target_pairs={{0,4},{1,5},{2,6},{3,7},{4,0},{5,1},{6,2},{7,3},{8,12},{9,13},{10,... | collective-permute-start | bytes 491528 | tf_op jit(solution)/shard_map/ppermute | solution.py:429
  784.6 28.4 %copy-start.1 = (bf16[352,1024]{1,0:T(8,128)(2,1)S(1)}, bf16[352,1024]{1,0:T(8,128)(2,1)}, u32[]{:S(2)}) copy-start(bf16[352,1024]{1,0:T(8,128)(2,1)} %param.31) | copy-start | bytes 2162692
  (36 other events, 92.1 us)
Sparse Core Ops, SparseCore 0:
  11.2 186.0 all-gather.1
  343.9 237.6 reduce-scatter.2
  589.3 221.5 reduce-scatter.4

commit v2 on v1

v2 whole, which is shorter than its diff:
```python
import functools
import math

import jax
import jax.numpy as jnp
from jax import lax
from jax.experimental import pallas as pl
from jax.experimental.pallas import tpu as pltpu
from jax.sharding import PartitionSpec as P

D = 1024
HEADS = 16
HD = 64
LGROUPS = 2
LAT = 256
RD = 32
LEN = 2048
EPS = 1e-05
THETA = 10000.0
NEG_LARGE = -1e30
LANES = 128
PAIR = 2
GROUP = HEADS // LGROUPS
TALL = 80
CHUNKS = 4
SHARES = (2, 2, 1)
LOG2E = math.log2(math.e)
LN2 = math.log(2.0)
SCALE = (HD + RD) ** (-0.5)

bf16 = jnp.bfloat16
f32 = jnp.float32


def dot_nn(a, b):
    return jnp.dot(a, b, preferred_element_type=f32)


def dot_nt(a, b):
    return lax.dot_general(a, b, (((1,), (1,)), ((), ())), preferred_element_type=f32)


def dot_tn(a, b):
    return lax.dot_general(a, b, (((0,), (0,)), ((), ())), preferred_element_type=f32)


def rms_scale(values):
    return lax.rsqrt(jnp.mean(values * values, axis=-1, keepdims=True) + EPS)


def norm_backward(source, scale_rows, gain, grad_normed):
    scaled = source * scale_rows
    weighted = grad_normed * gain
    grad_source = scale_rows * (
        weighted - scaled * jnp.mean(weighted * scaled, axis=-1, keepdims=True)
    )
    return (grad_source, jnp.sum(grad_normed * scaled, axis=0))


def keys_values(groups, latent_ref, rope_ref, up_ref, rows, count):
    rope = rope_ref[rows, :]
    lane = lax.broadcasted_iota(jnp.int32, (count, LANES), 1)
    keys, values = [], []
    for e in range(0, GROUP, PAIR):
        latent = latent_ref[rows, groups[e] * LAT : (groups[e] + 1) * LAT]
        up = [up_ref[:, e + i].reshape(LAT, LANES) for i in range(PAIR)]
        up = jnp.concatenate(up, axis=1)
        wide = dot_nn(latent, up).astype(bf16)
        for i in range(PAIR):
            both = wide[:, i * LANES : (i + 1) * LANES]
            keys.append(jnp.where(lane < HD, both, rope))
            values.append(both)
    return keys, values


def values_ones(value):
    count = value.shape[0]
    return jnp.concatenate([value.T[HD:], jnp.ones((TALL - HD, count), bf16)], axis=0)


def attend_forward_kernel(
    groups, block, own, halo, place_ref, q_ref, latent_ref, rope_ref, up_ref, mixed_ref, log_ref,
    query_s, top_s, sum_s,
):
    rows = own * block
    ahead, until = place_ref[0], place_ref[1]
    for e in range(GROUP):
        query_s[e] = q_ref[:, e * LANES : (e + 1) * LANES].T
    keys, values = keys_values(
        groups, latent_ref, rope_ref, up_ref, slice(halo * block, (halo + own) * block), rows
    )
    values = [values_ones(value) for value in values]
    for j in range(own):
        count = (j + 1) * block
        key_at = lax.broadcasted_iota(jnp.int32, (count, block), 0)
        query_at = lax.broadcasted_iota(jnp.int32, (count, block), 1) + j * block
        keep = (key_at <= query_at) & (key_at >= jnp.where(j >= until, until * block, 0))
        cols = slice(j * block, count)
        scores = [
            jnp.where(keep, dot_nn(keys[e][:count], query_s[e, :, cols]), NEG_LARGE)
            for e in range(GROUP)
        ]
        for e in range(GROUP):
            top = jnp.max(scores[e], axis=0, keepdims=True)
            terms = jnp.exp2(scores[e] - top).astype(bf16)
            top_s[e, :, cols] = top
            sum_s[e, :, cols] = dot_nn(values[e][:, :count], terms)
    for blocks in range(1, own + 1):
        wide = blocks * block

        def step(index, _):
            at = pl.ds(pl.multiple_of(index * block, block), block)
            keys, values = keys_values(groups, latent_ref, rope_ref, up_ref, at, block)
            values = [values_ones(value) for value in values]
            scores = [dot_nn(keys[e], query_s[e, :, :wide]) for e in range(GROUP)]
            for e in range(GROUP):
                top = top_s[e, :, :wide]
                higher = jnp.maximum(top, jnp.max(scores[e], axis=0, keepdims=True))
                shrink = jnp.exp2(top - higher)
                terms = jnp.exp2(scores[e] - higher).astype(bf16)
                top_s[e, :, :wide] = higher
                sum_s[e, :, :wide] = sum_s[e, :, :wide] * shrink + dot_nn(values[e], terms)
            return 0

        lax.fori_loop(jnp.where(until == blocks, halo - ahead, halo), halo, step, 0)
    for e in range(GROUP):
        total = sum_s[e]
        sums = total[HD : HD + 1]
        mixed_ref[e * HD : (e + 1) * HD, :] = (total[:HD] * (1.0 / sums)).astype(bf16)
        log_ref[e] = top_s[e] + jnp.log2(sums)


def attend_forward(part, groups, places, queries, window, up_weight, block, own, halo):
    rows, wide = own * block, (halo + own) * block
    cuts, shards, once = up_weight.shape[0], up_weight.shape[1], pl.Buffered(1)
    return pl.pallas_call(
        functools.partial(attend_forward_kernel, groups, block, own, halo),
        grid_spec=pltpu.PrefetchScalarGridSpec(
            num_scalar_prefetch=1,
            grid=(1,),
            in_specs=[
                pl.BlockSpec(
                    (None, rows, GROUP * LANES),
                    lambda g, p: (part * GROUP // shards, 0, part * GROUP % shards // GROUP),
                    pipeline_mode=once,
                ),
                pl.BlockSpec((wide, LGROUPS * LAT), lambda g, p: (0, 0)),
                pl.BlockSpec((wide, LANES), lambda g, p: (0, LGROUPS * LAT // LANES)),
                pl.BlockSpec(
                    (cuts, GROUP, LAT // cuts, LANES),
                    lambda g, p: (0, part * GROUP % shards // GROUP, D // LAT, part * GROUP // shards),
                    pipeline_mode=once,
                ),
            ],
            out_specs=[
                pl.BlockSpec((GROUP * HD, rows), lambda g, p: (0, 0)),
                pl.BlockSpec((GROUP, 1, rows), lambda g, p: (0, 0, 0)),
            ],
            scratch_shapes=[
                pltpu.VMEM((GROUP, LANES, rows), bf16),
                pltpu.VMEM((GROUP, 1, rows), f32),
                pltpu.VMEM((GROUP, TALL, rows), f32),
            ],
        ),
        out_shape=[
            jax.ShapeDtypeStruct((GROUP * HD, rows), bf16),
            jax.ShapeDtypeStruct((GROUP, 1, rows), f32),
        ],
        compiler_params=pltpu.CompilerParams(vmem_limit_bytes=56 << 20),
        cost_estimate=pl.CostEstimate(
            flops=40 * 10**9, bytes_accessed=30 * 10**6, transcendentals=0
        ),
        name="attend_forward",
    )(places, queries, window, window, up_weight)


def attend_backward_kernel(
    groups, block, own, halo, place_ref, q_ref, latent_ref, rope_ref, up_ref, mixed_ref, log_ref,
    grad_ref, cos_ref, low_ref, high_ref, dq_ref, dlatent_ref, drope_ref, dup_ref,
    query_s, grad_s, inner_s, dquery_s, both_s,
):
    rows = own * block
    ahead, until = place_ref[0], place_ref[1]
    first = halo - ahead
    drope_ref[...] = jnp.zeros_like(drope_ref)

    def clear(index, _):
        at = pl.ds(pl.multiple_of(index * block, block), block)
        both_s[at, :] = jnp.zeros((block, GROUP * LANES), bf16)
        return 0

    lax.fori_loop(0, first, clear, 0)
    for e in range(GROUP):
        query_s[e] = q_ref[:, e * LANES : (e + 1) * LANES].T
        grad = grad_ref[e * HD : (e + 1) * HD, :]
        grad_s[e] = jnp.concatenate([jnp.zeros((rows, HD), bf16), grad.T], axis=1)
        inner_s[e] = jnp.sum(
            grad.astype(f32) * mixed_ref[e * HD : (e + 1) * HD, :].astype(f32),
            axis=0,
            keepdims=True,
        )
        dquery_s[e] = jnp.zeros((LANES, rows), f32)
    lane = lax.broadcasted_iota(jnp.int32, (block, LANES), 1)

    def strip(at, low, high, keep):
        cols = slice(low, high)
        keys, values = keys_values(groups, latent_ref, rope_ref, up_ref, at, block)
        scores = [dot_nn(keys[e], query_s[e, :, cols]) for e in range(GROUP)]
        grads = [
            dot_nn(values[e][:, HD:], grad_ref[e * HD : (e + 1) * HD, cols]) for e in range(GROUP)
        ]
        grad_rope = None
        for e in range(GROUP):
            score = scores[e] if keep is None else jnp.where(keep, scores[e], NEG_LARGE)
            probs = jnp.exp2(score - log_ref[e, :, cols])
            grad_scores = (probs * (grads[e] - inner_s[e, :, cols])).astype(bf16)
            grad_value = dot_nn(probs.astype(bf16), grad_s[e, cols, :])
            grad_key = dot_nn(grad_scores, q_ref[cols, e * LANES : (e + 1) * LANES]) * LN2
            dquery_s[e, :, cols] += dot_nn(keys[e].T, grad_scores)
            both_s[at, e * LANES : (e + 1) * LANES] = jnp.where(
                lane < HD, grad_key, grad_value
            ).astype(bf16)
            grad_rope = grad_key if grad_rope is None else grad_rope + grad_key
        drope_ref[at, :] = grad_rope

    for i in range(own):
        count = rows - i * block
        key_at = lax.broadcasted_iota(jnp.int32, (block, count), 0)
        query_at = lax.broadcasted_iota(jnp.int32, (block, count), 1)
        keep = (key_at <= query_at) & (query_at < jnp.where(i < until, (until - i) * block, rows))
        strip(slice((halo + i) * block, (halo + i + 1) * block), i * block, rows, keep)
    for blocks in range(1, own + 1):

        def step(index, _):
            strip(pl.ds(pl.multiple_of(index * block, block), block), 0, blocks * block, None)
            return 0

        lax.fori_loop(jnp.where(until == blocks, first, halo), halo, step, 0)
    for e in range(GROUP):
        grad = dquery_s[e].T * SCALE
        grad = (
            grad * cos_ref[...]
            + pltpu.roll(grad, RD // 2, 1) * low_ref[...]
            + pltpu.roll(grad, LANES - RD // 2, 1) * high_ref[...]
        )
        dq_ref[:, e * LANES : (e + 1) * LANES] = grad.astype(bf16)
    for group in range(LGROUPS):
        at = slice(group * LAT, (group + 1) * LAT)
        heads = [e for e in range(GROUP) if groups[e] == group]
        if not heads:
            dlatent_ref[:, at] = jnp.zeros((dlatent_ref.shape[0], LAT), bf16)
            continue
        lanes = slice(heads[0] * LANES, (heads[-1] + 1) * LANES)
        up = jnp.concatenate([up_ref[:, e].reshape(LAT, LANES) for e in heads], axis=1)
        dlatent_ref[:, at] = dot_nt(both_s[:, lanes], up).astype(bf16)
        dup_ref[:, lanes] = dot_nn(latent_ref[:, at].T, both_s[:, lanes]).astype(bf16)


def attend_backward(
    part, groups, places, queries, window, up_weight, mixed, logs, grad_mixed, tables, block, own, halo
):
    rows, wide = own * block, (halo + own) * block
    cuts, shards, once = up_weight.shape[0], up_weight.shape[1], pl.Buffered(1)
    table = pl.BlockSpec((rows, LANES), lambda g, p: (0, 0), pipeline_mode=once)
    return pl.pallas_call(
        functools.partial(attend_backward_kernel, groups, block, own, halo),
        grid_spec=pltpu.PrefetchScalarGridSpec(
            num_scalar_prefetch=1,
            grid=(1,),
            in_specs=[
                pl.BlockSpec(
                    (None, rows, GROUP * LANES),
                    lambda g, p: (part * GROUP // shards, 0, part * GROUP % shards // GROUP),
                    pipeline_mode=once,
                ),
                pl.BlockSpec((wide, LGROUPS * LAT), lambda g, p: (0, 0), pipeline_mode=once),
                pl.BlockSpec(
                    (wide, LANES), lambda g, p: (0, LGROUPS * LAT // LANES), pipeline_mode=once
                ),
                pl.BlockSpec(
                    (cuts, GROUP, LAT // cuts, LANES),
                    lambda g, p: (0, part * GROUP % shards // GROUP, D // LAT, part * GROUP // shards),
                    pipeline_mode=once,
                ),
                pl.BlockSpec((GROUP * HD, rows), lambda g, p: (0, 0), pipeline_mode=once),
                pl.BlockSpec((GROUP, 1, rows), lambda g, p: (0, 0, 0), pipeline_mode=once),
                pl.BlockSpec((GROUP * HD, rows), lambda g, p: (0, 0), pipeline_mode=once),
                table,
                table,
                table,
            ],
            out_specs=[
                pl.BlockSpec((rows, GROUP * LANES), lambda g, p: (0, 0), pipeline_mode=once),
                pl.BlockSpec((wide, LGROUPS * LAT), lambda g, p: (0, 0), pipeline_mode=once),
                pl.BlockSpec((wide, LANES), lambda g, p: (0, 0), pipeline_mode=once),
                pl.BlockSpec((LAT, GROUP * LANES), lambda g, p: (0, 0), pipeline_mode=once),
            ],
            scratch_shapes=[
                pltpu.VMEM((GROUP, LANES, rows), bf16),
                pltpu.VMEM((GROUP, rows, LANES), bf16),
                pltpu.VMEM((GROUP, 1, rows), f32),
                pltpu.VMEM((GROUP, LANES, rows), f32),
                pltpu.VMEM((wide, GROUP * LANES), bf16),
            ],
        ),
        out_shape=[
            jax.ShapeDtypeStruct((rows, GROUP * LANES), bf16),
            jax.ShapeDtypeStruct((wide, LGROUPS * LAT), bf16),
            jax.ShapeDtypeStruct((wide, LANES), f32),
            jax.ShapeDtypeStruct((LAT, GROUP * LANES), bf16),
        ],
        compiler_params=pltpu.CompilerParams(vmem_limit_bytes=56 << 20),
        cost_estimate=pl.CostEstimate(
            flops=40 * 10**9, bytes_accessed=30 * 10**6, transcendentals=0
        ),
        name="attend_backward",
    )(places, queries, window, window, up_weight, mixed, logs, grad_mixed, *tables)


def bits_of(size):
    return size.bit_length() - 1


def bit_pairs(size, bit):
    return [(i, i ^ (1 << bit)) for i in range(size)]


def upper_bit(axis, bit):
    return (lax.axis_index(axis) >> bit) & 1


def leading(shape):
    lead = [("rows", b) for b in reversed(range(bits_of(shape["rows"])))]
    return lead + [("heads", b) for b in reversed(range(bits_of(shape["heads"])))]


def gather_orders(shape):
    rows = [("rows", b) for b in reversed(range(1, bits_of(shape["rows"])))]
    heads = [("heads", b) for b in reversed(range(bits_of(shape["heads"])))]
    last = [("rows", 0)]
    return [
        heads + rows + last,
        heads[:1] + rows + heads[1:] + last,
        heads[-1:] + rows + heads[:-1] + last,
    ]


def flip(index, bit):
    size = 1 << bit
    return index + size * (1 - 2 * (index // size % 2))


def start_barrier(shape):
    barrier = pltpu.get_barrier_semaphore()
    for axis in ("rows", "heads"):
        for away in range(1, shape[axis]):
            pl.semaphore_signal(
                barrier,
                inc=1,
                device_id={axis: lax.rem(lax.axis_index(axis) + away, shape[axis])},
                device_id_type=pl.DeviceIdType.MESH,
            )
    pl.semaphore_wait(barrier, shape["rows"] + shape["heads"] - 2)


def exchange_index(lead, done, bits):
    return tuple(pl.ds(0, 2) if item in done else bits[item] for item in lead)


def gather_kernel(
    shape, orders, plan, block, own, halo, latent_ref, near_ref, large_ref, window_ref, near_all, large_all,
    zero_s, local_sem, halo_send, halo_recv, send_sem, recv_sem,
):
    row, head = lax.axis_index("rows"), lax.axis_index("heads")
    lead = leading(shape)
    index = {"rows": row, "heads": head}
    bits = {(axis, bit): lax.rem(index[axis] // (1 << bit), 2) for axis, bit in lead}
    zero_s[...] = jnp.zeros_like(zero_s)
    mine = exchange_index(lead, (), bits)
    local = [
        pltpu.make_async_copy(near_ref, near_all.at[mine], local_sem.at[0]),
        pltpu.make_async_copy(large_ref, large_all.at[mine], local_sem.at[1]),
        pltpu.make_async_copy(
            latent_ref, window_ref.at[pl.ds(halo * block, own * block), :], local_sem.at[2]
        ),
    ]
    for copy in local:
        copy.start()
    start_barrier(shape)

    ahead = lax.rem(head * own, halo + 1)
    passed = []
    for k in range(1, halo + 1):
        back = -(-k // own)
        at = own - 1 - (k - 1) % own
        there = lax.rem(head + back, shape["heads"])
        copy = pltpu.make_async_remote_copy(
            src_ref=latent_ref.at[pl.ds(at * block, block), :],
            dst_ref=window_ref.at[pl.ds((halo - k) * block, block), :],
            send_sem=halo_send.at[k - 1],
            recv_sem=halo_recv.at[k - 1],
            device_id={"heads": there},
            device_id_type=pl.DeviceIdType.MESH,
        )
        blank = pltpu.make_async_copy(
            zero_s, window_ref.at[pl.ds((halo - k) * block, block), :], local_sem.at[2 + k]
        )
        goes = (head + back < shape["heads"]) & (lax.rem((head + back) * own, halo + 1) >= k)
        passed.append((copy, blank, goes, ahead >= k))

    for copy, blank, goes, comes in passed:

        @pl.when(goes)
        def _():
            copy.start()

        @pl.when(jnp.logical_not(comes))
        def _():
            blank.start()

    for copy in local:
        copy.wait()
    stages = len(orders[0])
    flying = [None] * len(plan)
    for time in range(max(item[0] for item in plan) + stages):
        for i, (delay, which, order, begin, count) in enumerate(plan):
            stage = time - delay
            if not 0 <= stage < stages:
                continue
            if flying[i] is not None:
                flying[i].wait()
            axis, bit = orders[order][stage]
            target = (near_all, large_all)[which]
            held = exchange_index(lead, orders[order][:stage], bits)
            piece = target.at[held + (pl.ds(begin, count), slice(None))]
            flying[i] = pltpu.make_async_remote_copy(
                src_ref=piece,
                dst_ref=piece,
                send_sem=send_sem.at[i * stages + stage],
                recv_sem=recv_sem.at[i * stages + stage],
                device_id={axis: flip(index[axis], bit)},
                device_id_type=pl.DeviceIdType.MESH,
            )
            flying[i].start()
    for copy in flying:
        copy.wait()
    for copy, blank, goes, comes in passed:

        @pl.when(goes)
        def _():
            copy.wait_send()

        @pl.when(comes)
        def _():
            copy.wait_recv()

        @pl.when(jnp.logical_not(comes))
        def _():
            blank.wait()


def gather_weights(shape, latent, near, large, block, own, halo):
    orders = gather_orders(shape)
    stages = len(orders[0])
    plan = []
    for which, (piece, cuts) in enumerate(((near, 1), (large, CHUNKS))):
        units, total, passed = piece.shape[0] // 16, cuts * sum(SHARES), 0
        for i in range(cuts):
            for order, share in enumerate(SHARES):
                begin = 16 * (units * passed // total)
                passed += share
                count = 16 * (units * passed // total) - begin
                plan.append((i, which, order, begin, count))
    anywhere = pl.BlockSpec(memory_space=pl.ANY)
    twos = (2,) * stages
    window, near_all, large_all = pl.pallas_call(
        functools.partial(gather_kernel, shape, orders, plan, block, own, halo),
        in_specs=[anywhere] * 3,
        out_specs=[anywhere] * 3,
        out_shape=[
            jax.ShapeDtypeStruct(((halo + own) * block, latent.shape[1]), bf16),
            jax.ShapeDtypeStruct(twos + near.shape, bf16),
            jax.ShapeDtypeStruct(twos + large.shape, bf16),
        ],
        scratch_shapes=[
            pltpu.VMEM((block, latent.shape[1]), bf16),
            pltpu.SemaphoreType.DMA((3 + halo,)),
            pltpu.SemaphoreType.DMA((halo,)),
            pltpu.SemaphoreType.DMA((halo,)),
            pltpu.SemaphoreType.DMA((len(plan) * stages,)),
            pltpu.SemaphoreType.DMA((len(plan) * stages,)),
        ],
        compiler_params=pltpu.CompilerParams(
            collective_id=0, has_side_effects=True, vmem_limit_bytes=16 << 20
        ),
        name="gather_weights",
    )(latent, near, large)
    full = (shape["rows"], shape["heads"])
    return window, near_all.reshape(full + near.shape), large_all.reshape(full + large.shape)


def project_kernel(here, normed_ref, weight_ref, cos_ref, sin_ref, out_ref):
    raw = dot_nn(normed_ref[...], weight_ref[...].reshape(D, here * LANES))
    for e in range(here):
        part = raw[:, e * LANES : (e + 1) * LANES]
        part = part * cos_ref[...] + pltpu.roll(part, LANES - RD, 1) * sin_ref[...]
        out_ref[e] = part.astype(bf16)


def project_queries(normed, weights, cos_t, sin_t):
    rows = normed.shape[0]
    cuts, shards, here = weights.shape[0], weights.shape[1], weights.shape[3] // LANES
    table = pl.BlockSpec((rows, LANES), lambda h: (0, 0))
    return pl.pallas_call(
        functools.partial(project_kernel, here),
        grid=(shards,),
        in_specs=[
            pl.BlockSpec((rows, D), lambda h: (0, 0)),
            pl.BlockSpec((cuts, None, D // cuts, here * LANES), lambda h: (0, h, 0, 0)),
            table,
            table,
        ],
        out_specs=pl.BlockSpec((here, rows, LANES), lambda h: (0, 0, h)),
        out_shape=jax.ShapeDtypeStruct((here, rows, shards * LANES), bf16),
        compiler_params=pltpu.CompilerParams(vmem_limit_bytes=40 << 20),
        name="project_queries",
    )(normed, weights, cos_t, sin_t)


def feed_kernel(
    cuts, shards, units, side_ref, normed_ref, grad_ref, weight_ref, out_ref, dnormed_ref, kept_ref, sent_ref
):
    def whole(which):
        return jnp.concatenate(
            [
                jnp.concatenate(
                    [weight_ref[q, t, which * units : (which + 1) * units, :] for q in range(cuts)],
                    axis=1,
                )
                for t in range(shards)
            ],
            axis=0,
        )

    wide = D // cuts
    side = side_ref[0]

    def put(which, grad):
        at = slice(which * units, (which + 1) * units)
        for t in range(shards):
            rows = slice(t * units, (t + 1) * units)
            for q in range(cuts // 2):
                even = grad[rows, 2 * q * wide : (2 * q + 1) * wide].astype(bf16)
                odd = grad[rows, (2 * q + 1) * wide : (2 * q + 2) * wide].astype(bf16)
                kept_ref[q, t, at, :] = jnp.where(side == 0, even, odd)
                sent_ref[q, t, at, :] = jnp.where(side == 0, odd, even)

    @pl.when(pl.program_id(0) == 0)
    def _():
        out_ref[...] = jnp.zeros_like(out_ref)
        dnormed_ref[...] = jnp.zeros_like(dnormed_ref)

    normed = normed_ref[...]
    grad = grad_ref[...]
    w_gate, w_up, w_down = whole(0), whole(1), whole(2)
    gate = dot_nt(w_gate, normed)
    upper = dot_nt(w_up, normed)
    grad_inner = dot_nt(w_down, grad)
    sig = jax.nn.sigmoid(gate)
    silu = gate * sig
    inner = (silu * upper).astype(bf16)
    grad_gate = (grad_inner * upper * sig * (1.0 + gate * (1.0 - sig))).astype(bf16)
    grad_upper = (grad_inner * silu).astype(bf16)
    out_ref[...] += dot_tn(inner, w_down)
    dnormed_ref[...] += dot_tn(grad_gate, w_gate)
    dnormed_ref[...] += dot_tn(grad_upper, w_up)
    put(0, dot_nn(grad_gate, normed))
    put(1, dot_nn(grad_upper, normed))
    put(2, dot_nn(inner, grad))


def feed_forward_both(side, normed, grad, weights, units):
    rows = normed.shape[0]
    cuts, pieces, _, wide = weights.shape
    shards = max(1, min(pieces, 704 // units))
    once = pl.Buffered(1)
    half = (cuts // 2, shards, 3 * units, wide)
    whole = pl.BlockSpec((rows, D), lambda f, s: (0, 0), pipeline_mode=once)
    return pl.pallas_call(
        functools.partial(feed_kernel, cuts, shards, units),
        grid_spec=pltpu.PrefetchScalarGridSpec(
            num_scalar_prefetch=1,
            grid=(pieces // shards,),
            in_specs=[
                whole,
                whole,
                pl.BlockSpec((cuts, shards, 3 * units, wide), lambda f, s: (0, f, 0, 0)),
            ],
            out_specs=[
                whole,
                whole,
                pl.BlockSpec(half, lambda f, s: (0, f, 0, 0)),
                pl.BlockSpec(half, lambda f, s: (0, f, 0, 0)),
            ],
        ),
        out_shape=[
            jax.ShapeDtypeStruct((rows, D), f32),
            jax.ShapeDtypeStruct((rows, D), f32),
            jax.ShapeDtypeStruct((cuts // 2, pieces, 3 * units, wide), bf16),
            jax.ShapeDtypeStruct((cuts // 2, pieces, 3 * units, wide), bf16),
        ],
        compiler_params=pltpu.CompilerParams(vmem_limit_bytes=60 << 20),
        cost_estimate=pl.CostEstimate(
            flops=40 * 10**9, bytes_accessed=50 * 10**6, transcendentals=0
        ),
        name="feed_forward_both",
    )(side, normed, grad, weights)


def scatter_orders(shape):
    return [order[::-1] for order in gather_orders(shape)]


class Scatter:

    def __init__(self, shape, order, array, started=None):
        self.shape = shape
        self.order = list(scatter_orders(shape)[order])
        self.lead = leading(shape)
        self.terms = [array]
        if started is not None:
            self.order.pop(0)
            self.lead.remove(("rows", 0))
            self.terms = [array, started]
        self.terms = [t.reshape((2,) * len(self.lead) + t.shape[2:]) for t in self.terms]

    def total(self, terms):
        if len(terms) == 1:
            return terms[0]
        return sum(t.astype(f32) for t in terms).astype(bf16)

    def halves(self):
        axis, bit = self.order[0]
        at = self.lead.index((axis, bit))
        upper = upper_bit(axis, bit)

        def half(which):
            return self.total(
                [lax.dynamic_index_in_dim(t, which, at, keepdims=False) for t in self.terms]
            )

        return half(upper), half(1 - upper)

    def send(self, kept, sent):
        axis, bit = self.order.pop(0)
        self.lead.remove((axis, bit))
        self.terms = [kept, lax.ppermute(sent, axis, bit_pairs(self.shape[axis], bit))]

    def left(self):
        perm = [self.lead.index(item) for item in self.order]
        array = self.total(self.terms)
        array = array.transpose(perm + list(range(len(perm), array.ndim)))
        return array.reshape((2 ** len(perm),) + array.shape[len(perm) :])


def step_all(scatters, tied):
    halves = [scatter.halves() for scatter in scatters]
    sent, tied = lax.optimization_barrier(([half[1] for half in halves], tied))
    for scatter, half, out in zip(scatters, halves, sent):
        scatter.send(half[0], out)
    return tied


def scatter_kernel(shape, orders, *refs):
    count = len(orders)
    arrays, outs = refs[:count], refs[count : 2 * count]
    scratch, (send_sem, recv_sem) = list(refs[2 * count : -2]), refs[-2:]
    index = {"rows": lax.axis_index("rows"), "heads": lax.axis_index("heads")}
    start_barrier(shape)
    held, flying = list(arrays), [None] * count
    semaphore = 0
    for stage in range(max(len(order) for order in orders) + 1):
        for i, order in enumerate(orders):
            if flying[i] is not None:
                copy, kept, landed, begin, half = flying[i]
                copy.wait()
                flying[i] = None
                if stage < len(order):
                    summed = scratch.pop(0)

                    def add(at, _):
                        both = kept[begin + at].astype(f32) + landed[at].astype(f32)
                        summed[at] = both.astype(bf16)
                        return 0

                    lax.fori_loop(0, half, add, 0)
                    held[i] = summed
                else:
                    outs[i][...] = kept[begin].astype(f32) + landed[0].astype(f32)
            if stage < len(order):
                axis, bit = order[stage]
                upper = lax.rem(index[axis] // (1 << bit), 2)
                half = held[i].shape[0] // 2
                landed = scratch.pop(0)
                copy = pltpu.make_async_remote_copy(
                    src_ref=held[i].at[pl.ds((1 - upper) * half, half)],
                    dst_ref=landed,
                    send_sem=send_sem.at[semaphore],
                    recv_sem=recv_sem.at[semaphore],
                    device_id={axis: flip(index[axis], bit)},
                    device_id_type=pl.DeviceIdType.MESH,
                )
                copy.start()
                flying[i] = (copy, held[i], landed, upper * half, half)
                semaphore += 1


def scatter_rest(shape, scatters):
    orders = [tuple(scatter.order) for scatter in scatters]
    arrays = [scatter.left() for scatter in scatters]
    scratch = []
    for stage in range(max(len(order) for order in orders) + 1):
        for order, array in zip(orders, arrays):
            tail = array.shape[1:]
            if 0 < stage < len(order):
                scratch.append(pltpu.VMEM((array.shape[0] >> stage,) + tail, bf16))
            if stage < len(order):
                scratch.append(pltpu.VMEM((array.shape[0] >> (stage + 1),) + tail, bf16))
    total = sum(len(order) for order in orders)
    inside = pl.BlockSpec(memory_space=pltpu.VMEM)
    return pl.pallas_call(
        functools.partial(scatter_kernel, shape, orders),
        in_specs=[inside] * len(arrays),
        out_specs=[inside] * len(arrays),
        out_shape=[jax.ShapeDtypeStruct(array.shape[1:], f32) for array in arrays],
        scratch_shapes=scratch
        + [pltpu.SemaphoreType.DMA((total,)), pltpu.SemaphoreType.DMA((total,))],
        compiler_params=pltpu.CompilerParams(
            collective_id=1, has_side_effects=True, vmem_limit_bytes=48 << 20
        ),
        name="scatter_rest",
    )(*arrays)


def lane_table(rows, entries):
    columns = []
    for width, value in entries:
        columns.append(
            jnp.full((rows, width), value, f32) if isinstance(value, float) else value
        )
    return jnp.concatenate(columns, axis=1)


def on_device(
    shape,
    tokens,
    cotangent,
    domain,
    group_weight,
    gain_attn,
    w_query,
    w_query_rope,
    w_latent,
    w_key_rope,
    w_key_up,
    w_value_up,
    w_out,
    gain_mlp,
    w_gate,
    w_up,
    w_down,
):
    n_rows, n_heads = shape["rows"], shape["heads"]
    row_at, head_at = lax.axis_index("rows"), lax.axis_index("heads")
    local = tokens.shape[0]
    block = math.gcd(local, LEN)
    own, halo = local // block, LEN // block - 1
    here = w_query.shape[1] // HD
    units = w_gate.shape[1]
    cut = D // n_rows
    half = RD // 2

    head_of = [(i % n_heads) * here + i // n_heads for i in range(HEADS)]
    group_of = [head // GROUP for head in head_of]
    parts = [tuple(group_of[p * GROUP : (p + 1) * GROUP]) for p in range(HEADS // GROUP)]

    def part_of(weight):
        return lax.dynamic_slice_in_dim(weight, row_at * cut, cut, 1)

    start = head_at * local
    positions = ((start + jnp.arange(local)) % LEN).astype(f32)
    frequency = THETA ** (-jnp.arange(half).astype(f32) / half)
    angles = positions[:, None] * frequency[None, :]
    cos, sin = jnp.cos(angles), jnp.sin(angles)
    ahead = start // block % (LEN // block)
    places = jnp.stack([ahead, jnp.minimum(LEN // block - ahead, own)]).astype(jnp.int32)
    front = SCALE * LOG2E
    query_cos = lane_table(local, [(HD, front), (0, front * cos), (0, front * cos), (RD, 0.0)])
    query_sin = lane_table(local, [(HD, 0.0), (0, front * sin), (0, front * sin), (RD, 0.0)])
    key_cos = lane_table(local, [(HD, 0.0), (0, cos), (0, cos), (RD, 0.0)])
    key_sin = lane_table(local, [(HD, 0.0), (0, sin), (0, sin), (RD, 0.0)])
    back_cos = lane_table(local, [(HD, 1.0), (0, cos), (0, cos), (RD, 0.0)])
    back_low = lane_table(local, [(HD + half, 0.0), (0, -sin), (RD, 0.0)])
    back_high = lane_table(local, [(HD, 0.0), (0, sin), (half + RD, 0.0)])

    source = tokens.astype(f32)
    scale_attn = rms_scale(source)
    gain_one = gain_attn.astype(f32)
    normed = (source * scale_attn * gain_one).astype(bf16)
    blank = jnp.zeros((D, HD), bf16)
    latent_weight = jnp.concatenate(
        [w_latent, blank, w_key_rope, -w_key_rope[:, half:], w_key_rope[:, :half]], axis=1
    )
    raw = dot_nn(normed, latent_weight)
    raw_rope = raw[:, LGROUPS * LAT :]
    key_rope = raw_rope * key_cos + jnp.roll(raw_rope, -RD, axis=1) * key_sin
    latent = jnp.concatenate([raw[:, : LGROUPS * LAT], key_rope], axis=1).astype(bf16)

    def halo_pairs(k):
        back = -(-k // own)
        needs = [i for i in range(n_heads) if (i * local % LEN) // block >= k]
        return [(i - back, i) for i in needs]

    def halo_rows(k):
        at = own - 1 - (k - 1) % own
        return slice(at * block, (at + 1) * block)

    rope_here = w_query_rope.reshape(D, here, RD)
    query_here = jnp.concatenate(
        [
            w_query.reshape(D, here, HD),
            rope_here,
            -rope_here[:, :, half:],
            rope_here[:, :, :half],
        ],
        axis=2,
    ).reshape(D, here * LANES)
    up_here = jnp.concatenate(
        [w_key_up.reshape(LAT, here, HD), w_value_up.reshape(LAT, here, HD)], axis=2
    ).reshape(LAT, here * LANES)
    near = jnp.concatenate(
        [
            lax.dynamic_slice_in_dim(query_here, row_at * cut, cut, 0),
            lax.dynamic_slice_in_dim(up_here, row_at * (LAT // n_rows), LAT // n_rows, 0),
        ],
        axis=0,
    )
    large = jnp.concatenate(
        [part_of(w_gate.T), part_of(w_up.T), part_of(w_down), part_of(w_out)], axis=0
    )
    direct = cut % LANES == 0
    if direct:
        window, near_all, large_all = gather_weights(shape, latent, near, large, block, own, halo)
    else:
        pieces = [
            lax.ppermute(latent[halo_rows(k)], "heads", halo_pairs(k)) for k in range(halo, 0, -1)
        ]
        window = jnp.concatenate(pieces + [latent], axis=0)
        near_all = lax.all_gather(near, ("rows", "heads"), axis=0).reshape(
            (n_rows, n_heads) + near.shape
        )
        large_all = lax.all_gather(large, ("rows", "heads"), axis=0).reshape(
            (n_rows, n_heads) + large.shape
        )
    query_weights, out_weights = [], []
    for p in range(len(parts)):
        e, begin = p * GROUP // n_heads, p * GROUP % n_heads
        weight = near_all[:, begin : begin + GROUP, :cut, e * LANES : (e + 1) * LANES]
        query_weights.append(weight.transpose(0, 2, 1, 3).reshape(D, GROUP * LANES))
        weight = large_all[:, begin : begin + GROUP, 3 * units + e * HD : 3 * units + (e + 1) * HD]
        out_weights.append(weight.transpose(1, 2, 0, 3).reshape(GROUP * HD, D))
    out_weights, query_weights = lax.optimization_barrier((out_weights, query_weights))

    queries = project_queries(normed, near_all, query_cos, query_sin)
    forward = [
        attend_forward(p, groups, places, queries, window, near_all, block, own, halo)
        for p, groups in enumerate(parts)
    ]
    hidden = source
    for f, weight in zip(forward, out_weights):
        hidden = hidden + dot_tn(f[0], weight)

    scale_mlp = rms_scale(hidden)
    gain_two = gain_mlp.astype(f32)
    normed_mlp = (hidden * scale_mlp * gain_two).astype(bf16)
    seq_weights = jnp.sum(
        (domain[:, None] == jnp.arange(group_weight.shape[0])[None, :]).astype(f32)
        * group_weight[None, :],
        axis=1,
    )
    token_seq = (start + jnp.arange(local)) // LEN
    token_weight = jnp.sum(
        (token_seq[:, None] == jnp.arange(domain.shape[0])[None, :]).astype(f32)
        * seq_weights[None, :],
        axis=1,
    )
    grad_output = cotangent.astype(f32) * token_weight[:, None]
    core = upper_bit("rows", 0)
    if direct:
        feed_out, grad_normed_mlp, feed_kept, feed_sent = feed_forward_both(
            core.astype(jnp.int32).reshape(1),
            normed_mlp,
            grad_output.astype(bf16),
            large_all,
            units,
        )
    else:
        feed_weights = large_all[:, :, : 3 * units].transpose(1, 2, 0, 3)
        feed_weights = feed_weights.reshape(n_heads, 3 * units, 2, D // 2)
        feed_out, grad_normed_mlp, low_half, high_half = feed_forward_both(
            jnp.zeros((1,), jnp.int32),
            normed_mlp,
            grad_output.astype(bf16),
            feed_weights.transpose(2, 0, 1, 3),
            units,
        )
        grad_feed = jnp.concatenate([low_half[0], high_half[0]], axis=2)
        grad_feed = grad_feed.reshape(n_heads, 3 * units, n_rows // 2, 2, cut)
        grad_feed = grad_feed.transpose(3, 2, 0, 1, 4)
        feed_kept = lax.dynamic_index_in_dim(grad_feed, core, 0, keepdims=False)
        feed_sent = lax.dynamic_index_in_dim(grad_feed, 1 - core, 0, keepdims=False)
    feed_got = lax.ppermute(feed_sent, "rows", bit_pairs(n_rows, 0))
    middle = 3 * units // 2
    scatter_feed = [
        Scatter(shape, 0, feed_kept[:, :, :middle], feed_got[:, :, :middle]),
        Scatter(shape, 1, feed_kept[:, :, middle:], feed_got[:, :, middle:]),
    ]
    block_output = (hidden + feed_out).astype(bf16)
    grad_hidden_part, grad_gain_two = norm_backward(hidden, scale_mlp, gain_two, grad_normed_mlp)
    grad_hidden = grad_output + grad_hidden_part
    grad_hidden_low = grad_hidden.astype(bf16)

    grad_mixed = [dot_nt(weight, grad_hidden_low).astype(bf16) for weight in out_weights]
    grad_out_weight = []
    for f in forward:
        by_cut = [
            dot_nn(f[0], grad_hidden_low[:, r * cut : (r + 1) * cut]).astype(bf16)
            for r in range(n_rows)
        ]
        grad_out_weight.append(jnp.stack(by_cut).reshape(n_rows, GROUP, HD, cut))
    if GROUP % n_heads == 0:
        grad_out_weight = jnp.concatenate(grad_out_weight, axis=2)
    else:
        grad_out_weight = jnp.concatenate(grad_out_weight, axis=1)
    tables = (back_cos, back_low, back_high)

    def pieces_of(grad_query_part, grad_up_part):
        both = []
        for grad in (grad_query_part, grad_up_part):
            tall = grad.shape[0] // n_rows
            grad = grad.astype(bf16).reshape(n_rows, tall, -1, n_heads, LANES)
            both.append(grad.transpose(0, 3, 1, 2, 4).reshape(n_rows, n_heads, tall, -1))
        return jnp.concatenate(both, axis=2)

    by_part = GROUP % n_heads == 0
    scatter_near, backward = [], []
    scatter_out = Scatter(shape, 0, grad_out_weight)
    for p, groups in enumerate(parts):
        under_way = scatter_feed + ([scatter_out] + scatter_near if p else [])
        queries = step_all(under_way, queries)
        backward.append(
            attend_backward(
                p, groups, places, queries, window, near_all, forward[p][0], forward[p][1],
                grad_mixed[p], tables, block, own, halo,
            )
        )
        if by_part:
            last = backward[-1]
            scatter_near.append(Scatter(shape, 1, pieces_of(dot_tn(normed, last[0]), last[3])))
    if not by_part:
        grad_query_weight = dot_tn(normed, jnp.concatenate([b[0] for b in backward], axis=1))
        grad_up_weight = jnp.concatenate([b[3] for b in backward], axis=1)
        scatter_near.append(Scatter(shape, 1, pieces_of(grad_query_weight, grad_up_weight)))
    grad_window = jnp.concatenate(
        [sum(b[1].astype(f32) for b in backward), sum(b[2] for b in backward)], axis=1
    ).astype(bf16)
    own_blocks = [
        grad_window[(halo + j) * block : (halo + j + 1) * block].astype(f32) for j in range(own)
    ]
    for k in range(1, halo + 1):
        got = lax.ppermute(
            grad_window[(halo - k) * block : (halo - k + 1) * block],
            "heads",
            [(b, a) for a, b in halo_pairs(k)],
        )
        at = own - 1 - (k - 1) % own
        own_blocks[at] = own_blocks[at] + got.astype(f32)
    grad_own = jnp.concatenate(own_blocks, axis=0)
    at = LGROUPS * LAT
    grad_rope_own = grad_own[:, at:]
    grad_rope_own = (
        grad_rope_own * key_cos
        + jnp.roll(grad_rope_own, half, axis=1) * back_low
        + jnp.roll(grad_rope_own, -half, axis=1) * back_high
    )
    grad_own = jnp.concatenate([grad_own[:, :at], grad_rope_own], axis=1).astype(bf16)

    grad_normed = dot_nt(grad_own, latent_weight)
    for p, b in enumerate(backward):
        grad_normed = grad_normed + dot_nt(b[0], query_weights[p])
    grad_source_part, grad_gain_one = norm_backward(source, scale_attn, gain_one, grad_normed)
    grad_tokens = grad_hidden + grad_source_part
    grad_latent_weight = dot_tn(normed, grad_own)
    grad_latent_weight = jnp.concatenate(
        [
            grad_latent_weight[:, :at],
            grad_gain_one[:, None],
            grad_gain_two[:, None],
            jnp.zeros((D, HD - 2), f32),
            grad_latent_weight[:, at + HD :],
        ],
        axis=1,
    ).astype(bf16)
    grad_latent_weight = grad_latent_weight.reshape(
        n_rows, n_heads, D // (n_rows * n_heads), at + LANES
    )
    scatter_latent = Scatter(shape, 0, grad_latent_weight)
    own_first, own_second, own_out, own_latent, *own_small = scatter_rest(
        shape, scatter_feed + [scatter_out, scatter_latent] + scatter_near
    )
    own_feed = jnp.concatenate([own_first, own_second], axis=0)
    own_small = jnp.concatenate(own_small, axis=1)
    own_query = own_small[: D // n_rows].reshape(D // n_rows, here, LANES)
    own_up = own_small[D // n_rows :].reshape(LAT // n_rows, here, LANES)
    return (
        block_output,
        grad_tokens,
        own_latent[:, at],
        own_query[:, :, :HD].reshape(D // n_rows, here * HD),
        own_query[:, :, HD : HD + RD].reshape(D // n_rows, here * RD),
        own_latent[:, :at],
        own_latent[:, at + HD : at + HD + RD],
        own_up[:, :, :HD].reshape(LAT // n_rows, here * HD),
        own_up[:, :, HD:].reshape(LAT // n_rows, here * HD),
        own_out,
        own_latent[:, at + 1],
        own_feed[:units].T,
        own_feed[units : 2 * units].T,
        own_feed[2 * units :],
    )


def solution(mesh):
    in_specs = (
        P(("rows", "heads"), None),
        P(("rows", "heads"), None),
        P("rows"),
        P(),
        P(),
        P(None, "heads"),
        P(None, "heads"),
        P(),
        P(),
        P(None, "heads"),
        P(None, "heads"),
        P("heads", None),
        P(),
        P(None, "heads"),
        P(None, "heads"),
        P("heads", None),
    )
    out_specs = (
        P(("rows", "heads"), None),
        P(("rows", "heads"), None),
        P(("rows", "heads")),
        P("rows", "heads"),
        P("rows", "heads"),
        P(("rows", "heads"), None),
        P(("rows", "heads"), None),
        P("rows", "heads"),
        P("rows", "heads"),
        P("heads", "rows"),
        P(("rows", "heads")),
        P("rows", "heads"),
        P("rows", "heads"),
        P("heads", "rows"),
    )
    return jax.shard_map(
        functools.partial(on_device, dict(mesh.shape)),
        mesh=mesh,
        in_specs=in_specs,
        out_specs=out_specs,
        check_vma=False,
    )
```

time: 828 us -> 619 us (0.75)
  waiting for transfers between devices: 413 us -> 55.4 us
  Pallas kernels: 157 us -> 354 us
  starting transfers between devices: 76.1 us -> 29.6 us
  between operations: 15.5 us -> 2.08 us
  local copies, waits for them, and re-layouts: 74.6 us -> 83.4 us
    ppermute x22 -> x7, waiting for transfers between devices: 213 us -> 12.6 us  [the longest x6 12.6 us: send(): lax.ppermute(sent, axis, bit_pairs(self.shape[axis], bit))]
    pallas_call x4 -> x8, Pallas kernels: 157 us -> 354 us  [the longest x1 158 us: gather_weights(): pl.pallas_call(functools.partial(gather_kernel, shape, orders, plan, bloc...]
    ppermute x7, waiting for transfers between devices: 177 us -> 42.7 us  [on_device(): lax.ppermute(grad_window[(halo - k) * block:(halo - k + 1) * block], 'hea...]
    ppermute x22 -> x7, starting transfers between devices: 67.2 us -> 20.9 us  [the longest x6 20.5 us: send(): lax.ppermute(sent, axis, bit_pairs(self.shape[axis], bit))]
    reduce_scatter x2 -> x0, waiting for transfers between devices: 22.6 us -> none  [the longest x1 22.5 us: on_device(): lax.psum_scatter(grad_feed.reshape((n_rows * n_heads,) + grad_feed.shape[...]
    unnamed x152 -> x144, local copies, waits for them, and re-layouts: 23 us -> 36.8 us
    reshape x10 -> x8, local copies, waits for them, and re-layouts: 13.8 us -> 2.8 us  [the longest x4 1.19 us: pieces_of(): grad = grad.astype(bf16).reshape(n_rows, tall, -1, n_heads, LANES)]
    convert_element_type x14 -> x9, other arithmetic: 11 us -> 21 us  [the longest x8 14.3 us: total(): return sum((t.astype(f32) for t in terms)).astype(bf16)]
  transfers between devices with their start and end apart: 32 -> 14, of which waited for: 18 -> 6; matrix products, arithmetic and copies ran while one was open for 13% -> 10% of each run, Pallas kernels for 13% -> 4%
where the time goes in v2:
time: 619 us; the launch traced here: 613 us
  Pallas kernels  354 us (57%)
  local copies, waits for them, and re-layouts  83.4 us (13%)
  other arithmetic  61.6 us (10%)
  waiting for transfers between devices  55.4 us (9%)
  starting transfers between devices  29.6 us (5%)
  matrix products  27.3 us (4%)
    pallas_call x1, Pallas kernels, gather_weights(): pl.pallas_call(functools.partial(gather_kernel, shape, orders, plan, bloc...  158 us
    pallas_call x1, Pallas kernels, scatter_rest(): pl.pallas_call(functools.partial(scatter_kernel, shape, orders), in_specs...  67.9 us
    pallas_call x2, Pallas kernels, attend_backward(): pl.pallas_call(functools.partial(attend_backward_kernel, groups, block, o...  53.6 us
    pallas_call x1, Pallas kernels, feed_forward_both(): pl.pallas_call(functools.partial(feed_kernel, cuts, shards, units), grid_...  49.9 us
    ppermute x7, waiting for transfers between devices, on_device(): lax.ppermute(grad_window[(halo - k) * block:(halo - k + 1) * block], 'hea...  42.7 us
    unnamed x144, local copies, waits for them, and re-layouts  36.8 us
    ppermute x6, starting transfers between devices, send(): lax.ppermute(sent, axis, bit_pairs(self.shape[axis], bit))  20.5 us
    pallas_call x2, Pallas kernels, attend_forward(): pl.pallas_call(functools.partial(attend_forward_kernel, groups, block, ow...  17.9 us
  transfers between devices with their start and end apart: 14, of which 6 were waited for; matrix products, arithmetic and copies ran while one was open for 10% of the time, Pallas kernels for 4%

profile of v2, /device:TPU:0, one launch (start us, length us, event | category | flops | bytes accessed | tf_op | source)
XLA Modules:
  0.0 612.9 jit_solution(15511695076387605546)
XLA Ops:
  1.5 1.7 copy.89
  3.2 1.8 fusion.10
  7.5 1.8 fusion.4.normed_ref
  10.1 3.6 concatenate.103
  13.7 2.7 fusion.75
  27.7 3.1 fusion.57
  30.8 3.2 fusion.38
  35.2 157.9 %gather_weights.1 = (bf16[2560,640]{1,0:T(8,128)(2,1)S(1)}, bf16[2,2,2,2,2,320,256]{6,5,4,3,2,1,0:T(8,128)(2,1)S(1)}, bf16[2,2,2,2,2,1184,256]{6,5,4,3,2,1,0:T(8,128)(2,1)S(1)}) custom-call(bf16[768,640]{1,0:T(8,128)(2,1)S(1)} %pad_maximum_fusion.1.latent_ref, bf16[320,256]{1,0:T(8,128)(2,1)S(1)} %pad_maximum_fusion.10.near_ref, ...), custom_call_target="tpu_custom_call" | custom-call | tf_op jit(solution)/shard_map/gather_weights/pallas_call | solution.py:476
  193.2 6.5 %copy-done.5 = bf16[2,2,2,2,2,1184,256]{6,5,4,3,2,1,0:T(8,128)(2,1)} copy-done((bf16[2,2,2,2,2,1184,256]{6,5,4,3,2,1,0:T(8,128)(2,1)}, bf16[2,2,2,2,2,1184,256]{6,5,4,3,2,1,0:T(8,128)(2,1)S(1)}, u32[]{:S(2)}) %copy-start.5) | copy-done | bytes 19398680
  199.7 1.7 copy-done.6
  201.3 3.2 slice_bitcast_fusion
  204.6 2.3 copy-done.2
  207.7 2.5 copy-done.3
  210.2 6.3 %project_queries.1.q_ref = bf16[2,768,1024]{2,1,0:T(8,128)(2,1)S(1)} custom-call(bf16[768,1024]{1,0:T(8,128)(2,1)S(1)} %fusion.4.normed_ref, bf16[4,8,320,256]{3,2,1,0:T(8,128)(2,1)S(1)} %bitcast.184, f32[768,128]{1,0:T(8,128)S(1)} %maximum_maximum_fusion.2.cos_ref, f32[768,128]{1,0:T(8,128)S(1)} %get-tuple-element.172.sin_ref), custom_call_target="tpu_custom_call" | custom-call | tf_op jit(solution)/shard_map/project_queries/pallas_call | solution.py:514
  216.5 1.7 copy-done.4
  218.2 8.8 %attend_forward.2 = (bf16[512,768]{1,0:T(8,128)(2,1)}, f32[8,1,768]{2,1,0:T(1,128)}) custom-call(s32[2]{0:T(128)} %pad_add_fusion.place_ref, bf16[2,768,1024]{2,1,0:T(8,128)(2,1)} %copy-done.4, bf16[2560,640]{1,0:T(8,128)(2,1)} %copy-done.6, bf16[2560,640]{1,0:T(8,128)(2,1)} %copy-done.6, bf16[4,8,320,256]{3,2,1,0:T(8,128)(2,1)} %bitcast.180), custom_call_target="tpu_custom_call" | custom-call | flops 40000000000 | bytes 30000000 | tf_op jit(solution)/shard_map/attend_forward/pallas_call | solution.py:136
  227.0 9.0 %attend_forward.3 = (bf16[512,768]{1,0:T(8,128)(2,1)}, f32[8,1,768]{2,1,0:T(1,128)}) custom-call(s32[2]{0:T(128)} %pad_add_fusion.place_ref, bf16[2,768,1024]{2,1,0:T(8,128)(2,1)} %copy-done.4, bf16[2560,640]{1,0:T(8,128)(2,1)} %copy-done.6, bf16[2560,640]{1,0:T(8,128)(2,1)} %copy-done.6, bf16[4,8,320,256]{3,2,1,0:T(8,128)(2,1)} %bitcast.181), custom_call_target="tpu_custom_call" | custom-call | flops 40000000000 | bytes 30000000 | tf_op jit(solution)/shard_map/attend_forward/pallas_call | solution.py:136
  236.1 2.9 copy.104
  239.0 1.9 copy.159
  241.0 1.4 copy.103
  242.3 2.0 copy.160
  244.3 1.7 slice_bitcast_fusion.2
  250.2 2.9 multiply_reduce_fusion.2
  253.4 3.0 fusion.12.grad_ref
  256.4 1.5 multiply_convert_fusion.normed_ref
  257.9 49.9 %feed_forward_both.1 = (f32[768,1024]{1,0:T(8,128)}, f32[768,1024]{1,0:T(8,128)}, bf16[2,8,1056,256]{3,2,1,0:T(8,128)(2,1)}, bf16[2,8,1056,256]{3,2,1,0:T(8,128)(2,1)}) custom-call(s32[1]{0:T(128)} %bitcast.16.side_ref, bf16[768,1024]{1,0:T(8,128)(2,1)} %multiply_convert_fusion.normed_ref, bf16[768,1024]{1,0:T(8,128)(2,1)} %fusion.12.grad_ref, ...), custom_call_target="tpu_custom_call" | custom-call | flops 40000000000 | bytes 50000000 | tf_op jit(solution)/shard_map/feed_forward_both/pallas_call | solution.py:589
  308.2 3.7 multiply_reduce_fusion
  312.9 6.7 %fusion.67 = (bf16[768,1024]{1,0:T(8,128)(2,1)S(1)}, f32[768,1024]{1,0:T(8,128)}, bf16[768,1024]{1,0:T(8,128)(2,1)}) fusion(f32[768]{0:T(1024)S(1)} %broadcast_multiply_fusion.2, f32[768,1024]{1,0:T(8,128)} %get-tuple-element.175, f32[768,1024]{1,0:T(8,128)} %get-tuple-element.59, f32[1024]{0:T(1024)S(1)} %convert_element_type.289, ...), kind=kLoop, calls=%fused_computation.202 | loop fusion | flops 8650752 | bytes 17314816 | tf_op jit(solution)/shard_map/convert_element_type | solution.py:931
  326.8 2.0 convolution_convert_fusion.2.grad_ref
  328.8 1.9 convolution_convert_fusion.1.grad_ref
  330.7 3.8 fusion.69
  334.6 1.6 constant_dynamic-slice_fusion
  336.2 1.6 constant_dynamic-slice_fusion.2
  337.8 2.0 fusion.15
  339.8 2.0 fusion.14
  341.8 12.5 %collective-permute-start.2 = (bf16[2,2,2,528,256]{4,3,1,0,2:T(8,128)(2,1)}, bf16[2,2,2,528,256]{4,3,1,0,2:T(8,128)(2,1)}, u32[]{:S(2)}, u32[]{:S(2)}) collective-permute-start(bf16[2,2,2,528,256]{4,3,1,0,2:T(8,128)(2,1)} %fusion.15), channel_id=1, source_target_pairs={{0,1},{1,0},{2,3},{3,2},{4,5},{5,4},{6,7},{7,6},{8,9},{9,8},{10,11... | collective-permute-start | bytes 6488072 | tf_op jit(solution)/shard_map/ppermute | solution.py:657
  355.7 27.2 %attend_backward.2 = (bf16[768,1024]{1,0:T(8,128)(2,1)}, bf16[2560,512]{1,0:T(8,128)(2,1)}, f32[2560,128]{1,0:T(8,128)}, bf16[256,1024]{1,0:T(8,128)(2,1)}) custom-call(s32[2]{0:T(128)} %pad_add_fusion.place_ref, bf16[2,768,1024]{2,1,0:T(8,128)(2,1)} %copy-done.4, bf16[2560,640]{1,0:T(8,128)(2,1)} %copy-done.6, bf16[2560,640]{1,0:T(8,128)(2,1)} %copy-done.6, ...), custom_call_target="tpu_custom_call" | custom-call | flops 40000000000 | bytes 30000000 | tf_op jit(solution)/shard_map/attend_backward/pallas_call | solution.py:265
  382.9 3.2 convert_bitcast_fusion.1
  394.2 1.8 fusion.77
  396.0 7.4 %collective-permute-done.1 = bf16[2,2,2,528,256]{4,3,0,1,2:T(8,128)(2,1)} collective-permute-done((bf16[2,2,2,528,256]{4,3,0,1,2:T(8,128)(2,1)}, bf16[2,2,2,528,256]{4,3,0,1,2:T(8,128)(2,1)}, u32[]{:S(2)}, u32[]{:S(2)}) %collective-permute-start.1) | collective-permute-done | bytes 2162720 | tf_op jit(solution)/shard_map/ppermute | solution.py:657
  403.5 2.5 fusion.28
  406.0 2.6 fusion.29
  408.6 26.4 %attend_backward.3 = (bf16[768,1024]{1,0:T(8,128)(2,1)}, bf16[2560,512]{1,0:T(8,128)(2,1)}, f32[2560,128]{1,0:T(8,128)}, bf16[256,1024]{1,0:T(8,128)(2,1)}) custom-call(s32[2]{0:T(128)} %pad_add_fusion.place_ref, bf16[2,768,1024]{2,1,0:T(8,128)(2,1)} %copy-done.4, bf16[2560,640]{1,0:T(8,128)(2,1)} %copy-done.6, bf16[2560,640]{1,0:T(8,128)(2,1)} %copy-done.6, ...), custom_call_target="tpu_custom_call" | custom-call | flops 40000000000 | bytes 30000000 | tf_op jit(solution)/shard_map/attend_backward/pallas_call | solution.py:265
  435.0 1.6 add_convert_fusion.6
  437.1 2.5 add_convert_fusion
  439.9 1.4 collective-permute-start.3
  442.6 1.9 convert_bitcast_fusion
  446.6 1.7 copy.123
  452.2 3.8 collective-permute-done.3
  457.3 20.2 %collective-permute-done.4 = bf16[256,640]{1,0:T(8,128)(2,1)S(1)} collective-permute-done((bf16[256,640]{1,0:T(8,128)(2,1)S(1)}, bf16[256,640]{1,0:T(8,128)(2,1)S(1)}, u32[]{:S(2)}, u32[]{:S(2)}) %collective-permute-start.4) | collective-permute-done | bytes 327712 | tf_op jit(solution)/shard_map/ppermute | solution.py:981
  478.4 1.8 fusion.78
  480.4 11.2 %collective-permute-done.6 = bf16[256,640]{1,0:T(8,128)(2,1)S(1)} collective-permute-done((bf16[256,640]{1,0:T(8,128)(2,1)S(1)}, bf16[256,640]{1,0:T(8,128)(2,1)S(1)}, u32[]{:S(2)}, u32[]{:S(2)}) %collective-permute-start.6) | collective-permute-done | bytes 327712 | tf_op jit(solution)/shard_map/ppermute | solution.py:981
  491.6 6.6 %collective-permute-start.11 = (bf16[2,2,528,256]{3,2,1,0:T(8,128)(2,1)}, bf16[2,2,528,256]{3,2,1,0:T(8,128)(2,1)}, u32[]{:S(2)}, u32[]{:S(2)}) collective-permute-start(bf16[2,2,528,256]{3,2,1,0:T(8,128)(2,1)} %fusion.29), channel_id=1, source_target_pairs={{0,2},{1,3},{2,0},{3,1},{4,6},{5,7},{6,4},{7,5},{8,10},{9,11},{10,... | collective-permute-start | bytes 3244040 | tf_op jit(solution)/shard_map/ppermute | solution.py:657
  498.1 7.5 %collective-permute-done.8 = bf16[256,640]{1,0:T(8,128)(2,1)S(1)} collective-permute-done((bf16[256,640]{1,0:T(8,128)(2,1)S(1)}, bf16[256,640]{1,0:T(8,128)(2,1)S(1)}, u32[]{:S(2)}, u32[]{:S(2)}) %collective-permute-start.8) | collective-permute-done | bytes 327712 | tf_op jit(solution)/shard_map/ppermute | solution.py:981
  508.5 3.5 fusion.9
  512.0 1.4 convolution_convert_fusion
  515.0 2.3 concatenate.130
  517.3 5.9 fusion.8
  523.2 1.7 fusion.32
  525.0 5.2 collective-permute-done.10
  530.2 2.0 fusion.18
  532.2 2.1 fusion.16
  534.5 1.7 fusion.27
  537.3 67.9 %scatter_rest.1 = (f32[528,256]{1,0:T(8,128)S(1)}, f32[528,256]{1,0:T(8,128)S(1)}, f32[128,256]{1,0:T(8,128)S(1)}, f32[32,640]{1,0:T(8,128)S(1)}, f32[320,128]{1,0:T(8,128)S(1)}, /*index=5*/f32[320,128]{1,0:T(8,128)S(1)}) custom-call(bf16[4,528,256]{2,1,0:T(8,128)(2,1)S(1)} %bitcast.186, bf16[4,528,256]{2,1,0:T(8,128)(2,1)S(1)} %bitcast.187, ...), custom_call_target="tpu_custom_call" | custom-call | tf_op jit(solution)/shard_map/scatter_rest/pallas_call | solution.py:731
  (254 shorter events, 62.9 us)
Async XLA Ops:
  0.6 19.2 %copy-start = (bf16[352,1024]{1,0:T(8,128)(2,1)S(1)}, bf16[352,1024]{1,0:T(8,128)(2,1)}, u32[]{:S(2)}) copy-start(bf16[352,1024]{1,0:T(8,128)(2,1)} %param.31) | copy-start | bytes 2162692
  5.0 5.1 copy-start.38
  5.0 8.7 %copy-start.46 = (f32[768]{0:T(1024)}, f32[768]{0:T(1024)S(1)}, u32[]{:S(2)}) copy-start(f32[768]{0:T(1024)S(1)} %add_rsqrt_fusion.1) | copy-start | bytes 9220
  5.8 7.9 %copy-start.48 = (f32[1024]{0:T(1024)}, f32[1024]{0:T(1024)S(1)}, u32[]{:S(2)}) copy-start(f32[1024]{0:T(1024)S(1)} %convert_element_type.285) | copy-start | bytes 12292
  16.4 1.6 copy-start.31
  18.2 189.2 %copy-start.50 = (f32[128]{0:T(128)}, f32[128]{0:T(128)S(1)}, u32[]{:S(2)}) copy-start(f32[128]{0:T(128)S(1)} %pad.66.clone) | copy-start | bytes 1540
  18.2 12.6 %copy-start.52 = (f32[128]{0:T(128)}, f32[128]{0:T(128)S(1)}, u32[]{:S(2)}) copy-start(f32[128]{0:T(128)S(1)} %pad.63.clone) | copy-start | bytes 1540
  30.8 3.2 copy-start.26
  193.2 6.5 %copy-start.5 = (bf16[2,2,2,2,2,1184,256]{6,5,4,3,2,1,0:T(8,128)(2,1)}, bf16[2,2,2,2,2,1184,256]{6,5,4,3,2,1,0:T(8,128)(2,1)S(1)}, u32[]{:S(2)}) copy-start(bf16[2,2,2,2,2,1184,256]{6,5,4,3,2,1,0:T(8,128)(2,1)S(1)} %get-tuple-element.54) | copy-start | bytes 58195972
  199.7 1.7 copy-start.6
  201.3 6.1 copy-start.34
  201.3 6.1 copy-start.55
  204.6 2.3 copy-start.2
  207.7 2.5 copy-start.3
  216.5 1.7 copy-start.4
  239.0 2.0 copy-start.20
  247.0 2.5 copy-start.24
  247.0 1.5 copy-start.35
  248.5 1.6 copy-start.40
  250.2 2.9 copy-start.54
  250.2 2.9 copy-start.56
  250.2 2.9 copy-start.57
  253.1 3.3 copy-start.7
  307.8 22.9 %collective-permute-start = (bf16[2,8,1056,256]{3,2,1,0:T(8,128)(2,1)}, bf16[2,8,1056,256]{3,2,1,0:T(8,128)(2,1)}, u32[]{:S(2)}, u32[]{:S(2)}) collective-permute-start(bf16[2,8,1056,256]{3,2,1,0:T(8,128)(2,1)} %get-tuple-element.61), channel_id=1, source_target_pairs={{0,8},{8,0},{16,24},{24,16},{1,9},{9,1},{17,25},{25,17},{2,10},{10... | collective-permute-start | bytes 25952264 | tf_op jit(solution)/shard_map/ppermute | solution.py:922
  312.9 6.7 %copy-start.36 = (bf16[512,768]{1,0:T(8,128)(2,1)S(1)}, bf16[512,768]{1,0:T(8,128)(2,1)}, u32[]{:S(2)}) copy-start(bf16[512,768]{1,0:T(8,128)(2,1)} %get-tuple-element.53.mixed_ref) | copy-start | bytes 2359300
  312.9 11.7 %slice-start = ((s8[8650752]{0:T(1024)(128)(4,1)}), s8[4194304]{0:T(1024)(128)(4,1)S(1)}, s32[]{:S(2)}) async-start(s8[8650752]{0:T(1024)(128)(4,1)} %bitcast.198), calls=%async_computation | async-start | bytes 8388608
  312.9 11.7 %slice-start.1 = ((s8[8650752]{0:T(1024)(128)(4,1)}), s8[4194304]{0:T(1024)(128)(4,1)S(1)}, s32[]{:S(2)}) async-start(s8[8650752]{0:T(1024)(128)(4,1)} %bitcast.198), calls=%async_computation.1 | async-start | bytes 8388608
  320.0 1.7 copy-start.41
  321.7 3.0 slice-start.2
  323.4 1.8 copy-start.18
  341.8 64.2 %collective-permute-start.2 = (bf16[2,2,2,528,256]{4,3,1,0,2:T(8,128)(2,1)}, bf16[2,2,2,528,256]{4,3,1,0,2:T(8,128)(2,1)}, u32[]{:S(2)}, u32[]{:S(2)}) collective-permute-start(bf16[2,2,2,528,256]{4,3,1,0,2:T(8,128)(2,1)} %fusion.15), channel_id=1, source_target_pairs={{0,1},{1,0},{2,3},{3,2},{4,5},{5,4},{6,7},{7,6},{8,9},{9,8},{10,11... | collective-permute-start | bytes 6488072 | tf_op jit(solution)/shard_map/ppermute | solution.py:657
  354.4 49.1 %collective-permute-start.1 = (bf16[2,2,2,528,256]{4,3,0,1,2:T(8,128)(2,1)}, bf16[2,2,2,528,256]{4,3,0,1,2:T(8,128)(2,1)}, u32[]{:S(2)}, u32[]{:S(2)}) collective-permute-start(bf16[2,2,2,528,256]{4,3,0,1,2:T(8,128)(2,1)} %fusion.14), channel_id=1, source_target_pairs={{0,16},{8,24},{16,0},{24,8},{1,17},{9,25},{17,1},{25,9},{2,18},{10... | collective-permute-start | bytes 6488072 | tf_op jit(solution)/shard_map/ppermute | solution.py:657
  387.3 2.0 copy-start.10
  388.1 2.8 copy-start.22
  388.1 2.3 copy-start.16
  390.4 1.8 copy-start.17
  390.9 15.1 %copy-start.12 = (bf16[2,2,2,1,528,256]{5,4,1,0,3,2:T(8,128)(2,1)}, bf16[2,2,2,1,528,256]{5,4,1,0,3,2:T(8,128)(2,1)S(1)}, u32[]{:S(2)}) copy-start(bf16[2,2,2,1,528,256]{5,4,1,0,3,2:T(8,128)(2,1)S(1)} %add_convert_fusion.1) | copy-start | bytes 6488068
  392.2 1.6 copy-start.30
  392.2 2.0 copy-start.59
  394.2 9.3 %copy-start.14 = (bf16[1,2,2,2,528,256]{5,4,1,2,3,0:T(8,128)(2,1)}, bf16[1,2,2,2,528,256]{5,4,1,2,3,0:T(8,128)(2,1)S(1)}, u32[]{:S(2)}) copy-start(bf16[1,2,2,2,528,256]{5,4,1,2,3,0:T(8,128)(2,1)S(1)} %add_convert_fusion.2) | copy-start | bytes 6488068
  408.6 26.4 %copy-start.37 = (f32[2560,128]{1,0:T(8,128)S(1)}, f32[2560,128]{1,0:T(8,128)}, u32[]{:S(2)}) copy-start(f32[2560,128]{1,0:T(8,128)} %get-tuple-element.72) | copy-start | bytes 3932164
  434.9 2.1 copy-start.28
  439.6 3.0 copy-start.58
  439.9 16.2 %collective-permute-start.3 = (bf16[256,640]{1,0:T(8,128)(2,1)S(1)}, bf16[256,640]{1,0:T(8,128)(2,1)S(1)}, u32[]{:S(2)}, u32[]{:S(2)}) collective-permute-start(bf16[256,640]{1,0:T(8,128)(2,1)S(1)} %get-tuple-element.143), channel_id=1, source_target_pairs={{1,0},{2,1},{4,3},{5,4},{7,6},{9,8},{10,9},{12,11},{13,12},{15,14}... | collective-permute-start | bytes 983048 | tf_op jit(solution)/shard_map/ppermute | solution.py:981
  441.3 36.2 %collective-permute-start.4 = (bf16[256,640]{1,0:T(8,128)(2,1)S(1)}, bf16[256,640]{1,0:T(8,128)(2,1)S(1)}, u32[]{:S(2)}, u32[]{:S(2)}) collective-permute-start(bf16[256,640]{1,0:T(8,128)(2,1)S(1)} %get-tuple-element.144), channel_id=1, source_target_pairs={{2,0},{5,3},{10,8},{13,11},{18,16},{21,19},{26,24},{29,27}} | collective-permute-start | bytes 983048 | tf_op jit(solution)/shard_map/ppermute | solution.py:981
  446.6 31.8 %copy-start.29 = (bf16[128,8,8,128]{3,1,2,0:T(8,128)(2,1)S(1)}, bf16[128,8,8,128]{3,1,2,0:T(8,128)(2,1)}, u32[]{:S(2)}) copy-start(bf16[128,8,8,128]{3,1,2,0:T(8,128)(2,1)} %copy.159) | copy-start | bytes 6291460
  448.3 31.9 %collective-permute-start.5 = (bf16[256,640]{1,0:T(8,128)(2,1)S(1)}, bf16[256,640]{1,0:T(8,128)(2,1)S(1)}, u32[]{:S(2)}, u32[]{:S(2)}) collective-permute-start(bf16[256,640]{1,0:T(8,128)(2,1)S(1)} %get-tuple-element.145), channel_id=1, source_target_pairs={{1,0},{2,1},{4,3},{5,4},{6,5},{7,6},{9,8},{10,9},{12,11},{13,12},{... | collective-permute-start | bytes 983048 | tf_op jit(solution)/shard_map/ppermute | solution.py:981
  449.6 42.0 %collective-permute-start.6 = (bf16[256,640]{1,0:T(8,128)(2,1)S(1)}, bf16[256,640]{1,0:T(8,128)(2,1)S(1)}, u32[]{:S(2)}, u32[]{:S(2)}) collective-permute-start(bf16[256,640]{1,0:T(8,128)(2,1)S(1)} %get-tuple-element.146), channel_id=1, source_target_pairs={{2,0},{5,3},{7,5},{10,8},{13,11},{15,13},{18,16},{21,19},{23,21},{... | collective-permute-start | bytes 983048 | tf_op jit(solution)/shard_map/ppermute | solution.py:981
  450.9 40.7 %collective-permute-start.7 = (bf16[256,640]{1,0:T(8,128)(2,1)S(1)}, bf16[256,640]{1,0:T(8,128)(2,1)S(1)}, u32[]{:S(2)}, u32[]{:S(2)}) collective-permute-start(bf16[256,640]{1,0:T(8,128)(2,1)S(1)} %get-tuple-element.147), channel_id=1, source_target_pairs={{1,0},{2,1},{3,2},{4,3},{5,4},{6,5},{7,6},{9,8},{10,9},{11,10},{12... | collective-permute-start | bytes 983048 | tf_op jit(solution)/shard_map/ppermute | solution.py:981
  456.1 49.6 %collective-permute-start.8 = (bf16[256,640]{1,0:T(8,128)(2,1)S(1)}, bf16[256,640]{1,0:T(8,128)(2,1)S(1)}, u32[]{:S(2)}, u32[]{:S(2)}) collective-permute-start(bf16[256,640]{1,0:T(8,128)(2,1)S(1)} %get-tuple-element.149), channel_id=1, source_target_pairs={{2,0},{4,2},{5,3},{7,5},{10,8},{12,10},{13,11},{15,13},{18,16},{20... | collective-permute-start | bytes 983048 | tf_op jit(solution)/shard_map/ppermute | solution.py:981
  477.5 28.1 %collective-permute-start.9 = (bf16[256,640]{1,0:T(8,128)(2,1)S(1)}, bf16[256,640]{1,0:T(8,128)(2,1)S(1)}, u32[]{:S(2)}, u32[]{:S(2)}) collective-permute-start(bf16[256,640]{1,0:T(8,128)(2,1)S(1)} %get-tuple-element.148), channel_id=1, source_target_pairs={{5,2},{13,10},{21,18},{29,26}} | collective-permute-start | bytes 983048 | tf_op jit(solution)/shard_map/ppermute | solution.py:981
  480.3 54.1 %collective-permute-start.13 = (bf16[2,2,2,2,320,128]{5,4,3,2,1,0:T(8,128)(2,1)}, bf16[2,2,2,2,320,128]{5,4,3,2,1,0:T(8,128)(2,1)}, u32[]{:S(2)}, u32[]{:S(2)}) collective-permute-start(bf16[2,2,2,2,320,128]{5,4,3,2,1,0:T(8,128)(2,1)} %fusion.26), channel_id=1, source_target_pairs={{0,8},{8,0},{16,24},{24,16},{1,9},{9,1},{17,25},{25,17},{2,10},{10... | collective-permute-start | bytes 3932168 | tf_op jit(solution)/shard_map/ppermute | solution.py:657
  491.6 31.6 %collective-permute-start.12 = (bf16[2,2,2,2,128,256]{5,4,3,2,1,0:T(8,128)(2,1)}, bf16[2,2,2,2,128,256]{5,4,3,2,1,0:T(8,128)(2,1)}, u32[]{:S(2)}, u32[]{:S(2)}) collective-permute-start(bf16[2,2,2,2,128,256]{5,4,3,2,1,0:T(8,128)(2,1)} %dynamic-slice_bitcast_fusion), channel_id=1, source_target_pairs={{0,8},{8,0},{16,24},{24,16},{1,9},{9,1},{17,25},{25,17},{2,10},{10... | collective-permute-start | bytes 3145736 | tf_op jit(solution)/shard_map/ppermute | solution.py:657
  491.6 40.6 %collective-permute-start.11 = (bf16[2,2,528,256]{3,2,1,0:T(8,128)(2,1)}, bf16[2,2,528,256]{3,2,1,0:T(8,128)(2,1)}, u32[]{:S(2)}, u32[]{:S(2)}) collective-permute-start(bf16[2,2,528,256]{3,2,1,0:T(8,128)(2,1)} %fusion.29), channel_id=1, source_target_pairs={{0,2},{1,3},{2,0},{3,1},{4,6},{5,7},{6,4},{7,5},{8,10},{9,11},{10,... | collective-permute-start | bytes 3244040 | tf_op jit(solution)/shard_map/ppermute | solution.py:657
  505.6 24.6 %collective-permute-start.10 = (bf16[2,2,528,256]{3,2,0,1:T(8,128)(2,1)}, bf16[2,2,528,256]{3,2,0,1:T(8,128)(2,1)}, u32[]{:S(2)}, u32[]{:S(2)}) collective-permute-start(bf16[2,2,528,256]{3,2,0,1:T(8,128)(2,1)} %fusion.28), channel_id=1, source_target_pairs={{0,1},{1,0},{2,3},{3,2},{4,5},{5,4},{6,7},{7,6},{8,9},{9,8},{10,11... | collective-permute-start | bytes 3244040 | tf_op jit(solution)/shard_map/ppermute | solution.py:657
  506.6 1.9 copy-start.21
  506.6 1.9 copy-start.47
  506.6 1.9 copy-start.49
  517.3 5.9 copy-start.19
  523.2 7.0 %copy-start.15 = (bf16[1,2,2,2,528,256]{5,4,1,2,3,0:T(8,128)(2,1)S(1)}, bf16[1,2,2,2,528,256]{5,4,1,2,3,0:T(8,128)(2,1)}, u32[]{:S(2)}) copy-start(bf16[1,2,2,2,528,256]{5,4,1,2,3,0:T(8,128)(2,1)} %copy-done.14) | copy-start | bytes 6488068
  525.0 7.2 %copy-start.13 = (bf16[2,2,2,1,528,256]{5,4,1,0,3,2:T(8,128)(2,1)S(1)}, bf16[2,2,2,1,528,256]{5,4,1,0,3,2:T(8,128)(2,1)}, u32[]{:S(2)}) copy-start(bf16[2,2,2,1,528,256]{5,4,1,0,3,2:T(8,128)(2,1)} %copy-done.12) | copy-start | bytes 6488068
  532.2 2.2 copy-start.11
  532.2 2.3 copy-start.23
  608.5 4.2 copy-start.1
  (13 other events, 15.7 us)

commit v3 on v2

v3 whole, which is shorter than its diff:
```python
import functools
import math

import jax
import jax.numpy as jnp
from jax import lax
from jax.experimental import pallas as pl
from jax.experimental.pallas import tpu as pltpu
from jax.sharding import PartitionSpec as P

D = 1024
HEADS = 16
HD = 64
LGROUPS = 2
LAT = 256
RD = 32
LEN = 2048
EPS = 1e-05
THETA = 10000.0
NEG_LARGE = -1e30
LANES = 128
PAIR = 2
GROUP = HEADS // LGROUPS
TALL = 80
CHUNKS = 4
SHARES = (2, 2, 1)
LOG2E = math.log2(math.e)
LN2 = math.log(2.0)
SCALE = (HD + RD) ** (-0.5)

bf16 = jnp.bfloat16
f32 = jnp.float32


def dot_nn(a, b):
    return jnp.dot(a, b, preferred_element_type=f32)


def dot_nt(a, b):
    return lax.dot_general(a, b, (((1,), (1,)), ((), ())), preferred_element_type=f32)


def dot_tn(a, b):
    return lax.dot_general(a, b, (((0,), (0,)), ((), ())), preferred_element_type=f32)


def rms_scale(values):
    return lax.rsqrt(jnp.mean(values * values, axis=-1, keepdims=True) + EPS)


def rotate_lanes(values, cos, sin):
    lane = lax.broadcasted_iota(jnp.int32, values.shape, 1)
    turned = (lane >= HD) & (lane < HD + RD)
    cos = jnp.where(lane < HD, 1.0, jnp.where(turned, cos, 0.0))
    sin = jnp.where(turned, sin, 0.0)
    half = RD // 2
    swapped = jnp.where(
        lane < HD + half, -pltpu.roll(values, LANES - half, 1), pltpu.roll(values, half, 1)
    )
    return values * cos + swapped * sin


def rope_weight(w_key_rope):
    rows = w_key_rope.shape[0]
    blank = jnp.zeros((rows, HD), bf16)
    return jnp.concatenate([blank, w_key_rope, blank[:, : LANES - HD - RD]], axis=1)


def prepare_kernel(tokens_ref, gain_ref, latent_ref, rope_ref, cos_ref, sin_ref, normed_ref, out_ref):
    source = tokens_ref[...].astype(f32)
    normed = (source * rms_scale(source) * gain_ref[...].astype(f32)).astype(bf16)
    normed_ref[...] = normed
    out_ref[:, : LGROUPS * LAT] = dot_nn(normed, latent_ref[...]).astype(bf16)
    turned = rotate_lanes(dot_nn(normed, rope_weight(rope_ref[...])), cos_ref[...], sin_ref[...])
    out_ref[:, LGROUPS * LAT :] = turned.astype(bf16)


def prepare(tokens, gain, w_latent, w_key_rope, cos, sin):
    rows = tokens.shape[0]
    return pl.pallas_call(
        prepare_kernel,
        out_shape=[
            jax.ShapeDtypeStruct((rows, D), bf16),
            jax.ShapeDtypeStruct((rows, LGROUPS * LAT + LANES), bf16),
        ],
        compiler_params=pltpu.CompilerParams(vmem_limit_bytes=40 << 20),
        name="prepare",
    )(tokens, gain, w_latent, w_key_rope, cos, sin)


def pack_kernel(
    here, side_ref, query_ref, rope_ref, key_ref, value_ref, out_ref, gate_ref, up_ref, down_ref,
    near_ref, large_ref,
):
    cut, units = gate_ref.shape
    blank = jnp.zeros((cut, LANES - HD - RD), bf16)
    small = key_ref.shape[0]
    for e in range(here):
        lanes = slice(e * LANES, (e + 1) * LANES)
        heads, turns = slice(e * HD, (e + 1) * HD), slice(e * RD, (e + 1) * RD)
        near_ref[:cut, lanes] = jnp.concatenate(
            [query_ref[:, heads], rope_ref[:, turns], blank], axis=1
        )
        near_ref[cut : cut + small, lanes] = jnp.concatenate(
            [key_ref[:, heads], value_ref[:, heads]], axis=1
        )
    near_ref[cut + small :, :] = out_ref[...]
    large_ref[:units, :] = gate_ref[...].T
    large_ref[units : 2 * units, :] = up_ref[...].T
    large_ref[2 * units :, :] = down_ref[...]


def pack(side, n_rows, w_query, w_query_rope, w_key_up, w_value_up, w_out, w_gate, w_up, w_down):
    here, units = w_query.shape[1] // HD, w_gate.shape[1]
    cut, small = D // n_rows, LAT // n_rows

    def by_rows(weight):
        tall = weight.shape[0] // n_rows
        return pl.BlockSpec((tall, weight.shape[1]), lambda g, s: (s[0], 0))

    def by_columns(weight):
        return pl.BlockSpec((weight.shape[0], cut), lambda g, s: (0, s[0]))

    near = (cut + small + here * HD, here * LANES)
    large = (3 * units, cut)
    return pl.pallas_call(
        functools.partial(pack_kernel, here),
        grid_spec=pltpu.PrefetchScalarGridSpec(
            num_scalar_prefetch=1,
            grid=(1,),
            in_specs=[
                by_rows(w_query),
                by_rows(w_query_rope),
                by_rows(w_key_up),
                by_rows(w_value_up),
                by_columns(w_out),
                by_rows(w_gate),
                by_rows(w_up),
                by_columns(w_down),
            ],
            out_specs=[
                pl.BlockSpec(near, lambda g, s: (0, 0)),
                pl.BlockSpec(large, lambda g, s: (0, 0)),
            ],
        ),
        out_shape=[jax.ShapeDtypeStruct(near, bf16), jax.ShapeDtypeStruct(large, bf16)],
        name="pack",
    )(side, w_query, w_query_rope, w_key_up, w_value_up, w_out, w_gate, w_up, w_down)


def keys_values(groups, latent_ref, rope_ref, up_ref, rows, count):
    rope = rope_ref[rows, :]
    lane = lax.broadcasted_iota(jnp.int32, (count, LANES), 1)
    keys, values = [], []
    for e in range(0, GROUP, PAIR):
        latent = latent_ref[rows, groups[e] * LAT : (groups[e] + 1) * LAT]
        up = [up_ref[:, e + i].reshape(LAT, LANES) for i in range(PAIR)]
        up = jnp.concatenate(up, axis=1)
        wide = dot_nn(latent, up).astype(bf16)
        for i in range(PAIR):
            both = wide[:, i * LANES : (i + 1) * LANES]
            keys.append(jnp.where(lane < HD, both, rope))
            values.append(both)
    return keys, values


def values_ones(value):
    count = value.shape[0]
    return jnp.concatenate([value.T[HD:], jnp.ones((TALL - HD, count), bf16)], axis=0)


def shard_block(part, shards, rows_at):
    return lambda g, p: (0, part * GROUP % shards // GROUP, rows_at, part * GROUP // shards)


def forward_body(
    groups, block, own, halo, ahead, meanwhile, normed_ref, weight_ref, cos_ref, sin_ref, latent_ref, rope_ref,
    up_ref, mixed_ref, log_ref, q_ref, query_s, top_s, sum_s,
):
    rows = own * block
    until = halo + 1 - ahead
    weight = jnp.concatenate(
        [weight_ref[:, e].reshape(D, LANES) for e in range(GROUP)], axis=1
    )
    raw = dot_nn(normed_ref[...], weight)
    for e in range(GROUP):
        lanes = slice(e * LANES, (e + 1) * LANES)
        query = rotate_lanes(raw[:, lanes], cos_ref[...], sin_ref[...])
        query = (query * (SCALE * LOG2E)).astype(bf16)
        q_ref[:, lanes] = query
        query_s[e] = query.T
    keys, values = keys_values(
        groups, latent_ref, rope_ref, up_ref, slice(halo * block, (halo + own) * block), rows
    )
    values = [values_ones(value) for value in values]
    for j in range(own):
        count = (j + 1) * block
        key_at = lax.broadcasted_iota(jnp.int32, (count, block), 0)
        query_at = lax.broadcasted_iota(jnp.int32, (count, block), 1) + j * block
        keep = (key_at <= query_at) & (key_at >= jnp.where(j >= until, until * block, 0))
        cols = slice(j * block, count)
        scores = [
            jnp.where(keep, dot_nn(keys[e][:count], query_s[e, :, cols]), NEG_LARGE)
            for e in range(GROUP)
        ]
        for e in range(GROUP):
            top = jnp.max(scores[e], axis=0, keepdims=True)
            terms = jnp.exp2(scores[e] - top).astype(bf16)
            top_s[e, :, cols] = top
            sum_s[e, :, cols] = dot_nn(values[e][:, :count], terms)
    meanwhile(0)
    for blocks in range(1, own + 1):
        wide = blocks * block

        def step(index, _):
            at = pl.ds(pl.multiple_of(index * block, block), block)
            keys, values = keys_values(groups, latent_ref, rope_ref, up_ref, at, block)
            values = [values_ones(value) for value in values]
            scores = [dot_nn(keys[e], query_s[e, :, :wide]) for e in range(GROUP)]
            for e in range(GROUP):
                top = top_s[e, :, :wide]
                higher = jnp.maximum(top, jnp.max(scores[e], axis=0, keepdims=True))
                shrink = jnp.exp2(top - higher)
                terms = jnp.exp2(scores[e] - higher).astype(bf16)
                top_s[e, :, :wide] = higher
                sum_s[e, :, :wide] = sum_s[e, :, :wide] * shrink + dot_nn(values[e], terms)
            return 0

        @pl.when(until == blocks if blocks < own else until >= own)
        def _():
            lax.fori_loop(halo - ahead, halo, step, 0)

    meanwhile(1)
    for e in range(GROUP):
        total = sum_s[e]
        sums = total[HD : HD + 1]
        mixed_ref[e * HD : (e + 1) * HD, :] = (total[:HD] * (1.0 / sums)).astype(bf16)
        log_ref[e] = top_s[e] + jnp.log2(sums)


def attend_forward_kernel(groups, block, own, halo, place_ref, *refs):
    forward_body(groups, block, own, halo, place_ref[0], lambda at: None, *refs)


def attend_forward(part, groups, places, normed, near, cos, sin, window, block, own, halo):
    rows, wide = own * block, (halo + own) * block
    cuts, shards, once = near.shape[0], near.shape[1], pl.Buffered(1)

    def whole(shape):
        return pl.BlockSpec(shape, lambda g, p: (0,) * len(shape), pipeline_mode=once)

    return pl.pallas_call(
        functools.partial(attend_forward_kernel, groups, block, own, halo),
        grid_spec=pltpu.PrefetchScalarGridSpec(
            num_scalar_prefetch=1,
            grid=(1,),
            in_specs=[
                whole((rows, D)),
                pl.BlockSpec(
                    (cuts, GROUP, D // cuts, LANES),
                    shard_block(part, shards, 0),
                    pipeline_mode=once,
                ),
                whole((rows, LANES)),
                whole((rows, LANES)),
                whole((wide, LGROUPS * LAT)),
                pl.BlockSpec(
                    (wide, LANES), lambda g, p: (0, LGROUPS * LAT // LANES), pipeline_mode=once
                ),
                pl.BlockSpec(
                    (cuts, GROUP, LAT // cuts, LANES),
                    shard_block(part, shards, D // LAT),
                    pipeline_mode=once,
                ),
            ],
            out_specs=[
                whole((GROUP * HD, rows)),
                whole((GROUP, 1, rows)),
                whole((rows, GROUP * LANES)),
            ],
            scratch_shapes=[
                pltpu.VMEM((GROUP, LANES, rows), bf16),
                pltpu.VMEM((GROUP, 1, rows), f32),
                pltpu.VMEM((GROUP, TALL, rows), f32),
            ],
        ),
        out_shape=[
            jax.ShapeDtypeStruct((GROUP * HD, rows), bf16),
            jax.ShapeDtypeStruct((GROUP, 1, rows), f32),
            jax.ShapeDtypeStruct((rows, GROUP * LANES), bf16),
        ],
        compiler_params=pltpu.CompilerParams(vmem_limit_bytes=56 << 20),
        name="attend_forward",
    )(places, normed, near, cos, sin, window, window, near)


def attend_backward_kernel(
    groups, block, own, halo, carried, place_ref, q_ref, latent_ref, rope_ref, up_ref, mixed_ref, log_ref,
    grad_ref, cos_ref, sin_ref, normed_ref, weight_ref, *refs
):
    before = refs[:2] if carried else None
    dwindow_ref, dnormed_ref, dnear_ref, query_s, grad_s, inner_s, dquery_s, both_s, rope_s = refs[-9:]
    rows = own * block
    ahead, until = place_ref[0], place_ref[1]
    first = halo - ahead
    rope_s[...] = jnp.zeros_like(rope_s)

    def clear(index, _):
        at = pl.ds(pl.multiple_of(index * block, block), block)
        both_s[at, :] = jnp.zeros((block, GROUP * LANES), bf16)
        return 0

    lax.fori_loop(0, first, clear, 0)
    for e in range(GROUP):
        query_s[e] = q_ref[:, e * LANES : (e + 1) * LANES].T
        grad = grad_ref[e * HD : (e + 1) * HD, :]
        grad_s[e] = jnp.concatenate([jnp.zeros((rows, HD), bf16), grad.T], axis=1)
        inner_s[e] = jnp.sum(
            grad.astype(f32) * mixed_ref[e * HD : (e + 1) * HD, :].astype(f32),
            axis=0,
            keepdims=True,
        )
        dquery_s[e] = jnp.zeros((LANES, rows), f32)
    lane = lax.broadcasted_iota(jnp.int32, (block, LANES), 1)

    def strip(at, low, high, keep):
        cols = slice(low, high)
        keys, values = keys_values(groups, latent_ref, rope_ref, up_ref, at, block)
        scores = [dot_nn(keys[e], query_s[e, :, cols]) for e in range(GROUP)]
        grads = [
            dot_nn(values[e][:, HD:], grad_ref[e * HD : (e + 1) * HD, cols]) for e in range(GROUP)
        ]
        grad_rope = None
        for e in range(GROUP):
            score = scores[e] if keep is None else jnp.where(keep, scores[e], NEG_LARGE)
            probs = jnp.exp2(score - log_ref[e, :, cols])
            grad_scores = (probs * (grads[e] - inner_s[e, :, cols])).astype(bf16)
            grad_value = dot_nn(probs.astype(bf16), grad_s[e, cols, :])
            grad_key = dot_nn(grad_scores, q_ref[cols, e * LANES : (e + 1) * LANES]) * LN2
            dquery_s[e, :, cols] += dot_nn(keys[e].T, grad_scores)
            both_s[at, e * LANES : (e + 1) * LANES] = jnp.where(
                lane < HD, grad_key, grad_value
            ).astype(bf16)
            grad_rope = grad_key if grad_rope is None else grad_rope + grad_key
        rope_s[at, :] = grad_rope

    for i in range(own):
        count = rows - i * block
        key_at = lax.broadcasted_iota(jnp.int32, (block, count), 0)
        query_at = lax.broadcasted_iota(jnp.int32, (block, count), 1)
        keep = (key_at <= query_at) & (query_at < jnp.where(i < until, (until - i) * block, rows))
        strip(slice((halo + i) * block, (halo + i + 1) * block), i * block, rows, keep)
    for blocks in range(1, own + 1):

        def step(index, _):
            strip(pl.ds(pl.multiple_of(index * block, block), block), 0, blocks * block, None)
            return 0

        lax.fori_loop(jnp.where(until == blocks, first, halo), halo, step, 0)
    grads = []
    for e in range(GROUP):
        grad = rotate_lanes(dquery_s[e].T * SCALE, cos_ref[...], -sin_ref[...])
        grads.append(grad.astype(bf16))
    dquery = jnp.concatenate(grads, axis=1)
    cuts = weight_ref.shape[0]
    cut, small = D // cuts, LAT // cuts
    for q in range(cuts):
        weight = jnp.concatenate([weight_ref[q, e] for e in range(GROUP)], axis=1)
        part = dot_nt(dquery, weight)
        if carried:
            part = part + before[1][:, q * cut : (q + 1) * cut]
        dnormed_ref[:, q * cut : (q + 1) * cut] = part
    grad = dot_tn(normed_ref[...], dquery).astype(bf16)
    for q in range(cuts):
        for e in range(GROUP):
            dnear_ref[q, e, :cut, :] = grad[q * cut : (q + 1) * cut, e * LANES : (e + 1) * LANES]
    for group in range(LGROUPS):
        at = slice(group * LAT, (group + 1) * LAT)
        heads = [e for e in range(GROUP) if groups[e] == group]
        if heads:
            lanes = slice(heads[0] * LANES, (heads[-1] + 1) * LANES)
            up = jnp.concatenate([up_ref[:, e].reshape(LAT, LANES) for e in heads], axis=1)
            grad = dot_nt(both_s[:, lanes], up)
            dup = dot_nn(latent_ref[:, at].T, both_s[:, lanes]).astype(bf16)
            for q in range(cuts):
                for i, e in enumerate(heads):
                    dnear_ref[q, e, cut:, :] = dup[
                        q * small : (q + 1) * small, i * LANES : (i + 1) * LANES
                    ]
        else:
            grad = jnp.zeros((dwindow_ref.shape[0], LAT), f32)
        if carried:
            grad = grad + before[0][:, at].astype(f32)
        dwindow_ref[:, at] = grad.astype(bf16)
    grad = rope_s[...]
    if carried:
        grad = grad + before[0][:, LGROUPS * LAT :].astype(f32)
    dwindow_ref[:, LGROUPS * LAT :] = grad.astype(bf16)


def attend_backward(
    part, groups, places, forward, normed, near, cos, sin, window, grad_mixed, before, block, own, halo
):
    rows, wide = own * block, (halo + own) * block
    cuts, shards, once = near.shape[0], near.shape[1], pl.Buffered(1)
    near_rows = (D + LAT) // cuts
    lanes = LGROUPS * LAT + LANES
    mixed, logs, queries = forward

    def whole(shape):
        return pl.BlockSpec(shape, lambda g, p: (0,) * len(shape), pipeline_mode=once)

    return pl.pallas_call(
        functools.partial(attend_backward_kernel, groups, block, own, halo, before is not None),
        grid_spec=pltpu.PrefetchScalarGridSpec(
            num_scalar_prefetch=1,
            grid=(1,),
            in_specs=[
                whole((rows, GROUP * LANES)),
                whole((wide, LGROUPS * LAT)),
                pl.BlockSpec(
                    (wide, LANES), lambda g, p: (0, LGROUPS * LAT // LANES), pipeline_mode=once
                ),
                pl.BlockSpec(
                    (cuts, GROUP, LAT // cuts, LANES),
                    shard_block(part, shards, D // LAT),
                    pipeline_mode=once,
                ),
                whole((GROUP * HD, rows)),
                whole((GROUP, 1, rows)),
                whole((GROUP * HD, rows)),
                whole((rows, LANES)),
                whole((rows, LANES)),
                whole((rows, D)),
                pl.BlockSpec(
                    (cuts, GROUP, D // cuts, LANES),
                    shard_block(part, shards, 0),
                    pipeline_mode=once,
                ),
            ]
            + ([] if before is None else [whole((wide, lanes)), whole((rows, D))]),
            out_specs=[
                whole((wide, lanes)),
                whole((rows, D)),
                whole((cuts, GROUP, near_rows, LANES)),
            ],
            scratch_shapes=[
                pltpu.VMEM((GROUP, LANES, rows), bf16),
                pltpu.VMEM((GROUP, rows, LANES), bf16),
                pltpu.VMEM((GROUP, 1, rows), f32),
                pltpu.VMEM((GROUP, LANES, rows), f32),
                pltpu.VMEM((wide, GROUP * LANES), bf16),
                pltpu.VMEM((wide, LANES), f32),
            ],
        ),
        out_shape=[
            jax.ShapeDtypeStruct((wide, lanes), bf16),
            jax.ShapeDtypeStruct((rows, D), f32),
            jax.ShapeDtypeStruct((cuts, GROUP, near_rows, LANES), bf16),
        ],
        compiler_params=pltpu.CompilerParams(vmem_limit_bytes=60 << 20),
        cost_estimate=pl.CostEstimate(
            flops=40 * 10**9, bytes_accessed=30 * 10**6, transcendentals=0
        ),
        name="attend_backward",
    )(
        places, queries, window, window, near, mixed, logs, grad_mixed, cos, sin, normed, near,
        *(before or ()),
    )


def join_kernel(parts, tokens_ref, gain_ref, *refs):
    mixed, weights, (hidden_ref, normed_ref) = refs[:parts], refs[parts : 2 * parts], refs[2 * parts :]
    cuts, _, _, cut = weights[0].shape
    squares = 0.0
    for q in range(cuts):
        cols = slice(q * cut, (q + 1) * cut)
        total = tokens_ref[:, cols].astype(f32)
        for m, w in zip(mixed, weights):
            total = total + dot_tn(m[...], w[q].reshape(GROUP * HD, cut))
        hidden_ref[:, cols] = total
        squares = squares + jnp.sum(total * total, axis=1, keepdims=True)
    scale = lax.rsqrt(squares * (1.0 / D) + EPS)
    normed_ref[...] = (hidden_ref[...] * scale * gain_ref[...].astype(f32)).astype(bf16)


def out_specs_of(out, base, parts):
    cuts, shards, _, cut = out.shape
    return [
        pl.BlockSpec(
            (cuts, GROUP, HD, cut),
            lambda g, part=part: (
                0, part * GROUP % shards // GROUP, base // HD + part * GROUP // shards, 0
            ),
            pipeline_mode=pl.Buffered(1),
        )
        for part in range(parts)
    ]


def join(tokens, gain, mixed, out, base):
    rows, parts = tokens.shape[0], len(mixed)

    def whole(shape):
        return pl.BlockSpec(shape, lambda g: (0,) * len(shape), pipeline_mode=pl.Buffered(1))

    return pl.pallas_call(
        functools.partial(join_kernel, parts),
        grid=(1,),
        in_specs=[whole((rows, D)), whole((1, D))]
        + [whole((GROUP * HD, rows))] * parts
        + out_specs_of(out, base, parts),
        out_specs=[whole((rows, D)), whole((rows, D))],
        out_shape=[
            jax.ShapeDtypeStruct((rows, D), f32),
            jax.ShapeDtypeStruct((rows, D), bf16),
        ],
        compiler_params=pltpu.CompilerParams(vmem_limit_bytes=32 << 20),
        name="join",
    )(tokens, gain, *mixed, *([out] * parts))


def norm_backward(source, gain, grad_normed):
    scale = rms_scale(source)
    scaled = source * scale
    weighted = grad_normed * gain
    mean = jnp.mean(weighted * scaled, axis=-1, keepdims=True)
    return (
        scale * (weighted - scaled * mean),
        jnp.sum(grad_normed * scaled, axis=0, keepdims=True),
    )


def middle_kernel(parts, here, hidden_ref, feed_ref, dnormed_ref, cotangent_ref, weight_ref, gain_ref, *refs):
    mixed, weights = refs[:parts], refs[parts : 2 * parts]
    block_ref, grad_ref, dout_ref, dgain_ref = refs[2 * parts : 2 * parts + 4]
    dmixed = refs[2 * parts + 4 :]
    hidden = hidden_ref[...]
    block_ref[...] = (hidden + feed_ref[...]).astype(bf16)
    grad, dgain_ref[...] = norm_backward(hidden, gain_ref[...].astype(f32), dnormed_ref[...])
    grad = grad + cotangent_ref[...].astype(f32) * weight_ref[...]
    grad_ref[...] = grad
    low = grad.astype(bf16)
    cuts, _, _, cut = weights[0].shape
    shards = dout_ref.shape[1]
    for p in range(parts):
        e, begin = p * GROUP // shards, p * GROUP % shards
        total = None
        for q in range(cuts):
            cols = slice(q * cut, (q + 1) * cut)
            part = dot_nt(weights[p][q].reshape(GROUP * HD, cut), low[:, cols])
            total = part if total is None else total + part
            grad_out = dot_nn(mixed[p][...], low[:, cols]).astype(bf16)
            dout_ref[q, begin : begin + GROUP, e * HD : (e + 1) * HD, :] = grad_out.reshape(
                GROUP, HD, cut
            )
        dmixed[p][...] = total.astype(bf16)


def middle(hidden, feed, dnormed, cotangent, token_weight, gain, mixed, out, base):
    rows, parts = hidden.shape[0], len(mixed)
    cuts, shards, _, cut = out.shape
    here = HEADS // shards

    def whole(shape):
        return pl.BlockSpec(shape, lambda g: (0,) * len(shape), pipeline_mode=pl.Buffered(1))

    dout = (cuts, shards, here * HD, cut)
    return pl.pallas_call(
        functools.partial(middle_kernel, parts, here),
        grid=(1,),
        in_specs=[whole((rows, D))] * 4
        + [whole((rows, 1)), whole((1, D))]
        + [whole((GROUP * HD, rows))] * parts
        + out_specs_of(out, base, parts),
        out_specs=[whole((rows, D)), whole((rows, D)), whole(dout), whole((1, D))]
        + [whole((GROUP * HD, rows))] * parts,
        out_shape=[
            jax.ShapeDtypeStruct((rows, D), bf16),
            jax.ShapeDtypeStruct((rows, D), f32),
            jax.ShapeDtypeStruct(dout, bf16),
            jax.ShapeDtypeStruct((1, D), f32),
        ]
        + [jax.ShapeDtypeStruct((GROUP * HD, rows), bf16)] * parts,
        compiler_params=pltpu.CompilerParams(vmem_limit_bytes=50 << 20),
        name="middle",
    )(hidden, feed, dnormed, cotangent, token_weight, gain, *mixed, *([out] * parts))


def finish_kernel(
    block, own, halo, dwindow_ref, tokens_ref, normed_ref, dnormed_ref, grad_ref, gain_ref, latent_ref,
    rope_ref, cos_ref, sin_ref, *refs
):
    got, (dtokens_ref, dlatent_ref, dgain_ref) = refs[:halo], refs[halo:]
    at = LGROUPS * LAT
    grads = []
    for j in range(own):
        total = dwindow_ref[(halo + j) * block : (halo + j + 1) * block, :].astype(f32)
        for k in range(1, halo + 1):
            if own - 1 - (k - 1) % own == j:
                total = total + got[k - 1][...].astype(f32)
        grads.append(total)
    grad = jnp.concatenate(grads, axis=0)
    turned = rotate_lanes(grad[:, at:], cos_ref[...], -sin_ref[...])
    lane = lax.broadcasted_iota(jnp.int32, turned.shape, 1)
    turned = jnp.where(lane < HD, 0.0, turned).astype(bf16)
    grad = grad[:, :at].astype(bf16)
    dnormed = dnormed_ref[...] + dot_nt(grad, latent_ref[...])
    dnormed = dnormed + dot_nt(turned, rope_weight(rope_ref[...]))
    source = tokens_ref[...].astype(f32)
    dsource, dgain_ref[...] = norm_backward(source, gain_ref[...].astype(f32), dnormed)
    dtokens_ref[...] = grad_ref[...] + dsource
    dlatent_ref[:, :at] = dot_tn(normed_ref[...], grad).astype(bf16)
    dlatent_ref[:, at:] = dot_tn(normed_ref[...], turned).astype(bf16)


def finish(
    dwindow, got, tokens, normed, dnormed, grad_hidden, gain, w_latent, w_key_rope, cos, sin, block, own, halo
):
    rows = tokens.shape[0]
    return pl.pallas_call(
        functools.partial(finish_kernel, block, own, halo),
        out_shape=[
            jax.ShapeDtypeStruct((rows, D), f32),
            jax.ShapeDtypeStruct((D, LGROUPS * LAT + LANES), bf16),
            jax.ShapeDtypeStruct((1, D), f32),
        ],
        compiler_params=pltpu.CompilerParams(vmem_limit_bytes=60 << 20),
        name="finish",
    )(dwindow, tokens, normed, dnormed, grad_hidden, gain, w_latent, w_key_rope, cos, sin, *got)


def bits_of(size):
    return size.bit_length() - 1


def bit_pairs(size, bit):
    return [(i, i ^ (1 << bit)) for i in range(size)]


def upper_bit(axis, bit):
    return (lax.axis_index(axis) >> bit) & 1


def leading(shape):
    lead = [("rows", b) for b in reversed(range(bits_of(shape["rows"])))]
    return lead + [("heads", b) for b in reversed(range(bits_of(shape["heads"])))]


def gather_orders(shape):
    rows = [("rows", b) for b in reversed(range(1, bits_of(shape["rows"])))]
    heads = [("heads", b) for b in reversed(range(bits_of(shape["heads"])))]
    last = [("rows", 0)]
    return [
        heads + rows + last,
        heads[:1] + rows + heads[1:] + last,
        heads[-1:] + rows + heads[:-1] + last,
    ]


def flip(index, bit):
    size = 1 << bit
    return index + size * (1 - 2 * (index // size % 2))


def start_barrier(shape):
    barrier = pltpu.get_barrier_semaphore()
    for axis in ("rows", "heads"):
        for away in range(1, shape[axis]):
            pl.semaphore_signal(
                barrier,
                inc=1,
                device_id={axis: lax.rem(lax.axis_index(axis) + away, shape[axis])},
                device_id_type=pl.DeviceIdType.MESH,
            )
    pl.semaphore_wait(barrier, shape["rows"] + shape["heads"] - 2)


def exchange_index(lead, done, bits):
    return tuple(pl.ds(0, 2) if item in done else bits[item] for item in lead)


class Exchanges:

    def __init__(self, shape, plan, target, send_sem, recv_sem):
        self.orders, self.plan, self.target = gather_orders(shape), plan, target
        self.lead, self.stages = leading(shape), len(leading(shape))
        self.index = {axis: lax.axis_index(axis) for axis in ("rows", "heads")}
        self.bits = {
            (axis, bit): lax.rem(self.index[axis] // (1 << bit), 2) for axis, bit in self.lead
        }
        self.send_sem, self.recv_sem = send_sem, recv_sem
        self.times = max(item[0] for item in plan) + self.stages

    def mine(self):
        return self.target.at[exchange_index(self.lead, (), self.bits)]

    def copy(self, chunk, stage):
        _, order, begin, count = self.plan[chunk]
        axis, bit = self.orders[order][stage]
        held = exchange_index(self.lead, self.orders[order][:stage], self.bits)
        piece = self.target.at[held + (pl.ds(begin, count), slice(None))]
        return pltpu.make_async_remote_copy(
            src_ref=piece,
            dst_ref=piece,
            send_sem=self.send_sem.at[chunk * self.stages + stage],
            recv_sem=self.recv_sem.at[chunk * self.stages + stage],
            device_id={axis: flip(self.index[axis], bit)},
            device_id_type=pl.DeviceIdType.MESH,
        )

    def run(self, time):
        for chunk, item in enumerate(self.plan):
            stage = time - item[0]
            if 0 < stage <= self.stages:
                self.copy(chunk, stage - 1).wait()
            if 0 <= stage < self.stages:
                self.copy(chunk, stage).start()


def exchange_plan(rows, cuts):
    units, total, passed, plan = rows // 16, cuts * sum(SHARES), 0, []
    for i in range(cuts):
        for order, share in enumerate(SHARES):
            begin = 16 * (units * passed // total)
            passed += share
            plan.append((i, order, begin, 16 * (units * passed // total) - begin))
    return plan


def gather_kernel(
    shape, plan, block, own, halo, latent_ref, near_ref, window_ref, near_all,
    zero_s, local_sem, halo_send, halo_recv, send_sem, recv_sem,
):
    head = lax.axis_index("heads")
    exchanges = Exchanges(shape, plan, near_all, send_sem, recv_sem)
    zero_s[...] = jnp.zeros_like(zero_s)
    local = [
        pltpu.make_async_copy(near_ref, exchanges.mine(), local_sem.at[0]),
        pltpu.make_async_copy(
            latent_ref, window_ref.at[pl.ds(halo * block, own * block), :], local_sem.at[1]
        ),
    ]
    for copy in local:
        copy.start()
    start_barrier(shape)

    ahead = lax.rem(head * own, halo + 1)
    passed = []
    for k in range(1, halo + 1):
        back = -(-k // own)
        at = own - 1 - (k - 1) % own
        there = lax.rem(head + back, shape["heads"])
        copy = pltpu.make_async_remote_copy(
            src_ref=latent_ref.at[pl.ds(at * block, block), :],
            dst_ref=window_ref.at[pl.ds((halo - k) * block, block), :],
            send_sem=halo_send.at[k - 1],
            recv_sem=halo_recv.at[k - 1],
            device_id={"heads": there},
            device_id_type=pl.DeviceIdType.MESH,
        )
        blank = pltpu.make_async_copy(
            zero_s, window_ref.at[pl.ds((halo - k) * block, block), :], local_sem.at[2 + k]
        )
        goes = (head + back < shape["heads"]) & (lax.rem((head + back) * own, halo + 1) >= k)
        passed.append((copy, blank, goes, ahead >= k))

    for copy, blank, goes, comes in passed:

        @pl.when(goes)
        def _():
            copy.start()

        @pl.when(jnp.logical_not(comes))
        def _():
            blank.start()

    for copy in local:
        copy.wait()
    for time in range(exchanges.times + 1):
        exchanges.run(time)
    for copy, blank, goes, comes in passed:

        @pl.when(goes)
        def _():
            copy.wait_send()

        @pl.when(comes)
        def _():
            copy.wait_recv()

        @pl.when(jnp.logical_not(comes))
        def _():
            blank.wait()


def gather_near(shape, latent, near, block, own, halo):
    plan = exchange_plan(near.shape[0], 1)
    count = len(plan) * len(leading(shape))
    anywhere = pl.BlockSpec(memory_space=pl.ANY)
    outside = pl.BlockSpec(memory_space=pltpu.HBM)
    window, near_all = pl.pallas_call(
        functools.partial(gather_kernel, shape, plan, block, own, halo),
        in_specs=[anywhere] * 2,
        out_specs=[outside] * 2,
        out_shape=[
            jax.ShapeDtypeStruct(((halo + own) * block, latent.shape[1]), bf16),
            jax.ShapeDtypeStruct((2,) * len(leading(shape)) + near.shape, bf16),
        ],
        scratch_shapes=[
            pltpu.VMEM((block, latent.shape[1]), bf16),
            pltpu.SemaphoreType.DMA((3 + halo,)),
            pltpu.SemaphoreType.DMA((halo,)),
            pltpu.SemaphoreType.DMA((halo,)),
            pltpu.SemaphoreType.DMA((count,)),
            pltpu.SemaphoreType.DMA((count,)),
        ],
        compiler_params=pltpu.CompilerParams(
            collective_id=0, has_side_effects=True, vmem_limit_bytes=16 << 20
        ),
        name="gather_near",
    )(latent, near)
    return window, near_all.reshape((shape["rows"], shape["heads"]) + near.shape)


def attend_gather_kernel(
    shape, plan, groups, block, own, halo, normed_ref, weight_ref, cos_ref, sin_ref, latent_ref, rope_ref,
    up_ref, large_ref, mixed_ref, log_ref, q_ref, large_all, query_s, top_s, sum_s, local_sem, send_sem, recv_sem,
):
    part, parts = pl.program_id(0), HEADS // GROUP
    exchanges = Exchanges(shape, plan, large_all, send_sem, recv_sem)

    @pl.when(part == 0)
    def _():
        copy = pltpu.make_async_copy(large_ref, exchanges.mine(), local_sem.at[0])
        copy.start()
        start_barrier(shape)
        copy.wait()
        exchanges.run(0)

    def meanwhile(at):
        for p in range(parts):
            time = 1 + 2 * p + at

            @pl.when(part == p)
            def _():
                exchanges.run(time)

    ahead = lax.rem(lax.axis_index("heads") * own, halo + 1)
    forward_body(
        groups, block, own, halo, ahead, meanwhile, normed_ref, weight_ref, cos_ref, sin_ref, latent_ref,
        rope_ref, up_ref, mixed_ref, log_ref, q_ref, query_s, top_s, sum_s,
    )

    @pl.when(part == parts - 1)
    def _():
        for time in range(1 + 2 * parts, exchanges.times + 1):
            exchanges.run(time)


def attend_gather(shape, groups, normed, near, cos, sin, window, large, block, own, halo):
    rows, wide = own * block, (halo + own) * block
    cuts, shards, once = near.shape[0], near.shape[1], pl.Buffered(1)
    plan = exchange_plan(large.shape[0], CHUNKS)
    count = len(plan) * len(leading(shape))

    def whole(shape):
        return pl.BlockSpec(shape, lambda g: (0,) * len(shape), pipeline_mode=once)

    def heads_block(rows_at):
        return lambda g: (0, g * GROUP % shards // GROUP, rows_at, g * GROUP // shards)

    mixed, logs, queries, large_all = pl.pallas_call(
        functools.partial(attend_gather_kernel, shape, plan, groups, block, own, halo),
        grid=(HEADS // GROUP,),
        in_specs=[
            whole((rows, D)),
            pl.BlockSpec((cuts, GROUP, D // cuts, LANES), heads_block(0)),
            whole((rows, LANES)),
            whole((rows, LANES)),
            whole((wide, LGROUPS * LAT)),
            pl.BlockSpec((wide, LANES), lambda g: (0, LGROUPS * LAT // LANES), pipeline_mode=once),
            pl.BlockSpec((cuts, GROUP, LAT // cuts, LANES), heads_block(D // LAT)),
            pl.BlockSpec(memory_space=pl.ANY),
        ],
        out_specs=[
            pl.BlockSpec((None, GROUP * HD, rows), lambda g: (g, 0, 0)),
            pl.BlockSpec((None, GROUP, 1, rows), lambda g: (g, 0, 0, 0)),
            pl.BlockSpec((None, rows, GROUP * LANES), lambda g: (g, 0, 0)),
            pl.BlockSpec(memory_space=pltpu.HBM),
        ],
        out_shape=[
            jax.ShapeDtypeStruct((HEADS // GROUP, GROUP * HD, rows), bf16),
            jax.ShapeDtypeStruct((HEADS // GROUP, GROUP, 1, rows), f32),
            jax.ShapeDtypeStruct((HEADS // GROUP, rows, GROUP * LANES), bf16),
            jax.ShapeDtypeStruct((2,) * len(leading(shape)) + large.shape, bf16),
        ],
        scratch_shapes=[
            pltpu.VMEM((GROUP, LANES, rows), bf16),
            pltpu.VMEM((GROUP, 1, rows), f32),
            pltpu.VMEM((GROUP, TALL, rows), f32),
            pltpu.SemaphoreType.DMA((1,)),
            pltpu.SemaphoreType.DMA((count,)),
            pltpu.SemaphoreType.DMA((count,)),
        ],
        compiler_params=pltpu.CompilerParams(
            collective_id=2, has_side_effects=True, vmem_limit_bytes=60 << 20
        ),
        name="attend_gather",
    )(normed, near, cos, sin, window, window, near, large)
    large_all = large_all.reshape((shape["rows"], shape["heads"]) + large.shape)
    return [(mixed[p], logs[p], queries[p]) for p in range(HEADS // GROUP)], large_all


def feed_kernel(
    cuts, shards, units, side_ref, normed_ref, grad_ref, weight_ref, out_ref, dnormed_ref, kept_ref, sent_ref
):
    def whole(which):
        return jnp.concatenate(
            [
                jnp.concatenate(
                    [weight_ref[q, t, which * units : (which + 1) * units, :] for q in range(cuts)],
                    axis=1,
                )
                for t in range(shards)
            ],
            axis=0,
        )

    wide = D // cuts
    side = side_ref[0]

    def put(which, grad):
        at = slice(which * units, (which + 1) * units)
        for t in range(shards):
            rows = slice(t * units, (t + 1) * units)
            for q in range(cuts // 2):
                even = grad[rows, 2 * q * wide : (2 * q + 1) * wide].astype(bf16)
                odd = grad[rows, (2 * q + 1) * wide : (2 * q + 2) * wide].astype(bf16)
                kept_ref[q, t, at, :] = jnp.where(side == 0, even, odd)
                sent_ref[q, t, at, :] = jnp.where(side == 0, odd, even)

    @pl.when(pl.program_id(0) == 0)
    def _():
        out_ref[...] = jnp.zeros_like(out_ref)
        dnormed_ref[...] = jnp.zeros_like(dnormed_ref)

    normed = normed_ref[...]
    grad = grad_ref[...]
    w_gate, w_up, w_down = whole(0), whole(1), whole(2)
    gate = dot_nt(w_gate, normed)
    upper = dot_nt(w_up, normed)
    grad_inner = dot_nt(w_down, grad)
    sig = jax.nn.sigmoid(gate)
    silu = gate * sig
    inner = (silu * upper).astype(bf16)
    grad_gate = (grad_inner * upper * sig * (1.0 + gate * (1.0 - sig))).astype(bf16)
    grad_upper = (grad_inner * silu).astype(bf16)
    out_ref[...] += dot_tn(inner, w_down)
    dnormed_ref[...] += dot_tn(grad_gate, w_gate)
    dnormed_ref[...] += dot_tn(grad_upper, w_up)
    put(0, dot_nn(grad_gate, normed))
    put(1, dot_nn(grad_upper, normed))
    put(2, dot_nn(inner, grad))


def feed_forward_both(side, normed, grad, weights, units):
    rows = normed.shape[0]
    cuts, pieces, _, wide = weights.shape
    shards = max(1, min(pieces, 704 // units))
    once = pl.Buffered(1)
    half = (cuts // 2, shards, 3 * units, wide)
    whole = pl.BlockSpec((rows, D), lambda f, s: (0, 0), pipeline_mode=once)
    return pl.pallas_call(
        functools.partial(feed_kernel, cuts, shards, units),
        grid_spec=pltpu.PrefetchScalarGridSpec(
            num_scalar_prefetch=1,
            grid=(pieces // shards,),
            in_specs=[
                whole,
                whole,
                pl.BlockSpec((cuts, shards, 3 * units, wide), lambda f, s: (0, f, 0, 0)),
            ],
            out_specs=[
                whole,
                whole,
                pl.BlockSpec(half, lambda f, s: (0, f, 0, 0)),
                pl.BlockSpec(half, lambda f, s: (0, f, 0, 0)),
            ],
        ),
        out_shape=[
            jax.ShapeDtypeStruct((rows, D), f32),
            jax.ShapeDtypeStruct((rows, D), f32),
            jax.ShapeDtypeStruct((cuts // 2, pieces, 3 * units, wide), bf16),
            jax.ShapeDtypeStruct((cuts // 2, pieces, 3 * units, wide), bf16),
        ],
        compiler_params=pltpu.CompilerParams(vmem_limit_bytes=60 << 20),
        cost_estimate=pl.CostEstimate(
            flops=40 * 10**9, bytes_accessed=50 * 10**6, transcendentals=0
        ),
        name="feed_forward_both",
    )(side, normed, grad, weights)


def scatter_orders(shape):
    return [order[::-1] for order in gather_orders(shape)]


class Scatter:

    def __init__(self, shape, order, array, started=None):
        self.shape = shape
        self.order = list(scatter_orders(shape)[order])
        self.lead = leading(shape)
        self.terms = [array]
        if started is not None:
            self.order.pop(0)
            self.lead.remove(("rows", 0))
            self.terms = [array, started]
        self.terms = [t.reshape((2,) * len(self.lead) + t.shape[2:]) for t in self.terms]

    def total(self, terms):
        if len(terms) == 1:
            return terms[0]
        return sum(t.astype(f32) for t in terms).astype(bf16)

    def halves(self):
        axis, bit = self.order[0]
        at = self.lead.index((axis, bit))
        upper = upper_bit(axis, bit)

        def half(which):
            return self.total(
                [lax.dynamic_index_in_dim(t, which, at, keepdims=False) for t in self.terms]
            )

        return half(upper), half(1 - upper)

    def send(self, kept, sent):
        axis, bit = self.order.pop(0)
        self.lead.remove((axis, bit))
        self.terms = [kept, lax.ppermute(sent, axis, bit_pairs(self.shape[axis], bit))]

    def left(self):
        perm = [self.lead.index(item) for item in self.order]
        array = self.total(self.terms)
        array = array.transpose(perm + list(range(len(perm), array.ndim)))
        return array.reshape((2 ** len(perm),) + array.shape[len(perm) :])


def step_all(scatters, tied):
    halves = [scatter.halves() for scatter in scatters]
    sent, tied = lax.optimization_barrier(([half[1] for half in halves], tied))
    for scatter, half, out in zip(scatters, halves, sent):
        scatter.send(half[0], out)
    return tied


def scatter_kernel(shape, orders, *refs):
    count = len(orders)
    arrays, outs = refs[:count], refs[count : 2 * count]
    scratch, (send_sem, recv_sem) = list(refs[2 * count : -2]), refs[-2:]
    index = {"rows": lax.axis_index("rows"), "heads": lax.axis_index("heads")}
    start_barrier(shape)
    held, flying = list(arrays), [None] * count
    semaphore = 0
    for stage in range(max(len(order) for order in orders) + 1):
        for i, order in enumerate(orders):
            if flying[i] is not None:
                copy, kept, landed, begin, half = flying[i]
                copy.wait()
                flying[i] = None
                if stage < len(order):
                    summed = scratch.pop(0)

                    def add(at, _):
                        both = kept[begin + at].astype(f32) + landed[at].astype(f32)
                        summed[at] = both.astype(bf16)
                        return 0

                    lax.fori_loop(0, half, add, 0)
                    held[i] = summed
                else:
                    outs[i][...] = kept[begin].astype(f32) + landed[0].astype(f32)
            if stage < len(order):
                axis, bit = order[stage]
                upper = lax.rem(index[axis] // (1 << bit), 2)
                half = held[i].shape[0] // 2
                landed = scratch.pop(0)
                copy = pltpu.make_async_remote_copy(
                    src_ref=held[i].at[pl.ds((1 - upper) * half, half)],
                    dst_ref=landed,
                    send_sem=send_sem.at[semaphore],
                    recv_sem=recv_sem.at[semaphore],
                    device_id={axis: flip(index[axis], bit)},
                    device_id_type=pl.DeviceIdType.MESH,
                )
                copy.start()
                flying[i] = (copy, held[i], landed, upper * half, half)
                semaphore += 1


def scatter_rest(shape, scatters):
    orders = [tuple(scatter.order) for scatter in scatters]
    arrays = [scatter.left() for scatter in scatters]
    scratch = []
    for stage in range(max(len(order) for order in orders) + 1):
        for order, array in zip(orders, arrays):
            tail = array.shape[1:]
            if 0 < stage < len(order):
                scratch.append(pltpu.VMEM((array.shape[0] >> stage,) + tail, bf16))
            if stage < len(order):
                scratch.append(pltpu.VMEM((array.shape[0] >> (stage + 1),) + tail, bf16))
    total = sum(len(order) for order in orders)
    inside = pl.BlockSpec(memory_space=pltpu.VMEM)
    return pl.pallas_call(
        functools.partial(scatter_kernel, shape, orders),
        in_specs=[inside] * len(arrays),
        out_specs=[inside] * len(arrays),
        out_shape=[jax.ShapeDtypeStruct(array.shape[1:], f32) for array in arrays],
        scratch_shapes=scratch
        + [pltpu.SemaphoreType.DMA((total,)), pltpu.SemaphoreType.DMA((total,))],
        compiler_params=pltpu.CompilerParams(
            collective_id=1, has_side_effects=True, vmem_limit_bytes=48 << 20
        ),
        name="scatter_rest",
    )(*arrays)


def on_device(
    shape,
    tokens,
    cotangent,
    domain,
    group_weight,
    gain_attn,
    w_query,
    w_query_rope,
    w_latent,
    w_key_rope,
    w_key_up,
    w_value_up,
    w_out,
    gain_mlp,
    w_gate,
    w_up,
    w_down,
):
    n_rows, n_heads = shape["rows"], shape["heads"]
    row_at, head_at = lax.axis_index("rows"), lax.axis_index("heads")
    local = tokens.shape[0]
    block = math.gcd(local, LEN)
    own, halo = local // block, LEN // block - 1
    here = w_query.shape[1] // HD
    units = w_gate.shape[1]
    cut = D // n_rows
    half = RD // 2

    head_of = [(i % n_heads) * here + i // n_heads for i in range(HEADS)]
    group_of = [head // GROUP for head in head_of]
    parts = [tuple(group_of[p * GROUP : (p + 1) * GROUP]) for p in range(HEADS // GROUP)]

    start = head_at * local
    positions = ((start + jnp.arange(local)) % LEN).astype(f32)
    frequency = THETA ** (-(jnp.arange(LANES) % half).astype(f32) / half)
    angles = positions[:, None] * frequency[None, :]
    cos, sin = jnp.cos(angles), jnp.sin(angles)
    ahead = start // block % (LEN // block)
    places = jnp.stack([ahead, jnp.minimum(LEN // block - ahead, own)]).astype(jnp.int32)

    gain_one, gain_two = gain_attn.reshape(1, D), gain_mlp.reshape(1, D)
    normed, latent = prepare(tokens, gain_one, w_latent, w_key_rope, cos, sin)

    def halo_pairs(k):
        back = -(-k // own)
        needs = [i for i in range(n_heads) if (i * local % LEN) // block >= k]
        return [(i - back, i) for i in needs]

    direct = cut % LANES == 0 and GROUP % n_heads == 0
    if direct:
        near, large = pack(
            row_at.astype(jnp.int32).reshape(1),
            n_rows, w_query, w_query_rope, w_key_up, w_value_up, w_out, w_gate, w_up, w_down,
        )
        window, near = gather_near(shape, latent, near, block, own, halo)
        out, base = near, (D + LAT) // n_rows
    else:
        pieces = []
        for k in range(halo, 0, -1):
            at = own - 1 - (k - 1) % own
            pieces.append(
                lax.ppermute(latent[at * block : (at + 1) * block], "heads", halo_pairs(k))
            )
        window = jnp.concatenate(pieces + [latent], axis=0)
        queries = jnp.concatenate(
            [
                w_query.reshape(D, here, HD),
                w_query_rope.reshape(D, here, RD),
                jnp.zeros((D, here, LANES - HD - RD), bf16),
            ],
            axis=2,
        ).reshape(n_rows, cut, here * LANES)
        ups = jnp.concatenate(
            [w_key_up.reshape(LAT, here, HD), w_value_up.reshape(LAT, here, HD)], axis=2
        ).reshape(n_rows, LAT // n_rows, here * LANES)
        near = jnp.concatenate([queries, ups], axis=1)
        near = lax.all_gather(near, "heads", axis=1)
        out, base = lax.all_gather(w_out, "heads", axis=0)[None], 0
        large = jnp.concatenate([w_gate.T, w_up.T, w_down], axis=0)
        large = lax.all_gather(large, "heads", axis=0).reshape(n_heads, 3 * units, 2, D // 2)
        large = large.transpose(2, 0, 1, 3)

    if direct:
        forward, large = attend_gather(
            shape, parts[0], normed, near, cos, sin, window, large, block, own, halo
        )
    else:
        forward = [
            attend_forward(p, groups, places, normed, near, cos, sin, window, block, own, halo)
            for p, groups in enumerate(parts)
        ]
    mixed = [f[0] for f in forward]
    hidden, normed_mlp = join(tokens, gain_two, mixed, out, base)

    seq_weights = jnp.sum(
        (domain[:, None] == jnp.arange(group_weight.shape[0])[None, :]).astype(f32)
        * group_weight[None, :],
        axis=1,
    )
    token_seq = (start + jnp.arange(local)) // LEN
    token_weight = jnp.sum(
        (token_seq[:, None] == jnp.arange(domain.shape[0])[None, :]).astype(f32)
        * seq_weights[None, :],
        axis=1,
    )[:, None]
    grad_low = (cotangent.astype(f32) * token_weight).astype(bf16)
    core = upper_bit("rows", 0)
    side = core if direct else jnp.zeros_like(core)
    feed_out, grad_normed_mlp, feed_kept, feed_sent = feed_forward_both(
        side.astype(jnp.int32).reshape(1), normed_mlp, grad_low, large, units
    )
    if not direct:
        grad_feed = jnp.concatenate([feed_kept[0], feed_sent[0]], axis=2)
        grad_feed = grad_feed.reshape(n_heads, 3 * units, n_rows // 2, 2, cut)
        grad_feed = grad_feed.transpose(3, 2, 0, 1, 4)
        feed_kept = lax.dynamic_index_in_dim(grad_feed, core, 0, keepdims=False)
        feed_sent = lax.dynamic_index_in_dim(grad_feed, 1 - core, 0, keepdims=False)
    feed_got = lax.ppermute(feed_sent, "rows", bit_pairs(n_rows, 0))
    half_way = 3 * units // 2
    scatter_feed = [
        Scatter(shape, 0, feed_kept[:, :, :half_way], feed_got[:, :, :half_way]),
        Scatter(shape, 1, feed_kept[:, :, half_way:], feed_got[:, :, half_way:]),
    ]
    block_output, grad_hidden, grad_out, grad_gain_two, *grad_mixed = middle(
        hidden, feed_out, grad_normed_mlp, cotangent, token_weight, gain_two, mixed, out, base
    )
    if not direct:
        grad_out = grad_out.reshape(n_heads, here * HD, n_rows, cut).transpose(2, 0, 1, 3)

    by_part = GROUP % n_heads == 0
    scatter_near, pieces, before = [], [], None
    scatter_out = Scatter(shape, 0, grad_out)
    for p, groups in enumerate(parts):
        under_way = scatter_feed + ([scatter_out] + scatter_near if p else [])
        grad_mixed[p] = step_all(under_way, grad_mixed[p])
        *before, grad_near = attend_backward(
            p, groups, places, forward[p], normed, near, cos, sin, window, grad_mixed[p], before,
            block, own, halo,
        )
        if by_part:
            scatter_near.append(Scatter(shape, 1, grad_near))
        else:
            pieces.append(grad_near)
    if not by_part:
        scatter_near.append(Scatter(shape, 1, jnp.concatenate(pieces, axis=1)))
    grad_window, grad_normed = before
    got = [
        lax.ppermute(
            grad_window[(halo - k) * block : (halo - k + 1) * block],
            "heads",
            [(b, a) for a, b in halo_pairs(k)],
        )
        for k in range(1, halo + 1)
    ]
    grad_normed = step_all(scatter_feed + [scatter_out] + scatter_near, grad_normed)
    grad_tokens, grad_latent, grad_gain_one = finish(
        grad_window, got, tokens, normed, grad_normed, grad_hidden, gain_one, w_latent, w_key_rope, cos, sin,
        block, own, halo,
    )
    gains = jnp.concatenate([grad_gain_one, grad_gain_two], axis=0).astype(bf16)
    gains = gains.reshape(2, n_rows, n_heads, -1).transpose(1, 2, 0, 3)
    gains = jnp.pad(gains, ((0, 0), (0, 0), (0, 14), (0, LANES - gains.shape[3])))
    grad_latent = grad_latent.reshape(n_rows, n_heads, D // (n_rows * n_heads), -1)
    own_first, own_second, own_out, own_latent, own_gain, *own_near = scatter_rest(
        shape,
        scatter_feed
        + [scatter_out, Scatter(shape, 0, grad_latent), Scatter(shape, 1, gains)]
        + scatter_near,
    )
    own_feed = jnp.concatenate([own_first, own_second], axis=0)
    own_near = jnp.concatenate(own_near, axis=1)
    own_query = own_near[:cut].reshape(cut, here, LANES)
    own_up = own_near[cut:].reshape(LAT // n_rows, here, LANES)
    at, gain_cut = LGROUPS * LAT, D // (n_rows * n_heads)
    return (
        block_output,
        grad_tokens,
        own_gain[0, :gain_cut],
        own_query[:, :, :HD].reshape(cut, here * HD),
        own_query[:, :, HD : HD + RD].reshape(cut, here * RD),
        own_latent[:, :at],
        own_latent[:, at + HD : at + HD + RD],
        own_up[:, :, :HD].reshape(LAT // n_rows, here * HD),
        own_up[:, :, HD:].reshape(LAT // n_rows, here * HD),
        own_out,
        own_gain[1, :gain_cut],
        own_feed[:units].T,
        own_feed[units : 2 * units].T,
        own_feed[2 * units :],
    )


def solution(mesh):
    in_specs = (
        P(("rows", "heads"), None),
        P(("rows", "heads"), None),
        P("rows"),
        P(),
        P(),
        P(None, "heads"),
        P(None, "heads"),
        P(),
        P(),
        P(None, "heads"),
        P(None, "heads"),
        P("heads", None),
        P(),
        P(None, "heads"),
        P(None, "heads"),
        P("heads", None),
    )
    out_specs = (
        P(("rows", "heads"), None),
        P(("rows", "heads"), None),
        P(("rows", "heads")),
        P("rows", "heads"),
        P("rows", "heads"),
        P(("rows", "heads"), None),
        P(("rows", "heads"), None),
        P("rows", "heads"),
        P("rows", "heads"),
        P("heads", "rows"),
        P(("rows", "heads")),
        P("rows", "heads"),
        P("rows", "heads"),
        P("heads", "rows"),
    )
    return jax.shard_map(
        functools.partial(on_device, dict(mesh.shape)),
        mesh=mesh,
        in_specs=in_specs,
        out_specs=out_specs,
        check_vma=False,
    )
```

time: 619 us -> 581 us (0.939)
  Pallas kernels: 354 us -> 399 us
  matrix products: 27.3 us -> 0 us
  other arithmetic: 61.6 us -> 35.1 us
  local copies, waits for them, and re-layouts: 83.4 us -> 65.2 us
  starting transfers between devices: 29.6 us -> 18.9 us
    pallas_call x4 -> x7, Pallas kernels: 182 us -> 233 us  [the longest x1 112 us: attend_gather(): pl.pallas_call(functools.partial(attend_gather_kernel, shape, plan, group...]
    dot_general x19 -> x0, matrix products: 27.3 us -> none  [the longest x5 11.1 us: dot_nt(): lax.dot_general(a, b, (((1,), (1,)), ((), ())), preferred_element_type=f32)]
    pallas_call x1, Pallas kernels: 67.9 us -> 50.3 us  [scatter_rest(): pl.pallas_call(functools.partial(scatter_kernel, shape, orders), in_specs...]
    convert_element_type x8 -> x15, other arithmetic: 14.3 us -> 27.9 us  [total(): return sum((t.astype(f32) for t in terms)).astype(bf16)]
    pallas_call x2, Pallas kernels: 53.6 us -> 66.2 us  [attend_backward(): pl.pallas_call(functools.partial(attend_backward_kernel, groups, block, o...]
    ppermute x6 -> x11, starting transfers between devices: 20.5 us -> 9.24 us  [send(): lax.ppermute(sent, axis, bit_pairs(self.shape[axis], bit))]
    transpose x6 -> x0, local copies, waits for them, and re-layouts: 10.8 us -> none  [the longest x3 7.53 us: on_device(): query_weights.append(weight.transpose(0, 2, 1, 3).reshape(D, GROUP * LANES))]
    convert_element_type x6 -> x1, other arithmetic: 13.8 us -> 3.18 us  [on_device(): grad_low = (cotangent.astype(f32) * token_weight).astype(bf16)]
  transfers between devices with their start and end apart: 14 -> 19, of which waited for: 6 -> 8; matrix products, arithmetic and copies ran while one was open for 10% -> 7% of each run, Pallas kernels for 4% -> 15%
where the time goes in v3:
time: 581 us; the launch traced here: 576 us
  Pallas kernels  399 us (69%)
  local copies, waits for them, and re-layouts  65.2 us (11%)
  waiting for transfers between devices  55.3 us (10%)
  other arithmetic  35.1 us (6%)
  starting transfers between devices  18.9 us (3%)
    pallas_call x1, Pallas kernels, attend_gather(): pl.pallas_call(functools.partial(attend_gather_kernel, shape, plan, group...  112 us
    pallas_call x1, Pallas kernels, gather_near(): pl.pallas_call(functools.partial(gather_kernel, shape, plan, block, own,...  92.1 us
    pallas_call x2, Pallas kernels, attend_backward(): pl.pallas_call(functools.partial(attend_backward_kernel, groups, block, o...  66.2 us
    pallas_call x1, Pallas kernels, scatter_rest(): pl.pallas_call(functools.partial(scatter_kernel, shape, orders), in_specs...  50.3 us
    pallas_call x1, Pallas kernels, feed_forward_both(): pl.pallas_call(functools.partial(feed_kernel, cuts, shards, units), grid_...  49.9 us
    ppermute x7, waiting for transfers between devices, on_device(): lax.ppermute(grad_window[(halo - k) * block:(halo - k + 1) * block], 'hea...  36.2 us
    unnamed x86, local copies, waits for them, and re-layouts  28 us
    convert_element_type x15, other arithmetic, total(): return sum((t.astype(f32) for t in terms)).astype(bf16)  27.9 us
  transfers between devices with their start and end apart: 19, of which 8 were waited for; matrix products, arithmetic and copies ran while one was open for 7% of the time, Pallas kernels for 15%

profile of v3, /device:TPU:0, one launch (start us, length us, event | category | flops | bytes accessed | tf_op | source)
XLA Modules:
  0.0 575.7 jit_solution(821287665746711768)
XLA Ops:
  2.0 1.7 copy.80.rope_ref
  3.8 1.9 copy.81.rope_ref
  5.7 2.3 copy.82.gate_ref
  7.9 2.3 copy.83.up_ref
  10.2 1.4 multiply_sine_fusion
  12.9 1.8 prepare.1
  14.7 1.2 copy-done.6
  16.8 2.4 pack.1
  20.1 92.1 %gather_near.1 = (bf16[2560,640]{1,0:T(8,128)(2,1)S(1)}, bf16[2,2,2,2,2,448,256]{6,5,4,3,2,1,0:T(8,128)(2,1)S(1)}) custom-call(bf16[768,640]{1,0:T(8,128)(2,1)S(1)} %copy-done.13, bf16[448,256]{1,0:T(8,128)(2,1)S(1)} %copy-done.14), custom_call_target="tpu_custom_call" | custom-call | tf_op jit(solution)/shard_map/gather_near/pallas_call | solution.py:802
  112.3 3.0 copy-done
  115.3 1.7 copy-done.3
  116.9 112.2 %attend_gather.1 = (bf16[2,512,768]{2,1,0:T(8,128)(2,1)}, f32[2,8,1,768]{3,2,1,0:T(1,128)}, bf16[2,768,1024]{2,1,0:T(8,128)(2,1)}, bf16[2,2,2,2,2,1056,256]{6,5,4,3,2,1,0:T(8,128)(2,1)}) custom-call(bf16[768,1024]{1,0:T(8,128)(2,1)} %copy-done.6, bf16[4,8,448,256]{3,2,1,0:T(8,128)(2,1)} %bitcast.151, f32[768,128]{1,0:T(8,128)} %copy-done.8, ...), custom_call_target="tpu_custom_call" | custom-call | tf_op jit(solution)/shard_map/attend_gather/pallas_call | solution.py:873
  229.1 1.5 slice_bitcast_fusion.2
  230.9 3.2 multiply_convert_fusion.grad_ref
  234.1 3.1 copy-done.1
  237.2 2.4 join.1
  239.6 1.7 copy-done.10
  242.4 49.9 %feed_forward_both.1 = (f32[768,1024]{1,0:T(8,128)}, f32[768,1024]{1,0:T(8,128)}, bf16[2,8,1056,256]{3,2,1,0:T(8,128)(2,1)}, bf16[2,8,1056,256]{3,2,1,0:T(8,128)(2,1)}) custom-call(s32[1]{0:T(128)} %bitcast.4.side_ref, bf16[768,1024]{1,0:T(8,128)(2,1)} %copy-done.16, bf16[768,1024]{1,0:T(8,128)(2,1)} %multiply_convert_fusion.grad_ref, ...), custom_call_target="tpu_custom_call" | custom-call | flops 40000000000 | bytes 50000000 | tf_op jit(solution)/shard_map/feed_forward_both/pallas_call | solution.py:974
  293.1 11.0 %middle.1 = (bf16[768,1024]{1,0:T(8,128)(2,1)}, f32[768,1024]{1,0:T(8,128)}, bf16[4,8,128,256]{3,2,1,0:T(8,128)(2,1)}, f32[1,1024]{1,0:T(1,128)S(1)}, bf16[512,7...) custom-call(f32[768,1024]{1,0:T(8,128)} %copy-done.10, f32[768,1024]{1,0:T(8,128)} %get-tuple-element.76.feed_ref, ...), custom_call_target="tpu_custom_call" | custom-call | tf_op jit(solution)/shard_map/middle/pallas_call | solution.py:569
  304.6 2.9 copy_bitcast_fusion.3
  308.6 3.8 fusion.34
  312.8 1.6 constant_dynamic-slice_fusion.9
  315.5 2.0 slice_bitcast_fusion
  317.6 3.8 fusion.35
  321.4 1.6 constant_dynamic-slice_fusion.14
  323.1 1.7 constant_dynamic-slice_fusion.8
  324.8 2.0 fusion.1
  326.7 1.9 fusion.2
  328.7 2.2 collective-permute-start.2
  330.9 32.4 %attend_backward.2 = (bf16[2560,640]{1,0:T(8,128)(2,1)}, f32[768,1024]{1,0:T(8,128)}, bf16[4,8,320,128]{3,2,1,0:T(8,128)(2,1)}) custom-call(s32[2]{0:T(128)} %pad_add_fusion.place_ref, bf16[768,1024]{1,0:T(8,128)(2,1)} %get-tuple-element.169.q_ref, bf16[2560,640]{1,0:T(8,128)(2,1)} %copy-done.3, bf16[2560,640]{1,0:T(8,128)(2,1)} %copy-done.3, ...), custom_call_target="tpu_custom_call" | custom-call | flops 40000000000 | bytes 30000000 | tf_op jit(solution)/shard_map/attend_backward/pallas_call | solution.py:413
  363.4 2.6 copy_bitcast_fusion.2
  370.0 8.1 %collective-permute-done.1 = bf16[2,2,2,528,256]{4,3,0,2,1:T(8,128)(2,1)} collective-permute-done((bf16[2,2,2,528,256]{4,3,0,2,1:T(8,128)(2,1)}, bf16[2,2,2,528,256]{4,3,0,2,1:T(8,128)(2,1)}, u32[]{:S(2)}, u32[]{:S(2)}) %collective-permute-start.1) | collective-permute-done | bytes 2162720 | tf_op jit(solution)/shard_map/ppermute | solution.py:1042
  378.1 3.1 fusion.4
  381.2 3.1 fusion.3
  384.3 1.8 collective-permute-start.3
  387.4 33.8 %attend_backward.3 = (bf16[2560,640]{1,0:T(8,128)(2,1)}, f32[768,1024]{1,0:T(8,128)}, bf16[4,8,320,128]{3,2,1,0:T(8,128)(2,1)}) custom-call(s32[2]{0:T(128)} %pad_add_fusion.place_ref, bf16[768,1024]{1,0:T(8,128)(2,1)} %get-tuple-element.170.q_ref, bf16[2560,640]{1,0:T(8,128)(2,1)} %copy-done.3, bf16[2560,640]{1,0:T(8,128)(2,1)} %copy-done.3, ...), custom_call_target="tpu_custom_call" | custom-call | flops 40000000000 | bytes 30000000 | tf_op jit(solution)/shard_map/attend_backward/pallas_call | solution.py:413
  421.3 2.1 constant_dynamic-slice_fusion.7
  423.3 1.2 copy.151
  425.6 1.3 collective-permute-start.7
  426.9 1.3 collective-permute-start.8
  428.2 2.1 fusion.18
  430.3 1.3 collective-permute-start.9
  431.6 2.0 fusion.19
  433.6 1.3 collective-permute-start.10
  434.9 2.0 fusion.20
  436.9 7.6 %collective-permute-done.7.refs_0_ = bf16[256,640]{1,0:T(8,128)(2,1)S(1)} collective-permute-done((bf16[256,640]{1,0:T(8,128)(2,1)S(1)}, bf16[256,640]{1,0:T(8,128)(2,1)S(1)}, u32[]{:S(2)}, u32[]{:S(2)}) %collective-permute-start.7) | collective-permute-done | bytes 327712 | tf_op jit(solution)/shard_map/ppermute | solution.py:1278
  444.5 1.3 collective-permute-start.11
  445.8 5.7 collective-permute-done.8.refs_1_
  452.2 1.3 collective-permute-start.12
  453.5 1.6 collective-permute-start.13
  455.1 2.1 fusion.8
  457.9 2.0 collective-permute-start.16
  459.9 9.7 %collective-permute-done.10.refs_3_ = bf16[256,640]{1,0:T(8,128)(2,1)S(1)} collective-permute-done((bf16[256,640]{1,0:T(8,128)(2,1)S(1)}, bf16[256,640]{1,0:T(8,128)(2,1)S(1)}, u32[]{:S(2)}, u32[]{:S(2)}) %collective-permute-start.10) | collective-permute-done | bytes 327712 | tf_op jit(solution)/shard_map/ppermute | solution.py:1278
  470.5 6.1 %collective-permute-done.11.refs_4_ = bf16[256,640]{1,0:T(8,128)(2,1)S(1)} collective-permute-done((bf16[256,640]{1,0:T(8,128)(2,1)S(1)}, bf16[256,640]{1,0:T(8,128)(2,1)S(1)}, u32[]{:S(2)}, u32[]{:S(2)}) %collective-permute-start.11) | collective-permute-done | bytes 327712 | tf_op jit(solution)/shard_map/ppermute | solution.py:1278
  477.5 6.3 %collective-permute-done.12.refs_5_ = bf16[256,640]{1,0:T(8,128)(2,1)} collective-permute-done((bf16[256,640]{1,0:T(8,128)(2,1)}, bf16[256,640]{1,0:T(8,128)(2,1)}, u32[]{:S(2)}, u32[]{:S(2)}) %collective-permute-start.12) | collective-permute-done | bytes 327712 | tf_op jit(solution)/shard_map/ppermute | solution.py:1278
  484.6 11.2 %finish.1 = (f32[768,1024]{1,0:T(8,128)}, bf16[1024,640]{1,0:T(8,128)(2,1)}, f32[1,1024]{1,0:T(1,128)}) custom-call(bf16[2560,640]{1,0:T(8,128)(2,1)} %get-tuple-element.93.dwindow_ref, bf16[768,1024]{1,0:T(8,128)(2,1)} %tokens_ref.5, bf16[768,1024]{1,0:T(8,128)(2,1)} %copy-done.6, f32[768,1024]{1,0:T(8,128)} %get-tuple-element.100.dnormed_ref, ...), custom_call_target="tpu_custom_call" | custom-call | tf_op jit(solution)/shard_map/finish/pallas_call | solution.py:621
  496.7 1.6 copy.102
  498.4 1.4 add_convert_fusion.5
  499.9 1.5 fusion.13.refs_0_
  501.3 1.4 fusion.11.refs_1_
  502.8 11.0 %collective-permute-done.17 = bf16[2,2,2,320,128]{4,3,1,0,2:T(8,128)(2,1)S(1)} collective-permute-done((bf16[2,2,2,320,128]{4,3,1,0,2:T(8,128)(2,1)S(1)}, bf16[2,2,2,320,128]{4,3,1,0,2:T(8,128)(2,1)S(1)}, u32[]{:S(2)}, u32[]{:S(2)}) %collective-permute-start.17) | collective-permute-done | bytes 655392 | tf_op jit(solution)/shard_map/ppermute | solution.py:1042
  513.8 1.3 add_convert_fusion.4
  515.1 2.7 fusion
  517.9 50.3 %scatter_rest.1 = (f32[528,256]{1,0:T(8,128)S(1)}, f32[528,256]{1,0:T(8,128)S(1)}, f32[128,256]{1,0:T(8,128)S(1)}, f32[32,640]{1,0:T(8,128)S(1)}, f32[16,128]{1,...) custom-call(bf16[2,528,256]{2,1,0:T(8,128)(2,1)S(1)} %fusion.13.refs_0_, ...), custom_call_target="tpu_custom_call" | custom-call | tf_op jit(solution)/shard_map/scatter_rest/pallas_call | solution.py:1116
  (134 shorter events, 28.1 us)
Async XLA Ops:
  2.0 9.7 %copy-start.15 = (bf16[1,1024]{1,0:T(2,128)(2,1)}, bf16[1,1024]{1,0:T(2,128)(2,1)S(1)}, u32[]{:S(2)}) copy-start(bf16[1,1024]{1,0:T(2,128)(2,1)S(1)} %reshape.261.gain_ref) | copy-start | bytes 6148
  3.7 8.0 %copy-start.2 = (bf16[768,1024]{1,0:T(8,128)(2,1)S(1)}, bf16[768,1024]{1,0:T(8,128)(2,1)}, u32[]{:S(2)}) copy-start(bf16[768,1024]{1,0:T(8,128)(2,1)} %tokens_ref.5) | copy-start | bytes 4718596
  3.7 8.0 %copy-start.9 = (bf16[1024,512]{1,0:T(8,128)(2,1)S(1)}, bf16[1024,512]{1,0:T(8,128)(2,1)}, u32[]{:S(2)}) copy-start(bf16[1024,512]{1,0:T(8,128)(2,1)} %latent_ref.3) | copy-start | bytes 3145732
  11.7 7.5 %copy-start.7 = (f32[768,128]{1,0:T(8,128)}, f32[768,128]{1,0:T(8,128)S(1)}, u32[]{:S(2)}) copy-start(f32[768,128]{1,0:T(8,128)S(1)} %get-tuple-element.188.sin_ref) | copy-start | bytes 1179652
  11.7 7.5 %copy-start.8 = (f32[768,128]{1,0:T(8,128)}, f32[768,128]{1,0:T(8,128)S(1)}, u32[]{:S(2)}) copy-start(f32[768,128]{1,0:T(8,128)S(1)} %get-tuple-element.189.cos_ref) | copy-start | bytes 1179652
  11.7 1.2 copy-start.11
  14.7 1.2 copy-start.6
  15.8 0.9 copy-start.12
  16.8 2.4 copy-start.13
  19.2 0.9 copy-start.14
  112.3 3.0 copy-start
  115.2 1.7 copy-start.3
  229.1 1.5 copy-start.37
  229.1 1.5 copy-start.38
  230.6 62.4 %copy-start.4 = (bf16[512,768]{1,0:T(8,128)(2,1)}, bf16[512,768]{1,0:T(8,128)(2,1)S(1)}, u32[]{:S(2)}) copy-start(bf16[512,768]{1,0:T(8,128)(2,1)S(1)} %get-tuple-element.177.refs_1_.mixed_ref) | copy-start | bytes 2359300
  230.6 62.4 %copy-start.5 = (bf16[512,768]{1,0:T(8,128)(2,1)}, bf16[512,768]{1,0:T(8,128)(2,1)S(1)}, u32[]{:S(2)}) copy-start(bf16[512,768]{1,0:T(8,128)(2,1)S(1)} %get-tuple-element.178.refs_0_.mixed_ref) | copy-start | bytes 2359300
  234.1 3.1 copy-start.1
  239.6 1.7 copy-start.10
  241.3 1.1 copy-start.16
  292.4 25.2 %collective-permute-start = (bf16[2,8,1056,256]{3,2,1,0:T(8,128)(2,1)}, bf16[2,8,1056,256]{3,2,1,0:T(8,128)(2,1)}, u32[]{:S(2)}, u32[]{:S(2)}) collective-permute-start(bf16[2,8,1056,256]{3,2,1,0:T(8,128)(2,1)} %get-tuple-element.82), channel_id=1, source_target_pairs={{0,8},{8,0},{16,24},{24,16},{1,9},{9,1},{17,25},{25,17},{2,10},{10... | collective-permute-start | bytes 25952264 | tf_op jit(solution)/shard_map/ppermute | solution.py:1248
  304.0 8.5 %copy-start.17 = (bf16[512,768]{1,0:T(8,128)(2,1)}, bf16[512,768]{1,0:T(8,128)(2,1)S(1)}, u32[]{:S(2)}) copy-start(bf16[512,768]{1,0:T(8,128)(2,1)S(1)} %get-tuple-element.90.grad_ref) | copy-start | bytes 2359300
  304.0 8.5 %copy-start.18 = (bf16[512,768]{1,0:T(8,128)(2,1)}, bf16[512,768]{1,0:T(8,128)(2,1)S(1)}, u32[]{:S(2)}) copy-start(bf16[512,768]{1,0:T(8,128)(2,1)S(1)} %get-tuple-element.87.grad_ref) | copy-start | bytes 2359300
  304.0 3.5 copy-start.27
  312.8 1.6 copy-start.36
  312.8 2.7 copy-start.23
  328.7 49.4 %collective-permute-start.1 = (bf16[2,2,2,528,256]{4,3,0,2,1:T(8,128)(2,1)}, bf16[2,2,2,528,256]{4,3,0,2,1:T(8,128)(2,1)}, u32[]{:S(2)}, u32[]{:S(2)}) collective-permute-start(bf16[2,2,2,528,256]{4,3,0,2,1:T(8,128)(2,1)} %fusion.1), channel_id=1, source_target_pairs={{0,16},{8,24},{16,0},{24,8},{1,17},{9,25},{17,1},{25,9},{2,18},{10... | collective-permute-start | bytes 6488072 | tf_op jit(solution)/shard_map/ppermute | solution.py:1042
  328.7 52.5 %collective-permute-start.2 = (bf16[2,2,2,528,256]{4,3,1,2,0:T(8,128)(2,1)}, bf16[2,2,2,528,256]{4,3,1,2,0:T(8,128)(2,1)}, u32[]{:S(2)}, u32[]{:S(2)}) collective-permute-start(bf16[2,2,2,528,256]{4,3,1,2,0:T(8,128)(2,1)} %fusion.2), channel_id=1, source_target_pairs={{0,1},{1,0},{2,3},{3,2},{4,5},{5,4},{6,7},{7,6},{8,9},{9,8},{10,11... | collective-permute-start | bytes 6488072 | tf_op jit(solution)/shard_map/ppermute | solution.py:1042
  363.4 2.6 copy-start.24
  363.4 3.8 copy-start.21
  367.2 1.6 copy-start.20
  367.2 2.3 copy-start.22
  384.3 46.0 %collective-permute-start.3 = (bf16[2,2,528,256]{3,2,0,1:T(8,128)(2,1)}, bf16[2,2,528,256]{3,2,0,1:T(8,128)(2,1)}, u32[]{:S(2)}, u32[]{:S(2)}) collective-permute-start(bf16[2,2,528,256]{3,2,0,1:T(8,128)(2,1)} %get-tuple-element.94), channel_id=1, source_target_pairs={{0,1},{1,0},{2,3},{3,2},{4,5},{5,4},{6,7},{7,6},{8,9},{9,8},{10,11... | collective-permute-start | bytes 3244040 | tf_op jit(solution)/shard_map/ppermute | solution.py:1042
  386.1 47.5 %collective-permute-start.4 = (bf16[2,2,528,256]{3,2,1,0:T(8,128)(2,1)}, bf16[2,2,528,256]{3,2,1,0:T(8,128)(2,1)}, u32[]{:S(2)}, u32[]{:S(2)}) collective-permute-start(bf16[2,2,528,256]{3,2,1,0:T(8,128)(2,1)} %get-tuple-element.95), channel_id=1, source_target_pairs={{0,2},{1,3},{2,0},{3,1},{4,6},{5,7},{6,4},{7,5},{8,10},{9,11},{10,... | collective-permute-start | bytes 3244040 | tf_op jit(solution)/shard_map/ppermute | solution.py:1042
  386.9 39.9 %collective-permute-start.5 = (bf16[2,2,2,2,128,256]{5,4,1,2,3,0:T(8,128)(2,1)}, bf16[2,2,2,2,128,256]{5,4,1,2,3,0:T(8,128)(2,1)}, u32[]{:S(2)}, u32[]{:S(2)}) collective-permute-start(bf16[2,2,2,2,128,256]{5,4,1,2,3,0:T(8,128)(2,1)} %copy_bitcast_fusion.3), channel_id=1, source_target_pairs={{0,8},{8,0},{16,24},{24,16},{1,9},{9,1},{17,25},{25,17},{2,10},{10... | collective-permute-start | bytes 3145736 | tf_op jit(solution)/shard_map/ppermute | solution.py:1042
  386.9 66.6 %collective-permute-start.6 = (bf16[2,2,2,2,320,128]{5,4,1,0,2,3:T(8,128)(2,1)}, bf16[2,2,2,2,320,128]{5,4,1,0,2,3:T(8,128)(2,1)}, u32[]{:S(2)}, u32[]{:S(2)}) collective-permute-start(bf16[2,2,2,2,320,128]{5,4,1,0,2,3:T(8,128)(2,1)} %copy_bitcast_fusion.2), channel_id=1, source_target_pairs={{0,8},{8,0},{16,24},{24,16},{1,9},{9,1},{17,25},{25,17},{2,10},{10... | collective-permute-start | bytes 3932168 | tf_op jit(solution)/shard_map/ppermute | solution.py:1042
  421.3 3.3 copy-start.19
  424.5 3.6 copy-start.29
  425.6 18.9 %collective-permute-start.7 = (bf16[256,640]{1,0:T(8,128)(2,1)S(1)}, bf16[256,640]{1,0:T(8,128)(2,1)S(1)}, u32[]{:S(2)}, u32[]{:S(2)}) collective-permute-start(bf16[256,640]{1,0:T(8,128)(2,1)S(1)} %get-tuple-element.168), channel_id=1, source_target_pairs={{1,0},{2,1},{3,2},{4,3},{5,4},{6,5},{7,6},{9,8},{10,9},{11,10},{12... | collective-permute-start | bytes 983048 | tf_op jit(solution)/shard_map/ppermute | solution.py:1278
  426.9 24.6 %collective-permute-start.8 = (bf16[256,640]{1,0:T(8,128)(2,1)S(1)}, bf16[256,640]{1,0:T(8,128)(2,1)S(1)}, u32[]{:S(2)}, u32[]{:S(2)}) collective-permute-start(bf16[256,640]{1,0:T(8,128)(2,1)S(1)} %get-tuple-element.167), channel_id=1, source_target_pairs={{1,0},{2,1},{4,3},{5,4},{6,5},{7,6},{9,8},{10,9},{12,11},{13,12},{... | collective-permute-start | bytes 983048 | tf_op jit(solution)/shard_map/ppermute | solution.py:1278
  428.2 27.0 %copy-start.25 = (bf16[2,1,2,2,1,320,128]{6,5,4,3,2,1,0:T(8,128)(2,1)S(1)}, bf16[2,1,2,2,1,320,128]{6,5,4,3,2,1,0:T(8,128)(2,1)}, u32[]{:S(2)}) copy-start(bf16[2,1,2,2,1,320,128]{6,5,4,3,2,1,0:T(8,128)(2,1)} %get-tuple-element.174) | copy-start | bytes 1966084
  430.3 27.6 %collective-permute-start.9 = (bf16[256,640]{1,0:T(8,128)(2,1)S(1)}, bf16[256,640]{1,0:T(8,128)(2,1)S(1)}, u32[]{:S(2)}, u32[]{:S(2)}) collective-permute-start(bf16[256,640]{1,0:T(8,128)(2,1)S(1)} %get-tuple-element.166), channel_id=1, source_target_pairs={{1,0},{2,1},{4,3},{5,4},{7,6},{9,8},{10,9},{12,11},{13,12},{15,14}... | collective-permute-start | bytes 983048 | tf_op jit(solution)/shard_map/ppermute | solution.py:1278
  433.6 36.1 %collective-permute-start.10 = (bf16[256,640]{1,0:T(8,128)(2,1)S(1)}, bf16[256,640]{1,0:T(8,128)(2,1)S(1)}, u32[]{:S(2)}, u32[]{:S(2)}) collective-permute-start(bf16[256,640]{1,0:T(8,128)(2,1)S(1)} %get-tuple-element.165), channel_id=1, source_target_pairs={{2,0},{4,2},{5,3},{7,5},{10,8},{12,10},{13,11},{15,13},{18,16},{20... | collective-permute-start | bytes 983048 | tf_op jit(solution)/shard_map/ppermute | solution.py:1278
  444.5 7.0 %copy-start.31 = (bf16[256,640]{1,0:T(8,128)(2,1)}, bf16[256,640]{1,0:T(8,128)(2,1)S(1)}, u32[]{:S(2)}) copy-start(bf16[256,640]{1,0:T(8,128)(2,1)S(1)} %collective-permute-done.7.refs_0_) | copy-start | bytes 983044
  444.5 32.2 %collective-permute-start.11 = (bf16[256,640]{1,0:T(8,128)(2,1)S(1)}, bf16[256,640]{1,0:T(8,128)(2,1)S(1)}, u32[]{:S(2)}, u32[]{:S(2)}) collective-permute-start(bf16[256,640]{1,0:T(8,128)(2,1)S(1)} %get-tuple-element.164), channel_id=1, source_target_pairs={{2,0},{5,3},{7,5},{10,8},{13,11},{15,13},{18,16},{21,19},{23,21},{... | collective-permute-start | bytes 983048 | tf_op jit(solution)/shard_map/ppermute | solution.py:1278
  451.5 0.7 copy-start.32
  452.2 31.6 %collective-permute-start.12 = (bf16[256,640]{1,0:T(8,128)(2,1)}, bf16[256,640]{1,0:T(8,128)(2,1)}, u32[]{:S(2)}, u32[]{:S(2)}) collective-permute-start(bf16[256,640]{1,0:T(8,128)(2,1)} %get-tuple-element.163), channel_id=1, source_target_pairs={{2,0},{5,3},{10,8},{13,11},{18,16},{21,19},{26,24},{29,27}} | collective-permute-start | bytes 983048 | tf_op jit(solution)/shard_map/ppermute | solution.py:1278
  453.5 31.1 %collective-permute-start.13 = (bf16[256,640]{1,0:T(8,128)(2,1)}, bf16[256,640]{1,0:T(8,128)(2,1)}, u32[]{:S(2)}, u32[]{:S(2)}) collective-permute-start(bf16[256,640]{1,0:T(8,128)(2,1)} %get-tuple-element.162), channel_id=1, source_target_pairs={{5,2},{13,10},{21,18},{29,26}} | collective-permute-start | bytes 983048 | tf_op jit(solution)/shard_map/ppermute | solution.py:1278
  457.9 18.8 %copy-start.33 = (bf16[256,640]{1,0:T(8,128)(2,1)}, bf16[256,640]{1,0:T(8,128)(2,1)S(1)}, u32[]{:S(2)}) copy-start(bf16[256,640]{1,0:T(8,128)(2,1)S(1)} %collective-permute-done.9.refs_2_) | copy-start | bytes 983044
  457.9 40.5 %collective-permute-start.16 = (bf16[2,2,2,128,256]{4,3,0,1,2:T(8,128)(2,1)}, bf16[2,2,2,128,256]{4,3,0,1,2:T(8,128)(2,1)}, u32[]{:S(2)}, u32[]{:S(2)}) collective-permute-start(bf16[2,2,2,128,256]{4,3,0,1,2:T(8,128)(2,1)} %fusion.18), channel_id=1, source_target_pairs={{0,16},{8,24},{16,0},{24,8},{1,17},{9,25},{17,1},{25,9},{2,18},{10... | collective-permute-start | bytes 1572872 | tf_op jit(solution)/shard_map/ppermute | solution.py:1042
  469.6 7.0 %copy-start.34 = (bf16[256,640]{1,0:T(8,128)(2,1)}, bf16[256,640]{1,0:T(8,128)(2,1)S(1)}, u32[]{:S(2)}) copy-start(bf16[256,640]{1,0:T(8,128)(2,1)S(1)} %collective-permute-done.10.refs_3_) | copy-start | bytes 983044
  469.6 30.2 %collective-permute-start.14 = (bf16[2,528,256]{2,1,0:T(8,128)(2,1)}, bf16[2,528,256]{2,1,0:T(8,128)(2,1)}, u32[]{:S(2)}, u32[]{:S(2)}) collective-permute-start(bf16[2,528,256]{2,1,0:T(8,128)(2,1)} %fusion.19), channel_id=1, source_target_pairs={{0,2},{1,3},{2,0},{3,1},{4,6},{5,7},{6,4},{7,5},{8,10},{9,11},{10,... | collective-permute-start | bytes 1622024 | tf_op jit(solution)/shard_map/ppermute | solution.py:1042
  476.7 0.7 copy-start.35
  476.7 38.4 %collective-permute-start.18 = (bf16[2,2,2,2,320,128]{5,4,1,0,2,3:T(8,128)(2,1)}, bf16[2,2,2,2,320,128]{5,4,1,0,2,3:T(8,128)(2,1)}, u32[]{:S(2)}, u32[]{:S(2)}) collective-permute-start(bf16[2,2,2,2,320,128]{5,4,1,0,2,3:T(8,128)(2,1)} %bitcast.149), channel_id=1, source_target_pairs={{0,8},{8,0},{16,24},{24,16},{1,9},{9,1},{17,25},{25,17},{2,10},{10... | collective-permute-start | bytes 3932168 | tf_op jit(solution)/shard_map/ppermute | solution.py:1042
  483.8 17.5 %collective-permute-start.15 = (bf16[2,528,256]{2,1,0:T(8,128)(2,1)}, bf16[2,528,256]{2,1,0:T(8,128)(2,1)}, u32[]{:S(2)}, u32[]{:S(2)}) collective-permute-start(bf16[2,528,256]{2,1,0:T(8,128)(2,1)} %fusion.20), channel_id=1, source_target_pairs={{0,16},{8,24},{16,0},{24,8},{1,17},{9,25},{17,1},{25,9},{2,18},{10... | collective-permute-start | bytes 1622024 | tf_op jit(solution)/shard_map/ppermute | solution.py:1042
  496.6 1.7 copy-start.30
  496.6 1.8 copy-start.28
  498.3 15.4 %collective-permute-start.17 = (bf16[2,2,2,320,128]{4,3,1,0,2:T(8,128)(2,1)S(1)}, bf16[2,2,2,320,128]{4,3,1,0,2:T(8,128)(2,1)S(1)}, u32[]{:S(2)}, u32[]{:S(2)}) collective-permute-start(bf16[2,2,2,320,128]{4,3,1,0,2:T(8,128)(2,1)S(1)} %copy-done.30), channel_id=1, source_target_pairs={{0,1},{1,0},{2,3},{3,2},{4,5},{5,4},{6,7},{7,6},{8,9},{9,8},{10,11... | collective-permute-start | bytes 1966088 | tf_op jit(solution)/shard_map/ppermute | solution.py:1042
  499.8 13.9 %copy-start.26 = (bf16[2,1,2,2,1,320,128]{6,5,4,3,2,1,0:T(8,128)(2,1)S(1)}, bf16[2,1,2,2,1,320,128]{6,5,4,3,2,1,0:T(8,128)(2,1)}, u32[]{:S(2)}) copy-start(bf16[2,1,2,2,1,320,128]{6,5,4,3,2,1,0:T(8,128)(2,1)} %get-tuple-element.173) | copy-start | bytes 1966084

commit v4 on v3

--- a/solution.py
+++ b/solution.py
@@ -61,9 +61,8 @@
 
 
 def rope_weight(w_key_rope):
-    rows = w_key_rope.shape[0]
-    blank = jnp.zeros((rows, HD), bf16)
-    return jnp.concatenate([blank, w_key_rope, blank[:, : LANES - HD - RD]], axis=1)
+    blank = jnp.zeros((HD, w_key_rope.shape[1]), bf16)
+    return jnp.concatenate([blank, w_key_rope, blank[: LANES - HD - RD]], axis=0)
 
 
 def prepare_kernel(tokens_ref, gain_ref, latent_ref, rope_ref, cos_ref, sin_ref, normed_ref, out_ref):
@@ -71,7 +70,7 @@
     normed = (source * rms_scale(source) * gain_ref[...].astype(f32)).astype(bf16)
     normed_ref[...] = normed
     out_ref[:, : LGROUPS * LAT] = dot_nn(normed, latent_ref[...]).astype(bf16)
-    turned = rotate_lanes(dot_nn(normed, rope_weight(rope_ref[...])), cos_ref[...], sin_ref[...])
+    turned = rotate_lanes(dot_nt(normed, rope_weight(rope_ref[...])), cos_ref[...], sin_ref[...])
     out_ref[:, LGROUPS * LAT :] = turned.astype(bf16)
 
 
@@ -92,26 +91,27 @@
     here, side_ref, query_ref, rope_ref, key_ref, value_ref, out_ref, gate_ref, up_ref, down_ref,
     near_ref, large_ref,
 ):
-    cut, units = gate_ref.shape
+    units, cut = gate_ref.shape
     blank = jnp.zeros((cut, LANES - HD - RD), bf16)
     small = key_ref.shape[0]
+    turned = rope_ref[...].T
     for e in range(here):
         lanes = slice(e * LANES, (e + 1) * LANES)
         heads, turns = slice(e * HD, (e + 1) * HD), slice(e * RD, (e + 1) * RD)
         near_ref[:cut, lanes] = jnp.concatenate(
-            [query_ref[:, heads], rope_ref[:, turns], blank], axis=1
+            [query_ref[:, heads], turned[:, turns], blank], axis=1
         )
         near_ref[cut : cut + small, lanes] = jnp.concatenate(
             [key_ref[:, heads], value_ref[:, heads]], axis=1
         )
     near_ref[cut + small :, :] = out_ref[...]
-    large_ref[:units, :] = gate_ref[...].T
-    large_ref[units : 2 * units, :] = up_ref[...].T
+    large_ref[:units, :] = gate_ref[...]
+    large_ref[units : 2 * units, :] = up_ref[...]
     large_ref[2 * units :, :] = down_ref[...]
 
 
 def pack(side, n_rows, w_query, w_query_rope, w_key_up, w_value_up, w_out, w_gate, w_up, w_down):
-    here, units = w_query.shape[1] // HD, w_gate.shape[1]
+    here, units = w_query.shape[1] // HD, w_gate.shape[0]
     cut, small = D // n_rows, LAT // n_rows
 
     def by_rows(weight):
@@ -130,12 +130,12 @@
             grid=(1,),
             in_specs=[
                 by_rows(w_query),
-                by_rows(w_query_rope),
+                by_columns(w_query_rope),
                 by_rows(w_key_up),
                 by_rows(w_value_up),
                 by_columns(w_out),
-                by_rows(w_gate),
-                by_rows(w_up),
+                by_columns(w_gate),
+                by_columns(w_up),
                 by_columns(w_down),
             ],
             out_specs=[
@@ -148,14 +148,13 @@
     )(side, w_query, w_query_rope, w_key_up, w_value_up, w_out, w_gate, w_up, w_down)
 
 
-def keys_values(groups, latent_ref, rope_ref, up_ref, rows, count):
-    rope = rope_ref[rows, :]
+def keys_values(groups, window_ref, up_of, rows, count):
+    rope = window_ref[rows, LGROUPS * LAT :]
     lane = lax.broadcasted_iota(jnp.int32, (count, LANES), 1)
     keys, values = [], []
     for e in range(0, GROUP, PAIR):
-        latent = latent_ref[rows, groups[e] * LAT : (groups[e] + 1) * LAT]
-        up = [up_ref[:, e + i].reshape(LAT, LANES) for i in range(PAIR)]
-        up = jnp.concatenate(up, axis=1)
+        latent = window_ref[rows, groups[e] * LAT : (groups[e] + 1) * LAT]
+        up = jnp.concatenate([up_of(e + i) for i in range(PAIR)], axis=1)
         wide = dot_nn(latent, up).astype(bf16)
         for i in range(PAIR):
             both = wide[:, i * LANES : (i + 1) * LANES]
@@ -174,14 +173,12 @@
 
 
 def forward_body(
-    groups, block, own, halo, ahead, meanwhile, normed_ref, weight_ref, cos_ref, sin_ref, latent_ref, rope_ref,
-    up_ref, mixed_ref, log_ref, q_ref, query_s, top_s, sum_s,
+    groups, block, own, halo, ahead, meanwhile, weight_of, up_of, normed_ref, cos_ref, sin_ref, window_ref,
+    mixed_ref, log_ref, q_ref, query_s, top_s, sum_s,
 ):
     rows = own * block
     until = halo + 1 - ahead
-    weight = jnp.concatenate(
-        [weight_ref[:, e].reshape(D, LANES) for e in range(GROUP)], axis=1
-    )
+    weight = jnp.concatenate([weight_of(e) for e in range(GROUP)], axis=1)
     raw = dot_nn(normed_ref[...], weight)
     for e in range(GROUP):
         lanes = slice(e * LANES, (e + 1) * LANES)
@@ -190,7 +187,7 @@
         q_ref[:, lanes] = query
         query_s[e] = query.T
     keys, values = keys_values(
-        groups, latent_ref, rope_ref, up_ref, slice(halo * block, (halo + own) * block), rows
+        groups, window_ref, up_of, slice(halo * block, (halo + own) * block), rows
     )
     values = [values_ones(value) for value in values]
     for j in range(own):
@@ -214,7 +211,7 @@
 
         def step(index, _):
             at = pl.ds(pl.multiple_of(index * block, block), block)
-            keys, values = keys_values(groups, latent_ref, rope_ref, up_ref, at, block)
+            keys, values = keys_values(groups, window_ref, up_of, at, block)
             values = [values_ones(value) for value in values]
             scores = [dot_nn(keys[e], query_s[e, :, :wide]) for e in range(GROUP)]
             for e in range(GROUP):
@@ -238,8 +235,13 @@
         log_ref[e] = top_s[e] + jnp.log2(sums)
 
 
-def attend_forward_kernel(groups, block, own, halo, place_ref, *refs):
-    forward_body(groups, block, own, halo, place_ref[0], lambda at: None, *refs)
+def attend_forward_kernel(groups, block, own, halo, place_ref, weight_ref, up_ref, *refs):
+    forward_body(
+        groups, block, own, halo, place_ref[0], lambda at: None,
+        lambda e: weight_ref[:, e].reshape(D, LANES),
+        lambda e: up_ref[:, e].reshape(LAT, LANES),
+        *refs,
+    )
 
 
 def attend_forward(part, groups, places, normed, near, cos, sin, window, block, own, halo):
@@ -255,23 +257,20 @@
             num_scalar_prefetch=1,
             grid=(1,),
             in_specs=[
-                whole((rows, D)),
                 pl.BlockSpec(
                     (cuts, GROUP, D // cuts, LANES),
                     shard_block(part, shards, 0),
                     pipeline_mode=once,
-                ),
-                whole((rows, LANES)),
-                whole((rows, LANES)),
-                whole((wide, LGROUPS * LAT)),
-                pl.BlockSpec(
-                    (wide, LANES), lambda g, p: (0, LGROUPS * LAT // LANES), pipeline_mode=once
                 ),
                 pl.BlockSpec(
                     (cuts, GROUP, LAT // cuts, LANES),
                     shard_block(part, shards, D // LAT),
                     pipeline_mode=once,
                 ),
+                whole((rows, D)),
+                whole((rows, LANES)),
+                whole((rows, LANES)),
+                whole((wide, LGROUPS * LAT + LANES)),
             ],
             out_specs=[
                 whole((GROUP * HD, rows)),
@@ -291,11 +290,11 @@
         ],
         compiler_params=pltpu.CompilerParams(vmem_limit_bytes=56 << 20),
         name="attend_forward",
-    )(places, normed, near, cos, sin, window, window, near)
+    )(places, near, near, normed, cos, sin, window)
 
 
 def attend_backward_kernel(
-    groups, block, own, halo, carried, place_ref, q_ref, latent_ref, rope_ref, up_ref, mixed_ref, log_ref,
+    groups, block, own, halo, carried, place_ref, q_ref, window_ref, up_ref, mixed_ref, log_ref,
     grad_ref, cos_ref, sin_ref, normed_ref, weight_ref, *refs
 ):
     before = refs[:2] if carried else None
@@ -303,6 +302,10 @@
     rows = own * block
     ahead, until = place_ref[0], place_ref[1]
     first = halo - ahead
+
+    def up_of(e):
+        return up_ref[:, e].reshape(LAT, LANES)
+
     rope_s[...] = jnp.zeros_like(rope_s)
 
     def clear(index, _):
@@ -325,7 +328,7 @@
 
     def strip(at, low, high, keep):
         cols = slice(low, high)
-        keys, values = keys_values(groups, latent_ref, rope_ref, up_ref, at, block)
+        keys, values = keys_values(groups, window_ref, up_of, at, block)
         scores = [dot_nn(keys[e], query_s[e, :, cols]) for e in range(GROUP)]
         grads = [
             dot_nn(values[e][:, HD:], grad_ref[e * HD : (e + 1) * HD, cols]) for e in range(GROUP)
@@ -379,9 +382,9 @@
         heads = [e for e in range(GROUP) if groups[e] == group]
         if heads:
             lanes = slice(heads[0] * LANES, (heads[-1] + 1) * LANES)
-            up = jnp.concatenate([up_ref[:, e].reshape(LAT, LANES) for e in heads], axis=1)
+            up = jnp.concatenate([up_of(e) for e in heads], axis=1)
             grad = dot_nt(both_s[:, lanes], up)
-            dup = dot_nn(latent_ref[:, at].T, both_s[:, lanes]).astype(bf16)
+            dup = dot_nn(window_ref[:, at].T, both_s[:, lanes]).astype(bf16)
             for q in range(cuts):
                 for i, e in enumerate(heads):
                     dnear_ref[q, e, cut:, :] = dup[
@@ -410,24 +413,26 @@
     def whole(shape):
         return pl.BlockSpec(shape, lambda g, p: (0,) * len(shape), pipeline_mode=once)
 
+    def of_part(shape):
+        return pl.BlockSpec(
+            (None,) + shape, lambda g, p: (part,) + (0,) * len(shape), pipeline_mode=once
+        )
+
     return pl.pallas_call(
         functools.partial(attend_backward_kernel, groups, block, own, halo, before is not None),
         grid_spec=pltpu.PrefetchScalarGridSpec(
             num_scalar_prefetch=1,
             grid=(1,),
             in_specs=[
-                whole((rows, GROUP * LANES)),
-                whole((wide, LGROUPS * LAT)),
-                pl.BlockSpec(
-                    (wide, LANES), lambda g, p: (0, LGROUPS * LAT // LANES), pipeline_mode=once
-                ),
+                of_part((rows, GROUP * LANES)),
+                whole((wide, lanes)),
                 pl.BlockSpec(
                     (cuts, GROUP, LAT // cuts, LANES),
                     shard_block(part, shards, D // LAT),
                     pipeline_mode=once,
                 ),
-                whole((GROUP * HD, rows)),
-                whole((GROUP, 1, rows)),
+                of_part((GROUP * HD, rows)),
+                of_part((GROUP, 1, rows)),
                 whole((GROUP * HD, rows)),
                 whole((rows, LANES)),
                 whole((rows, LANES)),
@@ -464,7 +469,7 @@
         ),
         name="attend_backward",
     )(
-        places, queries, window, window, near, mixed, logs, grad_mixed, cos, sin, normed, near,
+        places, queries, window, near, mixed, logs, grad_mixed, cos, sin, normed, near,
         *(before or ()),
     )
 
@@ -499,7 +504,7 @@
 
 
 def join(tokens, gain, mixed, out, base):
-    rows, parts = tokens.shape[0], len(mixed)
+    rows, parts = tokens.shape[0], mixed.shape[0]
 
     def whole(shape):
         return pl.BlockSpec(shape, lambda g: (0,) * len(shape), pipeline_mode=pl.Buffered(1))
@@ -508,7 +513,12 @@
         functools.partial(join_kernel, parts),
         grid=(1,),
         in_specs=[whole((rows, D)), whole((1, D))]
-        + [whole((GROUP * HD, rows))] * parts
+        + [
+            pl.BlockSpec(
+                (None, GROUP * HD, rows), lambda g, part=part: (part, 0, 0), pipeline_mode=pl.Buffered(1)
+            )
+            for part in range(parts)
+        ]
         + out_specs_of(out, base, parts),
         out_specs=[whole((rows, D)), whole((rows, D))],
         out_shape=[
@@ -517,7 +527,7 @@
         ],
         compiler_params=pltpu.CompilerParams(vmem_limit_bytes=32 << 20),
         name="join",
-    )(tokens, gain, *mixed, *([out] * parts))
+    )(tokens, gain, *([mixed] * parts), *([out] * parts))
 
 
 def norm_backward(source, gain, grad_normed):
@@ -558,7 +568,7 @@
 
 
 def middle(hidden, feed, dnormed, cotangent, token_weight, gain, mixed, out, base):
-    rows, parts = hidden.shape[0], len(mixed)
+    rows, parts = hidden.shape[0], mixed.shape[0]
     cuts, shards, _, cut = out.shape
     here = HEADS // shards
 
@@ -571,7 +581,12 @@
         grid=(1,),
         in_specs=[whole((rows, D))] * 4
         + [whole((rows, 1)), whole((1, D))]
-        + [whole((GROUP * HD, rows))] * parts
+        + [
+            pl.BlockSpec(
+                (None, GROUP * HD, rows), lambda g, part=part: (part, 0, 0), pipeline_mode=pl.Buffered(1)
+            )
+            for part in range(parts)
+        ]
         + out_specs_of(out, base, parts),
         out_specs=[whole((rows, D)), whole((rows, D)), whole(dout), whole((1, D))]
         + [whole((GROUP * HD, rows))] * parts,
@@ -584,7 +599,7 @@
         + [jax.ShapeDtypeStruct((GROUP * HD, rows), bf16)] * parts,
         compiler_params=pltpu.CompilerParams(vmem_limit_bytes=50 << 20),
         name="middle",
-    )(hidden, feed, dnormed, cotangent, token_weight, gain, *mixed, *([out] * parts))
+    )(hidden, feed, dnormed, cotangent, token_weight, gain, *([mixed] * parts), *([out] * parts))
 
 
 def finish_kernel(
@@ -606,7 +621,7 @@
     turned = jnp.where(lane < HD, 0.0, turned).astype(bf16)
     grad = grad[:, :at].astype(bf16)
     dnormed = dnormed_ref[...] + dot_nt(grad, latent_ref[...])
-    dnormed = dnormed + dot_nt(turned, rope_weight(rope_ref[...]))
+    dnormed = dnormed + dot_nn(turned, rope_weight(rope_ref[...]))
     source = tokens_ref[...].astype(f32)
     dsource, dgain_ref[...] = norm_backward(source, gain_ref[...].astype(f32), dnormed)
     dtokens_ref[...] = grad_ref[...] + dsource
@@ -682,8 +697,8 @@
 
 class Exchanges:
 
-    def __init__(self, shape, plan, target, send_sem, recv_sem):
-        self.orders, self.plan, self.target = gather_orders(shape), plan, target
+    def __init__(self, shape, plan, targets, send_sem, recv_sem):
+        self.orders, self.plan, self.targets = gather_orders(shape), plan, targets
         self.lead, self.stages = leading(shape), len(leading(shape))
         self.index = {axis: lax.axis_index(axis) for axis in ("rows", "heads")}
         self.bits = {
@@ -692,14 +707,14 @@
         self.send_sem, self.recv_sem = send_sem, recv_sem
         self.times = max(item[0] for item in plan) + self.stages
 
-    def mine(self):
-        return self.target.at[exchange_index(self.lead, (), self.bits)]
+    def mine(self, which):
+        return self.targets[which].at[exchange_index(self.lead, (), self.bits)]
 
     def copy(self, chunk, stage):
-        _, order, begin, count = self.plan[chunk]
+        _, which, order, begin, count = self.plan[chunk]
         axis, bit = self.orders[order][stage]
         held = exchange_index(self.lead, self.orders[order][:stage], self.bits)
-        piece = self.target.at[held + (pl.ds(begin, count), slice(None))]
+        piece = self.targets[which].at[held + (pl.ds(begin, count), slice(None))]
         return pltpu.make_async_remote_copy(
             src_ref=piece,
             dst_ref=piece,
@@ -718,202 +733,199 @@
                 self.copy(chunk, stage).start()
 
 
-def exchange_plan(rows, cuts):
+def exchange_plan(delay, which, first, rows, cuts):
     units, total, passed, plan = rows // 16, cuts * sum(SHARES), 0, []
     for i in range(cuts):
         for order, share in enumerate(SHARES):
             begin = 16 * (units * passed // total)
             passed += share
-            plan.append((i, order, begin, 16 * (units * passed // total) - begin))
+            count = 16 * (units * passed // total) - begin
+            plan.append((delay + i, which, order, first + begin, count))
     return plan
 
 
-def gather_kernel(
-    shape, plan, block, own, halo, latent_ref, near_ref, window_ref, near_all,
-    zero_s, local_sem, halo_send, halo_recv, send_sem, recv_sem,
+def attend_gather_kernel(
+    shape, plan, ready, groups, block, own, halo, normed_ref, cos_ref, sin_ref, latent_ref, near_ref, large_ref,
+    mixed_ref, log_ref, q_ref, near_all, large_all, window_ref, query_s, top_s, sum_s, window_s, weight_s, up_s,
+    local_sem, halo_send, halo_recv, send_sem, recv_sem,
 ):
+    part, parts = pl.program_id(0), HEADS // GROUP
     head = lax.axis_index("heads")
-    exchanges = Exchanges(shape, plan, near_all, send_sem, recv_sem)
-    zero_s[...] = jnp.zeros_like(zero_s)
-    local = [
-        pltpu.make_async_copy(near_ref, exchanges.mine(), local_sem.at[0]),
+    exchanges = Exchanges(shape, plan, (near_all, large_all), send_sem, recv_sem)
+    ahead = lax.rem(head * own, halo + 1)
+
+    def latent_copies():
+        for k in range(1, halo + 1):
+            back = -(-k // own)
+            at = halo + own - 1 - (k - 1) % own
+            copy = pltpu.make_async_remote_copy(
+                src_ref=window_s.at[pl.ds(at * block, block), :],
+                dst_ref=window_s.at[pl.ds((halo - k) * block, block), :],
+                send_sem=halo_send.at[k - 1],
+                recv_sem=halo_recv.at[k - 1],
+                device_id={"heads": lax.rem(head + back, shape["heads"])},
+                device_id_type=pl.DeviceIdType.MESH,
+            )
+            there = lax.rem((head + back) * own, halo + 1)
+            yield k, copy, (head + back < shape["heads"]) & (there >= k)
+
+    keep_window = pltpu.make_async_copy(window_s, window_ref, local_sem.at[2])
+
+    @pl.when(part == 0)
+    def _():
+        local = [
+            pltpu.make_async_copy(near_ref, exchanges.mine(0), local_sem.at[0]),
+            pltpu.make_async_copy(large_ref, exchanges.mine(1), local_sem.at[1]),
+        ]
+        for copy in local:
+            copy.start()
+        window_s[halo * block :, :] = latent_ref[...]
+        for k in range(1, halo + 1):
+
+            @pl.when(ahead < k)
+            def _():
+                blank = jnp.zeros((block, window_s.shape[1]), bf16)
+                window_s[(halo - k) * block : (halo - k + 1) * block, :] = blank
+
+        start_barrier(shape)
+        for copy in local:
+            copy.wait()
+        for time in range(ready + 1):
+            exchanges.run(time)
+            if time == 0:
+                for _, copy, goes in latent_copies():
+
+                    @pl.when(goes)
+                    def _():
+                        copy.start()
+
+        for k, copy, goes in latent_copies():
+
+            @pl.when(goes)
+            def _():
+                copy.wait_send()
+
+            @pl.when(ahead >= k)
+            def _():
+                copy.wait_recv()
+
+        keep_window.start()
+
+    lead = exchanges.lead
+    everything = exchange_index(lead, lead, exchanges.bits)
+    cut = weight_s.shape[-2]
+    lanes = pl.ds(pl.multiple_of(part * LANES, LANES), LANES)
+    loads = [
         pltpu.make_async_copy(
-            latent_ref, window_ref.at[pl.ds(halo * block, own * block), :], local_sem.at[1]
+            near_all.at[everything + (pl.ds(0, cut), lanes)], weight_s, local_sem.at[3]
+        ),
+        pltpu.make_async_copy(
+            near_all.at[everything + (pl.ds(cut, up_s.shape[-2]), lanes)], up_s, local_sem.at[4]
         ),
     ]
-    for copy in local:
+    for copy in loads:
         copy.start()
-    start_barrier(shape)
-
-    ahead = lax.rem(head * own, halo + 1)
-    passed = []
-    for k in range(1, halo + 1):
-        back = -(-k // own)
-        at = own - 1 - (k - 1) % own
-        there = lax.rem(head + back, shape["heads"])
-        copy = pltpu.make_async_remote_copy(
-            src_ref=latent_ref.at[pl.ds(at * block, block), :],
-            dst_ref=window_ref.at[pl.ds((halo - k) * block, block), :],
-            send_sem=halo_send.at[k - 1],
-            recv_sem=halo_recv.at[k - 1],
-            device_id={"heads": there},
-            device_id_type=pl.DeviceIdType.MESH,
-        )
-        blank = pltpu.make_async_copy(
-            zero_s, window_ref.at[pl.ds((halo - k) * block, block), :], local_sem.at[2 + k]
-        )
-        goes = (head + back < shape["heads"]) & (lax.rem((head + back) * own, halo + 1) >= k)
-        passed.append((copy, blank, goes, ahead >= k))
-
-    for copy, blank, goes, comes in passed:
-
-        @pl.when(goes)
-        def _():
-            copy.start()
-
-        @pl.when(jnp.logical_not(comes))
-        def _():
-            blank.start()
-
-    for copy in local:
+    for copy in loads:
         copy.wait()
-    for time in range(exchanges.times + 1):
-        exchanges.run(time)
-    for copy, blank, goes, comes in passed:
-
-        @pl.when(goes)
-        def _():
-            copy.wait_send()
-
-        @pl.when(comes)
-        def _():
-            copy.wait_recv()
-
-        @pl.when(jnp.logical_not(comes))
-        def _():
-            blank.wait()
-
-
-def gather_near(shape, latent, near, block, own, halo):
-    plan = exchange_plan(near.shape[0], 1)
+
+    def of_shard(ref, rows):
+        count = bits_of(shape["rows"])
+
+        def get(e):
+            bits = [(e >> bit) & 1 for axis, bit in lead if axis == "heads"]
+            return ref[(slice(None),) * count + tuple(bits)].reshape(rows, LANES)
+
+        return get
+
+    def meanwhile(at):
+        for p in range(parts):
+            time = ready + 1 + 2 * p + at
+
+            @pl.when(part == p)
+            def _():
+                exchanges.run(time)
+
+    forward_body(
+        groups, block, own, halo, ahead, meanwhile, of_shard(weight_s, D), of_shard(up_s, LAT),
+        normed_ref, cos_ref, sin_ref, window_s, mixed_ref, log_ref, q_ref, query_s, top_s, sum_s,
+    )
+
+    @pl.when(part == parts - 1)
+    def _():
+        for time in range(ready + 1 + 2 * parts, exchanges.times + 1):
+            exchanges.run(time)
+        keep_window.wait()
+
+
+def attend_gather(shape, groups, normed, latent, near, large, cos, sin, block, own, halo):
+    rows, wide = own * block, (halo + own) * block
+    cut, small = D // shape["rows"], LAT // shape["rows"]
+    once = pl.Buffered(1)
+    first = cut + small
+    plan = exchange_plan(0, 0, 0, first, 2)
+    ready = max(item[0] for item in plan) + len(leading(shape))
+    plan = plan + exchange_plan(2, 1, 0, large.shape[0], CHUNKS)
+    plan = plan + exchange_plan(1 + CHUNKS, 0, first, near.shape[0] - first, 1)
     count = len(plan) * len(leading(shape))
+    twos = (2,) * len(leading(shape))
     anywhere = pl.BlockSpec(memory_space=pl.ANY)
     outside = pl.BlockSpec(memory_space=pltpu.HBM)
-    window, near_all = pl.pallas_call(
-        functools.partial(gather_kernel, shape, plan, block, own, halo),
-        in_specs=[anywhere] * 2,
-        out_specs=[outside] * 2,
+
+    def whole(shape):
+        return pl.BlockSpec(shape, lambda g: (0,) * len(shape), pipeline_mode=once)
+
+    mixed, logs, queries, near_all, large_all, window = pl.pallas_call(
+        functools.partial(attend_gather_kernel, shape, plan, ready, groups, block, own, halo),
+        grid=(HEADS // GROUP,),
+        in_specs=[
+            whole((rows, D)),
+            whole((rows, LANES)),
+            whole((rows, LANES)),
+            whole(latent.shape),
+            anywhere,
+            anywhere,
+        ],
+        out_specs=[
+            pl.BlockSpec((None, GROUP * HD, rows), lambda g: (g, 0, 0)),
+            pl.BlockSpec((None, GROUP, 1, rows), lambda g: (g, 0, 0, 0)),
+            pl.BlockSpec((None, rows, GROUP * LANES), lambda g: (g, 0, 0)),
+            outside,
+            outside,
+            outside,
+        ],
         out_shape=[
-            jax.ShapeDtypeStruct(((halo + own) * block, latent.shape[1]), bf16),
-            jax.ShapeDtypeStruct((2,) * len(leading(shape)) + near.shape, bf16),
+            jax.ShapeDtypeStruct((HEADS // GROUP, GROUP * HD, rows), bf16),
+            jax.ShapeDtypeStruct((HEADS // GROUP, GROUP, 1, rows), f32),
+            jax.ShapeDtypeStruct((HEADS // GROUP, rows, GROUP * LANES), bf16),
+            jax.ShapeDtypeStruct(twos + near.shape, bf16),
+            jax.ShapeDtypeStruct(twos + large.shape, bf16),
+            jax.ShapeDtypeStruct((wide, latent.shape[1]), bf16),
         ],
         scratch_shapes=[
-            pltpu.VMEM((block, latent.shape[1]), bf16),
-            pltpu.SemaphoreType.DMA((3 + halo,)),
+            pltpu.VMEM((GROUP, LANES, rows), bf16),
+            pltpu.VMEM((GROUP, 1, rows), f32),
+            pltpu.VMEM((GROUP, TALL, rows), f32),
+            pltpu.VMEM((wide, latent.shape[1]), bf16),
+            pltpu.VMEM(twos + (cut, LANES), bf16),
+            pltpu.VMEM(twos + (small, LANES), bf16),
+            pltpu.SemaphoreType.DMA((5,)),
             pltpu.SemaphoreType.DMA((halo,)),
             pltpu.SemaphoreType.DMA((halo,)),
             pltpu.SemaphoreType.DMA((count,)),
             pltpu.SemaphoreType.DMA((count,)),
         ],
         compiler_params=pltpu.CompilerParams(
-            collective_id=0, has_side_effects=True, vmem_limit_bytes=16 << 20
-        ),
-        name="gather_near",
-    )(latent, near)
-    return window, near_all.reshape((shape["rows"], shape["heads"]) + near.shape)
-
-
-def attend_gather_kernel(
-    shape, plan, groups, block, own, halo, normed_ref, weight_ref, cos_ref, sin_ref, latent_ref, rope_ref,
-    up_ref, large_ref, mixed_ref, log_ref, q_ref, large_all, query_s, top_s, sum_s, local_sem, send_sem, recv_sem,
-):
-    part, parts = pl.program_id(0), HEADS // GROUP
-    exchanges = Exchanges(shape, plan, large_all, send_sem, recv_sem)
-
-    @pl.when(part == 0)
-    def _():
-        copy = pltpu.make_async_copy(large_ref, exchanges.mine(), local_sem.at[0])
-        copy.start()
-        start_barrier(shape)
-        copy.wait()
-        exchanges.run(0)
-
-    def meanwhile(at):
-        for p in range(parts):
-            time = 1 + 2 * p + at
-
-            @pl.when(part == p)
-            def _():
-                exchanges.run(time)
-
-    ahead = lax.rem(lax.axis_index("heads") * own, halo + 1)
-    forward_body(
-        groups, block, own, halo, ahead, meanwhile, normed_ref, weight_ref, cos_ref, sin_ref, latent_ref,
-        rope_ref, up_ref, mixed_ref, log_ref, q_ref, query_s, top_s, sum_s,
-    )
-
-    @pl.when(part == parts - 1)
-    def _():
-        for time in range(1 + 2 * parts, exchanges.times + 1):
-            exchanges.run(time)
-
-
-def attend_gather(shape, groups, normed, near, cos, sin, window, large, block, own, halo):
-    rows, wide = own * block, (halo + own) * block
-    cuts, shards, once = near.shape[0], near.shape[1], pl.Buffered(1)
-    plan = exchange_plan(large.shape[0], CHUNKS)
-    count = len(plan) * len(leading(shape))
-
-    def whole(shape):
-        return pl.BlockSpec(shape, lambda g: (0,) * len(shape), pipeline_mode=once)
-
-    def heads_block(rows_at):
-        return lambda g: (0, g * GROUP % shards // GROUP, rows_at, g * GROUP // shards)
-
-    mixed, logs, queries, large_all = pl.pallas_call(
-        functools.partial(attend_gather_kernel, shape, plan, groups, block, own, halo),
-        grid=(HEADS // GROUP,),
-        in_specs=[
-            whole((rows, D)),
-            pl.BlockSpec((cuts, GROUP, D // cuts, LANES), heads_block(0)),
-            whole((rows, LANES)),
-            whole((rows, LANES)),
-            whole((wide, LGROUPS * LAT)),
-            pl.BlockSpec((wide, LANES), lambda g: (0, LGROUPS * LAT // LANES), pipeline_mode=once),
-            pl.BlockSpec((cuts, GROUP, LAT // cuts, LANES), heads_block(D // LAT)),
-            pl.BlockSpec(memory_space=pl.ANY),
-        ],
-        out_specs=[
-            pl.BlockSpec((None, GROUP * HD, rows), lambda g: (g, 0, 0)),
-            pl.BlockSpec((None, GROUP, 1, rows), lambda g: (g, 0, 0, 0)),
-            pl.BlockSpec((None, rows, GROUP * LANES), lambda g: (g, 0, 0)),
-            pl.BlockSpec(memory_space=pltpu.HBM),
-        ],
-        out_shape=[
-            jax.ShapeDtypeStruct((HEADS // GROUP, GROUP * HD, rows), bf16),
-            jax.ShapeDtypeStruct((HEADS // GROUP, GROUP, 1, rows), f32),
-            jax.ShapeDtypeStruct((HEADS // GROUP, rows, GROUP * LANES), bf16),
-            jax.ShapeDtypeStruct((2,) * len(leading(shape)) + large.shape, bf16),
-        ],
-        scratch_shapes=[
-            pltpu.VMEM((GROUP, LANES, rows), bf16),
-            pltpu.VMEM((GROUP, 1, rows), f32),
-            pltpu.VMEM((GROUP, TALL, rows), f32),
-            pltpu.SemaphoreType.DMA((1,)),
-            pltpu.SemaphoreType.DMA((count,)),
-            pltpu.SemaphoreType.DMA((count,)),
-        ],
-        compiler_params=pltpu.CompilerParams(
-            collective_id=2, has_side_effects=True, vmem_limit_bytes=60 << 20
+            collective_id=0, has_side_effects=True, vmem_limit_bytes=60 << 20
         ),
         name="attend_gather",
-    )(normed, near, cos, sin, window, window, near, large)
-    large_all = large_all.reshape((shape["rows"], shape["heads"]) + large.shape)
-    return [(mixed[p], logs[p], queries[p]) for p in range(HEADS // GROUP)], large_all
+    )(normed, cos, sin, latent, near, large)
+    full = (shape["rows"], shape["heads"])
+    return (mixed, logs, queries), near_all.reshape(full + near.shape), large_all.reshape(full + large.shape), window
 
 
 def feed_kernel(
-    cuts, shards, units, side_ref, normed_ref, grad_ref, weight_ref, out_ref, dnormed_ref, kept_ref, sent_ref
+    cuts, shards, units, side_ref, normed_ref, cotangent_ref, token_ref, weight_ref, out_ref, dnormed_ref,
+    kept_ref, sent_ref,
 ):
     def whole(which):
         return jnp.concatenate(
@@ -946,7 +958,7 @@
         dnormed_ref[...] = jnp.zeros_like(dnormed_ref)
 
     normed = normed_ref[...]
-    grad = grad_ref[...]
+    grad = (cotangent_ref[...].astype(f32) * token_ref[...]).astype(bf16)
     w_gate, w_up, w_down = whole(0), whole(1), whole(2)
     gate = dot_nt(w_gate, normed)
     upper = dot_nt(w_up, normed)
@@ -964,7 +976,7 @@
     put(2, dot_nn(inner, grad))
 
 
-def feed_forward_both(side, normed, grad, weights, units):
+def feed_forward_both(side, normed, cotangent, token_weight, weights, units):
     rows = normed.shape[0]
     cuts, pieces, _, wide = weights.shape
     shards = max(1, min(pieces, 704 // units))
@@ -979,6 +991,7 @@
             in_specs=[
                 whole,
                 whole,
+                pl.BlockSpec((rows, 1), lambda f, s: (0, 0), pipeline_mode=once),
                 pl.BlockSpec((cuts, shards, 3 * units, wide), lambda f, s: (0, f, 0, 0)),
             ],
             out_specs=[
@@ -999,7 +1012,7 @@
             flops=40 * 10**9, bytes_accessed=50 * 10**6, transcendentals=0
         ),
         name="feed_forward_both",
-    )(side, normed, grad, weights)
+    )(side, normed, cotangent, token_weight, weights)
 
 
 def scatter_orders(shape):
@@ -1024,6 +1037,13 @@
             return terms[0]
         return sum(t.astype(f32) for t in terms).astype(bf16)
 
+    def view(self):
+        at = self.lead.index(self.order[0])
+        before, after = 2**at, 2 ** (len(self.lead) - 1 - at)
+        return before, after, [
+            t.reshape((before, 2, after) + t.shape[len(self.lead) :]) for t in self.terms
+        ]
+
     def halves(self):
         axis, bit = self.order[0]
         at = self.lead.index((axis, bit))
@@ -1048,8 +1068,52 @@
         return array.reshape((2 ** len(perm),) + array.shape[len(perm) :])
 
 
-def step_all(scatters, tied):
-    halves = [scatter.halves() for scatter in scatters]
+def fold_kernel(counts, side_ref, *refs):
+    refs = list(refs)
+    ins = [[refs.pop(0) for _ in range(2 * count)] for count in counts]
+    for terms in ins:
+        half = len(terms) // 2
+        for part in (terms[:half], terms[half:]):
+            total = part[0][...].astype(f32)
+            for term in part[1:]:
+                total = total + term[...].astype(f32)
+            refs.pop(0)[...] = total.astype(bf16)
+
+
+def fold(scatters, blocks):
+    sides = jnp.stack([upper_bit(*scatter.order[0]) for scatter in scatters]).astype(jnp.int32)
+    ins, in_specs, out_specs, out_shape, steps = [], [], [], [], None
+    for i, (scatter, (row_block, rows)) in enumerate(zip(scatters, blocks)):
+        before, after, terms = scatter.view()
+        steps = before * after
+        columns = terms[0].shape[4]
+        for other in (0, 1):
+            spec = pl.BlockSpec(
+                (None, None, None, rows, columns),
+                lambda g, s, i=i, after=after, other=other, row_block=row_block: (
+                    g // after, s[i] * (1 - 2 * other) + other, g % after, row_block, 0
+                ),
+            )
+            in_specs += [spec] * len(terms)
+            ins += terms
+            out_specs.append(pl.BlockSpec((None, rows, columns), lambda g, s: (g, 0, 0)))
+            out_shape.append(jax.ShapeDtypeStruct((steps, rows, columns), bf16))
+    outs = pl.pallas_call(
+        functools.partial(fold_kernel, [len(scatter.terms) for scatter in scatters]),
+        grid_spec=pltpu.PrefetchScalarGridSpec(
+            num_scalar_prefetch=1, grid=(steps,), in_specs=in_specs, out_specs=out_specs
+        ),
+        out_shape=out_shape,
+        name="fold",
+    )(sides, *ins)
+    twos = [(2,) * (len(scatter.lead) - 1) for scatter in scatters for _ in (0, 1)]
+    outs = [out.reshape(two + out.shape[1:]) for two, out in zip(twos, outs)]
+    return list(zip(outs[::2], outs[1::2]))
+
+
+def step_all(scatters, tied, folded=0, blocks=()):
+    halves = fold(scatters[:folded], blocks) if folded else []
+    halves = halves + [scatter.halves() for scatter in scatters[folded:]]
     sent, tied = lax.optimization_barrier(([half[1] for half in halves], tied))
     for scatter, half, out in zip(scatters, halves, sent):
         scatter.send(half[0], out)
@@ -1169,7 +1233,7 @@
     places = jnp.stack([ahead, jnp.minimum(LEN // block - ahead, own)]).astype(jnp.int32)
 
     gain_one, gain_two = gain_attn.reshape(1, D), gain_mlp.reshape(1, D)
-    normed, latent = prepare(tokens, gain_one, w_latent, w_key_rope, cos, sin)
+    normed, latent = prepare(tokens, gain_one, w_latent, w_key_rope.T, cos, sin)
 
     def halo_pairs(k):
         back = -(-k // own)
@@ -1180,9 +1244,11 @@
     if direct:
         near, large = pack(
             row_at.astype(jnp.int32).reshape(1),
-            n_rows, w_query, w_query_rope, w_key_up, w_value_up, w_out, w_gate, w_up, w_down,
+            n_rows, w_query, w_query_rope.T, w_key_up, w_value_up, w_out, w_gate.T, w_up.T, w_down,
         )
-        window, near = gather_near(shape, latent, near, block, own, halo)
+        forward, near, large, window = attend_gather(
+            shape, parts[0], normed, latent, near, large, cos, sin, block, own, halo
+        )
         out, base = near, (D + LAT) // n_rows
     else:
         pieces = []
@@ -1209,17 +1275,12 @@
         large = jnp.concatenate([w_gate.T, w_up.T, w_down], axis=0)
         large = lax.all_gather(large, "heads", axis=0).reshape(n_heads, 3 * units, 2, D // 2)
         large = large.transpose(2, 0, 1, 3)
-
-    if direct:
-        forward, large = attend_gather(
-            shape, parts[0], normed, near, cos, sin, window, large, block, own, halo
-        )
-    else:
         forward = [
             attend_forward(p, groups, places, normed, near, cos, sin, window, block, own, halo)
             for p, groups in enumerate(parts)
         ]
-    mixed = [f[0] for f in forward]
+        forward = [jnp.stack(arrays) for arrays in zip(*forward)]
+    mixed = forward[0]
     hidden, normed_mlp = join(tokens, gain_two, mixed, out, base)
 
     seq_weights = jnp.sum(
@@ -1233,11 +1294,10 @@
         * seq_weights[None, :],
         axis=1,
     )[:, None]
-    grad_low = (cotangent.astype(f32) * token_weight).astype(bf16)
     core = upper_bit("rows", 0)
     side = core if direct else jnp.zeros_like(core)
     feed_out, grad_normed_mlp, feed_kept, feed_sent = feed_forward_both(
-        side.astype(jnp.int32).reshape(1), normed_mlp, grad_low, large, units
+        side.astype(jnp.int32).reshape(1), normed_mlp, cotangent, token_weight, large, units
     )
     if not direct:
         grad_feed = jnp.concatenate([feed_kept[0], feed_sent[0]], axis=2)
@@ -1248,8 +1308,8 @@
     feed_got = lax.ppermute(feed_sent, "rows", bit_pairs(n_rows, 0))
     half_way = 3 * units // 2
     scatter_feed = [
-        Scatter(shape, 0, feed_kept[:, :, :half_way], feed_got[:, :, :half_way]),
-        Scatter(shape, 1, feed_kept[:, :, half_way:], feed_got[:, :, half_way:]),
+        Scatter(shape, 0, feed_kept, feed_got),
+        Scatter(shape, 1, feed_kept, feed_got),
     ]
     block_output, grad_hidden, grad_out, grad_gain_two, *grad_mixed = middle(
         hidden, feed_out, grad_normed_mlp, cotangent, token_weight, gain_two, mixed, out, base
@@ -1262,9 +1322,10 @@
     scatter_out = Scatter(shape, 0, grad_out)
     for p, groups in enumerate(parts):
         under_way = scatter_feed + ([scatter_out] + scatter_near if p else [])
-        grad_mixed[p] = step_all(under_way, grad_mixed[p])
+        blocks = [(0, half_way), (0 if p else 1, half_way)]
+        grad_mixed[p] = step_all(under_way, grad_mixed[p], 2, blocks)
         *before, grad_near = attend_backward(
-            p, groups, places, forward[p], normed, near, cos, sin, window, grad_mixed[p], before,
+            p, groups, places, forward, normed, near, cos, sin, window, grad_mixed[p], before,
             block, own, halo,
         )
         if by_part:
@@ -1284,7 +1345,7 @@
     ]
     grad_normed = step_all(scatter_feed + [scatter_out] + scatter_near, grad_normed)
     grad_tokens, grad_latent, grad_gain_one = finish(
-        grad_window, got, tokens, normed, grad_normed, grad_hidden, gain_one, w_latent, w_key_rope, cos, sin,
+        grad_window, got, tokens, normed, grad_normed, grad_hidden, gain_one, w_latent, w_key_rope.T, cos, sin,
         block, own, halo,
     )
     gains = jnp.concatenate([grad_gain_one, grad_gain_two], axis=0).astype(bf16)

time: 581 us -> 541 us (0.931)
  local copies, waits for them, and re-layouts: 65.2 us -> 35.4 us
  other arithmetic: 35.1 us -> 22.6 us
  Pallas kernels: 399 us -> 391 us
  waiting for transfers between devices: 55.3 us -> 62.3 us
    unnamed x86 -> x66, local copies, waits for them, and re-layouts: 28 us -> 14.2 us
    convert_element_type x15 -> x9, other arithmetic: 27.9 us -> 16.6 us  [total(): return sum((t.astype(f32) for t in terms)).astype(bf16)]
    pallas_call x2 -> x3, Pallas kernels: 204 us -> 196 us  [the longest x1 177 us: attend_gather(): pl.pallas_call(functools.partial(attend_gather_kernel, shape, plan, ready...]
    slice x2 -> x0, local copies, waits for them, and re-layouts: 7.7 us -> none  [the longest x1 3.85 us: on_device(): feed_got[:, :, half_way:]]
    dynamic_slice x8 -> x4, local copies, waits for them, and re-layouts: 10.8 us -> 4.18 us  [half(): lax.dynamic_index_in_dim(t, which, at, keepdims=False)]
    ppermute x11, waiting for transfers between devices: 19.1 us -> 25.5 us  [send(): lax.ppermute(sent, axis, bit_pairs(self.shape[axis], bit))]
  transfers between devices with their start and end apart: 19 -> 19, of which waited for: 8 -> 9; matrix products, arithmetic and copies ran while one was open for 7% -> 5% of each run, Pallas kernels for 15% -> 16%
where the time goes in v4:
time: 541 us; the launch traced here: 536 us
  Pallas kernels  391 us (72%)
  waiting for transfers between devices  62.3 us (12%)
  local copies, waits for them, and re-layouts  35.4 us (7%)
  starting transfers between devices  23.3 us (4%)
  other arithmetic  22.6 us (4%)
    pallas_call x1, Pallas kernels, attend_gather(): pl.pallas_call(functools.partial(attend_gather_kernel, shape, plan, ready...  177 us
    pallas_call x2, Pallas kernels, attend_backward(): pl.pallas_call(functools.partial(attend_backward_kernel, groups, block, o...  64.7 us
    pallas_call x1, Pallas kernels, scatter_rest(): pl.pallas_call(functools.partial(scatter_kernel, shape, orders), in_specs...  52.4 us
    pallas_call x1, Pallas kernels, feed_forward_both(): pl.pallas_call(functools.partial(feed_kernel, cuts, shards, units), grid_...  49.9 us
    ppermute x7, waiting for transfers between devices, on_device(): lax.ppermute(grad_window[(halo - k) * block:(halo - k + 1) * block], 'hea...  36.7 us
    ppermute x11, waiting for transfers between devices, send(): lax.ppermute(sent, axis, bit_pairs(self.shape[axis], bit))  25.5 us
    pallas_call x2, Pallas kernels, fold(): pl.pallas_call(functools.partial(fold_kernel, [len(scatter.terms) for sca...  18.4 us
    convert_element_type x9, other arithmetic, total(): return sum((t.astype(f32) for t in terms)).astype(bf16)  16.6 us
  transfers between devices with their start and end apart: 19, of which 9 were waited for; matrix products, arithmetic and copies ran while one was open for 5% of the time, Pallas kernels for 16%

profile of v4, /device:TPU:0, one launch (start us, length us, event | category | flops | bytes accessed | tf_op | source)
XLA Modules:
  0.0 536.2 jit_solution(8491630368851264129)
XLA Ops:
  0.7 0.8 reshape.215.gain_ref
  2.2 0.9 select_reduce_fusion.1
  3.1 0.9 broadcast_in_dim.3.token_ref.weight_ref
  4.0 1.4 multiply_sine_fusion
  5.5 1.7 copy-done.2
  7.2 0.8 copy-done.12
  8.0 1.8 prepare.1
  9.8 1.1 copy-done.4
  11.0 0.9 copy-done.11
  11.9 2.2 pack.1
  14.1 177.3 %attend_gather.1 = (bf16[2,512,768]{2,1,0:T(8,128)(2,1)}, f32[2,8,1,768]{3,2,1,0:T(1,128)}, bf16[2,768,1024]{2,1,0:T(8,128)(2,1)}, bf16[2,2,2,2,2,448,256]{6,5,4...) custom-call(bf16[768,1024]{1,0:T(8,128)(2,1)} %copy-done.4, ...), custom_call_target="tpu_custom_call" | custom-call | tf_op jit(solution)/shard_map/attend_gather/pallas_call | solution.py:877
  191.5 3.1 copy-done
  194.5 1.4 copy-done.1
  195.9 2.4 join.1
  198.4 1.7 copy-done.8
  200.0 1.1 copy-done.14
  201.2 49.9 %feed_forward_both.1 = (f32[768,1024]{1,0:T(8,128)}, f32[768,1024]{1,0:T(8,128)}, bf16[2,8,1056,256]{3,2,1,0:T(8,128)(2,1)}, bf16[2,8,1056,256]{3,2,1,0:T(8,128)(2,1)}) custom-call(s32[1]{0:T(128)} %bitcast.6.side_ref, bf16[768,1024]{1,0:T(8,128)(2,1)} %copy-done.14, bf16[768,1024]{1,0:T(8,128)(2,1)} %cotangent_ref.3, ...), custom_call_target="tpu_custom_call" | custom-call | flops 40000000000 | bytes 50000000 | tf_op jit(solution)/shard_map/feed_forward_both/pallas_call | solution.py:986
  251.4 11.0 %middle.1 = (bf16[768,1024]{1,0:T(8,128)(2,1)}, f32[768,1024]{1,0:T(8,128)}, bf16[4,8,128,256]{3,2,1,0:T(8,128)(2,1)}, f32[1,1024]{1,0:T(1,128)S(1)}, bf16[512,7...) custom-call(f32[768,1024]{1,0:T(8,128)} %copy-done.8, f32[768,1024]{1,0:T(8,128)} %get-tuple-element.83.feed_ref, ...), custom_call_target="tpu_custom_call" | custom-call | tf_op jit(solution)/shard_map/middle/pallas_call | solution.py:579
  264.1 2.3 copy_bitcast_fusion.3
  266.4 0.9 constant_dynamic-slice_fusion.2
  267.3 11.8 %fold.2 = (bf16[8,528,256]{2,1,0:T(8,128)(2,1)}, bf16[8,528,256]{2,1,0:T(8,128)(2,1)}, bf16[8,528,256]{2,1,0:T(8,128)(2,1)}, bf16[8,528,256]{2,1,0:T(8,128)(2,1)}) custom-call(s32[2]{0:T(128)} %pad_add_fusion.2.side_ref, bf16[1,2,8,1056,256]{4,3,2,1,0:T(8,128)(2,1)} %bitcast.136, bf16[1,2,8,1056,256]{4,3,2,1,0:T(8,128)(2,1)} %bitcast.14.refs_1_.refs_3_, ...), custom_call_target="tpu_custom_call" | custom-call | tf_op jit(solution)/shard_map/fold/pallas_call | solution.py:1101
  279.1 1.5 collective-permute-start.1
  280.6 3.1 collective-permute-start.2
  283.7 31.3 %attend_backward.2 = (bf16[2560,640]{1,0:T(8,128)(2,1)}, f32[768,1024]{1,0:T(8,128)}, bf16[4,8,320,128]{3,2,1,0:T(8,128)(2,1)}) custom-call(s32[2]{0:T(128)} %pad_add_fusion.place_ref, bf16[2,768,1024]{2,1,0:T(8,128)(2,1)} %get-tuple-element.86.q_ref, bf16[2560,640]{1,0:T(8,128)(2,1)} %get-tuple-element.87.window_ref, bf16[4,8,448,256]{3,2,1,0:T(8,128)(2,1)} %bitcast.124, ...), custom_call_target="tpu_custom_call" | custom-call | flops 40000000000 | bytes 30000000 | tf_op jit(solution)/shard_map/attend_backward/pallas_call | solution.py:421
  315.0 2.6 copy_bitcast_fusion.2
  317.7 10.8 %collective-permute-done.1 = bf16[2,2,2,528,256]{4,3,2,1,0:T(8,128)(2,1)} collective-permute-done((bf16[2,2,2,528,256]{4,3,2,1,0:T(8,128)(2,1)}, bf16[2,2,2,528,256]{4,3,2,1,0:T(8,128)(2,1)}, u32[]{:S(2)}, u32[]{:S(2)}) %collective-permute-start.1) | collective-permute-done | bytes 2162720 | tf_op jit(solution)/shard_map/ppermute | solution.py:1062
  328.5 2.9 collective-permute-done.2
  331.4 6.6 %fold.3 = (bf16[4,528,256]{2,1,0:T(8,128)(2,1)}, bf16[4,528,256]{2,1,0:T(8,128)(2,1)}, bf16[4,528,256]{2,1,0:T(8,128)(2,1)}, bf16[4,528,256]{2,1,0:T(8,128)(2,1)}) custom-call(s32[2]{0:T(128)} %pad_add_fusion.1.side_ref, bf16[4,2,1,528,256]{4,3,2,1,0:T(8,128)(2,1)} %bitcast.140, bf16[4,2,1,528,256]{4,3,2,1,0:T(8,128)(2,1)} %bitcast.20.refs_1_.refs_3_, ...), custom_call_target="tpu_custom_call" | custom-call | tf_op jit(solution)/shard_map/fold/pallas_call | solution.py:1101
  338.0 2.3 copy.65
  340.3 1.7 collective-permute-start.3
  342.1 5.4 %collective-permute-start.4 = (bf16[2,2,528,256]{3,2,1,0:T(8,128)(2,1)}, bf16[2,2,528,256]{3,2,1,0:T(8,128)(2,1)}, u32[]{:S(2)}, u32[]{:S(2)}) collective-permute-start(bf16[2,2,528,256]{3,2,1,0:T(8,128)(2,1)} %bitcast.24), channel_id=1, source_target_pairs={{0,2},{1,3},{2,0},{3,1},{4,6},{5,7},{6,4},{7,5},{8,10},{9,11},{10,... | collective-permute-start | bytes 3244040 | tf_op jit(solution)/shard_map/ppermute | solution.py:1062
  348.0 33.5 %attend_backward.3 = (bf16[2560,640]{1,0:T(8,128)(2,1)}, f32[768,1024]{1,0:T(8,128)}, bf16[4,8,320,128]{3,2,1,0:T(8,128)(2,1)}) custom-call(s32[2]{0:T(128)} %pad_add_fusion.place_ref, bf16[2,768,1024]{2,1,0:T(8,128)(2,1)} %get-tuple-element.86.q_ref, bf16[2560,640]{1,0:T(8,128)(2,1)} %get-tuple-element.87.window_ref, bf16[4,8,448,256]{3,2,1,0:T(8,128)(2,1)} %bitcast.126, ...), custom_call_target="tpu_custom_call" | custom-call | flops 40000000000 | bytes 30000000 | tf_op jit(solution)/shard_map/attend_backward/pallas_call | solution.py:421
  381.4 2.1 constant_dynamic-slice_fusion
  383.5 1.1 copy.106
  384.7 0.9 fusion.22
  385.6 1.4 collective-permute-start.7
  387.0 1.3 collective-permute-start.8
  388.4 2.1 fusion.6
  390.4 1.3 collective-permute-start.9
  391.7 2.0 fusion.8
  393.7 1.3 collective-permute-start.10
  395.0 2.1 fusion.7
  397.1 7.2 %collective-permute-done.7.refs_0_ = bf16[256,640]{1,0:T(8,128)(2,1)S(1)} collective-permute-done((bf16[256,640]{1,0:T(8,128)(2,1)S(1)}, bf16[256,640]{1,0:T(8,128)(2,1)S(1)}, u32[]{:S(2)}, u32[]{:S(2)}) %collective-permute-start.7) | collective-permute-done | bytes 327712 | tf_op jit(solution)/shard_map/ppermute | solution.py:1339
  404.3 1.3 collective-permute-start.11
  405.6 5.7 %collective-permute-done.8.refs_1_ = bf16[256,640]{1,0:T(8,128)(2,1)S(1)} collective-permute-done((bf16[256,640]{1,0:T(8,128)(2,1)S(1)}, bf16[256,640]{1,0:T(8,128)(2,1)S(1)}, u32[]{:S(2)}, u32[]{:S(2)}) %collective-permute-start.8) | collective-permute-done | bytes 327712 | tf_op jit(solution)/shard_map/ppermute | solution.py:1339
  411.4 1.3 collective-permute-start.12
  412.7 1.7 collective-permute-start.13
  414.4 2.1 fusion.2
  416.5 1.3 collective-permute-done.9.refs_2_
  418.3 10.4 %collective-permute-done.10.refs_3_ = bf16[256,640]{1,0:T(8,128)(2,1)S(1)} collective-permute-done((bf16[256,640]{1,0:T(8,128)(2,1)S(1)}, bf16[256,640]{1,0:T(8,128)(2,1)S(1)}, u32[]{:S(2)}, u32[]{:S(2)}) %collective-permute-start.10) | collective-permute-done | bytes 327712 | tf_op jit(solution)/shard_map/ppermute | solution.py:1339
  429.2 6.5 %collective-permute-done.11.refs_4_ = bf16[256,640]{1,0:T(8,128)(2,1)S(1)} collective-permute-done((bf16[256,640]{1,0:T(8,128)(2,1)S(1)}, bf16[256,640]{1,0:T(8,128)(2,1)S(1)}, u32[]{:S(2)}, u32[]{:S(2)}) %collective-permute-start.11) | collective-permute-done | bytes 327712 | tf_op jit(solution)/shard_map/ppermute | solution.py:1339
  436.5 5.7 %collective-permute-done.12.refs_5_ = bf16[256,640]{1,0:T(8,128)(2,1)} collective-permute-done((bf16[256,640]{1,0:T(8,128)(2,1)}, bf16[256,640]{1,0:T(8,128)(2,1)}, u32[]{:S(2)}, u32[]{:S(2)}) %collective-permute-start.12) | collective-permute-done | bytes 327712 | tf_op jit(solution)/shard_map/ppermute | solution.py:1339
  442.2 11.0 %finish.1 = (f32[768,1024]{1,0:T(8,128)}, bf16[1024,640]{1,0:T(8,128)(2,1)}, f32[1,1024]{1,0:T(1,128)}) custom-call(bf16[2560,640]{1,0:T(8,128)(2,1)} %get-tuple-element.107.dwindow_ref, bf16[768,1024]{1,0:T(8,128)(2,1)} %tokens_ref.5, bf16[768,1024]{1,0:T(8,128)(2,1)} %copy-done.4, f32[768,1024]{1,0:T(8,128)} %get-tuple-element.116.dnormed_ref, ...), custom_call_target="tpu_custom_call" | custom-call | tf_op jit(solution)/shard_map/finish/pallas_call | solution.py:636
  454.1 1.6 copy.71
  455.8 1.5 add_convert_fusion.5
  457.4 1.4 fusion.3.refs_1_
  458.7 1.4 fusion.4.refs_0_
  460.2 11.7 %collective-permute-done.17 = bf16[2,2,2,320,128]{4,3,1,0,2:T(8,128)(2,1)S(1)} collective-permute-done((bf16[2,2,2,320,128]{4,3,1,0,2:T(8,128)(2,1)S(1)}, bf16[2,2,2,320,128]{4,3,1,0,2:T(8,128)(2,1)S(1)}, u32[]{:S(2)}, u32[]{:S(2)}) %collective-permute-start.17) | collective-permute-done | bytes 655392 | tf_op jit(solution)/shard_map/ppermute | solution.py:1062
  471.9 1.3 add_convert_fusion
  473.3 2.8 fusion
  476.0 52.4 %scatter_rest.1 = (f32[528,256]{1,0:T(8,128)S(1)}, f32[528,256]{1,0:T(8,128)S(1)}, f32[128,256]{1,0:T(8,128)S(1)}, f32[32,640]{1,0:T(8,128)S(1)}, f32[16,128]{1,...) custom-call(bf16[2,528,256]{2,1,0:T(8,128)(2,1)S(1)} %fusion.4.refs_0_, ...), custom_call_target="tpu_custom_call" | custom-call | tf_op jit(solution)/shard_map/scatter_rest/pallas_call | solution.py:1180
  530.9 0.8 copy.79
  531.7 0.7 copy.78
  534.0 1.0 fusion.23
  (102 shorter events, 11.2 us)
Async XLA Ops:
  0.6 4.8 copy-start.7
  2.1 7.7 %copy-start.13 = (bf16[1,1024]{1,0:T(2,128)(2,1)}, bf16[1,1024]{1,0:T(2,128)(2,1)S(1)}, u32[]{:S(2)}) copy-start(bf16[1,1024]{1,0:T(2,128)(2,1)S(1)} %reshape.216.gain_ref) | copy-start | bytes 6148
  5.5 4.3 copy-start.5
  5.5 4.3 copy-start.6
  5.5 1.7 copy-start.2
  7.2 0.8 copy-start.12
  9.8 1.2 copy-start.4
  11.0 0.9 copy-start.11
  14.1 177.3 %copy-start.3 = (bf16[768,1024]{1,0:T(8,128)(2,1)S(1)}, bf16[768,1024]{1,0:T(8,128)(2,1)}, u32[]{:S(2)}) copy-start(bf16[768,1024]{1,0:T(8,128)(2,1)} %tokens_ref.5) | copy-start | bytes 4718596
  191.5 3.1 copy-start
  194.5 1.4 copy-start.1
  198.3 1.7 copy-start.8
  200.0 1.1 copy-start.14
  201.2 50.2 %copy-start.9 = (f32[768,1]{1,0:T(8,128)S(1)}, f32[768,1]{1,0:T(8,128)}, u32[]{:S(2)}) copy-start(f32[768,1]{1,0:T(8,128)} %broadcast_in_dim.3.token_ref.weight_ref) | copy-start | bytes 9220
  201.2 50.2 %copy-start.10 = (bf16[768,1024]{1,0:T(8,128)(2,1)S(1)}, bf16[768,1024]{1,0:T(8,128)(2,1)}, u32[]{:S(2)}) copy-start(bf16[768,1024]{1,0:T(8,128)(2,1)} %cotangent_ref.3) | copy-start | bytes 4718596
  251.0 16.3 %collective-permute-start = (bf16[2,8,1056,256]{3,2,1,0:T(8,128)(2,1)}, bf16[2,8,1056,256]{3,2,1,0:T(8,128)(2,1)}, u32[]{:S(2)}, u32[]{:S(2)}) collective-permute-start(bf16[2,8,1056,256]{3,2,1,0:T(8,128)(2,1)} %get-tuple-element.90), channel_id=1, source_target_pairs={{0,8},{8,0},{16,24},{24,16},{1,9},{9,1},{17,25},{25,17},{2,10},{10... | collective-permute-start | bytes 25952264 | tf_op jit(solution)/shard_map/ppermute | solution.py:1308
  262.4 4.9 copy-start.15
  262.4 4.9 copy-start.16
  262.4 4.0 copy-start.19
  279.1 49.5 %collective-permute-start.1 = (bf16[2,2,2,528,256]{4,3,2,1,0:T(8,128)(2,1)}, bf16[2,2,2,528,256]{4,3,2,1,0:T(8,128)(2,1)}, u32[]{:S(2)}, u32[]{:S(2)}) collective-permute-start(bf16[2,2,2,528,256]{4,3,2,1,0:T(8,128)(2,1)} %bitcast.165), channel_id=1, source_target_pairs={{0,16},{8,24},{16,0},{24,8},{1,17},{9,25},{17,1},{25,9},{2,18},{10... | collective-permute-start | bytes 6488072 | tf_op jit(solution)/shard_map/ppermute | solution.py:1062
  280.6 50.8 %collective-permute-start.2 = (bf16[2,2,2,528,256]{4,3,2,1,0:T(8,128)(2,1)}, bf16[2,2,2,528,256]{4,3,2,1,0:T(8,128)(2,1)}, u32[]{:S(2)}, u32[]{:S(2)}) collective-permute-start(bf16[2,2,2,528,256]{4,3,2,1,0:T(8,128)(2,1)} %bitcast.164), channel_id=1, source_target_pairs={{0,1},{1,0},{2,3},{3,2},{4,5},{5,4},{6,7},{7,6},{8,9},{9,8},{10,11... | collective-permute-start | bytes 6488072 | tf_op jit(solution)/shard_map/ppermute | solution.py:1062
  315.0 2.6 copy-start.18
  340.3 53.4 %collective-permute-start.3 = (bf16[2,2,528,256]{3,2,0,1:T(8,128)(2,1)}, bf16[2,2,528,256]{3,2,0,1:T(8,128)(2,1)}, u32[]{:S(2)}, u32[]{:S(2)}) collective-permute-start(bf16[2,2,528,256]{3,2,0,1:T(8,128)(2,1)} %copy.65), channel_id=1, source_target_pairs={{0,1},{1,0},{2,3},{3,2},{4,5},{5,4},{6,7},{7,6},{8,9},{9,8},{10,11... | collective-permute-start | bytes 3244040 | tf_op jit(solution)/shard_map/ppermute | solution.py:1062
  342.1 48.4 %collective-permute-start.4 = (bf16[2,2,528,256]{3,2,1,0:T(8,128)(2,1)}, bf16[2,2,528,256]{3,2,1,0:T(8,128)(2,1)}, u32[]{:S(2)}, u32[]{:S(2)}) collective-permute-start(bf16[2,2,528,256]{3,2,1,0:T(8,128)(2,1)} %bitcast.24), channel_id=1, source_target_pairs={{0,2},{1,3},{2,0},{3,1},{4,6},{5,7},{6,4},{7,5},{8,10},{9,11},{10,... | collective-permute-start | bytes 3244040 | tf_op jit(solution)/shard_map/ppermute | solution.py:1062
  347.5 39.6 %collective-permute-start.5 = (bf16[2,2,2,2,128,256]{5,4,1,2,3,0:T(8,128)(2,1)}, bf16[2,2,2,2,128,256]{5,4,1,2,3,0:T(8,128)(2,1)}, u32[]{:S(2)}, u32[]{:S(2)}) collective-permute-start(bf16[2,2,2,2,128,256]{5,4,1,2,3,0:T(8,128)(2,1)} %copy_bitcast_fusion.3), channel_id=1, source_target_pairs={{0,8},{8,0},{16,24},{24,16},{1,9},{9,1},{17,25},{25,17},{2,10},{10... | collective-permute-start | bytes 3145736 | tf_op jit(solution)/shard_map/ppermute | solution.py:1062
  347.5 65.2 %collective-permute-start.6 = (bf16[2,2,2,2,320,128]{5,4,1,0,2,3:T(8,128)(2,1)}, bf16[2,2,2,2,320,128]{5,4,1,0,2,3:T(8,128)(2,1)}, u32[]{:S(2)}, u32[]{:S(2)}) collective-permute-start(bf16[2,2,2,2,320,128]{5,4,1,0,2,3:T(8,128)(2,1)} %copy_bitcast_fusion.2), channel_id=1, source_target_pairs={{0,8},{8,0},{16,24},{24,16},{1,9},{9,1},{17,25},{25,17},{2,10},{10... | collective-permute-start | bytes 3932168 | tf_op jit(solution)/shard_map/ppermute | solution.py:1062
  381.4 3.2 copy-start.17
  384.7 3.7 copy-start.20
  385.6 6.1 %copy-start.23 = (bf16[4,528,256]{2,1,0:T(8,128)(2,1)S(1)}, bf16[4,528,256]{2,1,0:T(8,128)(2,1)}, u32[]{:S(2)}) copy-start(bf16[4,528,256]{2,1,0:T(8,128)(2,1)} %get-tuple-element.110) | copy-start | bytes 3244036
  385.6 18.7 %collective-permute-start.7 = (bf16[256,640]{1,0:T(8,128)(2,1)S(1)}, bf16[256,640]{1,0:T(8,128)(2,1)S(1)}, u32[]{:S(2)}, u32[]{:S(2)}) collective-permute-start(bf16[256,640]{1,0:T(8,128)(2,1)S(1)} %get-tuple-element.168), channel_id=1, source_target_pairs={{1,0},{2,1},{3,2},{4,3},{5,4},{6,5},{7,6},{9,8},{10,9},{11,10},{12... | collective-permute-start | bytes 983048 | tf_op jit(solution)/shard_map/ppermute | solution.py:1339
  387.0 24.3 %collective-permute-start.8 = (bf16[256,640]{1,0:T(8,128)(2,1)S(1)}, bf16[256,640]{1,0:T(8,128)(2,1)S(1)}, u32[]{:S(2)}, u32[]{:S(2)}) collective-permute-start(bf16[256,640]{1,0:T(8,128)(2,1)S(1)} %get-tuple-element.167), channel_id=1, source_target_pairs={{1,0},{2,1},{4,3},{5,4},{6,5},{7,6},{9,8},{10,9},{12,11},{13,12},{... | collective-permute-start | bytes 983048 | tf_op jit(solution)/shard_map/ppermute | solution.py:1339
  388.3 6.7 %copy-start.21 = (bf16[4,528,256]{2,1,0:T(8,128)(2,1)S(1)}, bf16[4,528,256]{2,1,0:T(8,128)(2,1)}, u32[]{:S(2)}) copy-start(bf16[4,528,256]{2,1,0:T(8,128)(2,1)} %get-tuple-element.108) | copy-start | bytes 3244036
  390.4 27.3 %collective-permute-start.9 = (bf16[256,640]{1,0:T(8,128)(2,1)S(1)}, bf16[256,640]{1,0:T(8,128)(2,1)S(1)}, u32[]{:S(2)}, u32[]{:S(2)}) collective-permute-start(bf16[256,640]{1,0:T(8,128)(2,1)S(1)} %get-tuple-element.166), channel_id=1, source_target_pairs={{1,0},{2,1},{4,3},{5,4},{7,6},{9,8},{10,9},{12,11},{13,12},{15,14}... | collective-permute-start | bytes 983048 | tf_op jit(solution)/shard_map/ppermute | solution.py:1339
  393.7 34.9 %collective-permute-start.10 = (bf16[256,640]{1,0:T(8,128)(2,1)S(1)}, bf16[256,640]{1,0:T(8,128)(2,1)S(1)}, u32[]{:S(2)}, u32[]{:S(2)}) collective-permute-start(bf16[256,640]{1,0:T(8,128)(2,1)S(1)} %get-tuple-element.165), channel_id=1, source_target_pairs={{2,0},{4,2},{5,3},{7,5},{10,8},{12,10},{13,11},{15,13},{18,16},{20... | collective-permute-start | bytes 983048 | tf_op jit(solution)/shard_map/ppermute | solution.py:1339
  404.3 31.3 %copy-start.26 = (bf16[256,640]{1,0:T(8,128)(2,1)}, bf16[256,640]{1,0:T(8,128)(2,1)S(1)}, u32[]{:S(2)}) copy-start(bf16[256,640]{1,0:T(8,128)(2,1)S(1)} %collective-permute-done.7.refs_0_) | copy-start | bytes 983044
  404.3 31.3 %collective-permute-start.11 = (bf16[256,640]{1,0:T(8,128)(2,1)S(1)}, bf16[256,640]{1,0:T(8,128)(2,1)S(1)}, u32[]{:S(2)}, u32[]{:S(2)}) collective-permute-start(bf16[256,640]{1,0:T(8,128)(2,1)S(1)} %get-tuple-element.164), channel_id=1, source_target_pairs={{2,0},{5,3},{7,5},{10,8},{13,11},{15,13},{18,16},{21,19},{23,21},{... | collective-permute-start | bytes 983048 | tf_op jit(solution)/shard_map/ppermute | solution.py:1339
  411.4 24.3 %copy-start.27 = (bf16[256,640]{1,0:T(8,128)(2,1)}, bf16[256,640]{1,0:T(8,128)(2,1)S(1)}, u32[]{:S(2)}) copy-start(bf16[256,640]{1,0:T(8,128)(2,1)S(1)} %collective-permute-done.8.refs_1_) | copy-start | bytes 983044
  411.4 30.8 %collective-permute-start.12 = (bf16[256,640]{1,0:T(8,128)(2,1)}, bf16[256,640]{1,0:T(8,128)(2,1)}, u32[]{:S(2)}, u32[]{:S(2)}) collective-permute-start(bf16[256,640]{1,0:T(8,128)(2,1)} %get-tuple-element.163), channel_id=1, source_target_pairs={{2,0},{5,3},{10,8},{13,11},{18,16},{21,19},{26,24},{29,27}} | collective-permute-start | bytes 983048 | tf_op jit(solution)/shard_map/ppermute | solution.py:1339
  412.7 29.5 %collective-permute-start.13 = (bf16[256,640]{1,0:T(8,128)(2,1)S(1)}, bf16[256,640]{1,0:T(8,128)(2,1)}, u32[]{:S(2)}, u32[]{:S(2)}) collective-permute-start(bf16[256,640]{1,0:T(8,128)(2,1)S(1)} %get-tuple-element.162), channel_id=1, source_target_pairs={{5,2},{13,10},{21,18},{29,26}} | collective-permute-start | bytes 983048 | tf_op jit(solution)/shard_map/ppermute | solution.py:1339
  417.7 18.0 %copy-start.28 = (bf16[256,640]{1,0:T(8,128)(2,1)}, bf16[256,640]{1,0:T(8,128)(2,1)S(1)}, u32[]{:S(2)}) copy-start(bf16[256,640]{1,0:T(8,128)(2,1)S(1)} %collective-permute-done.9.refs_2_) | copy-start | bytes 983044
  417.7 38.1 %collective-permute-start.16 = (bf16[2,2,2,128,256]{4,3,0,1,2:T(8,128)(2,1)}, bf16[2,2,2,128,256]{4,3,0,1,2:T(8,128)(2,1)}, u32[]{:S(2)}, u32[]{:S(2)}) collective-permute-start(bf16[2,2,2,128,256]{4,3,0,1,2:T(8,128)(2,1)} %fusion.6), channel_id=1, source_target_pairs={{0,16},{8,24},{16,0},{24,8},{1,17},{9,25},{17,1},{25,9},{2,18},{10... | collective-permute-start | bytes 1572872 | tf_op jit(solution)/shard_map/ppermute | solution.py:1062
  428.7 7.1 %copy-start.29 = (bf16[256,640]{1,0:T(8,128)(2,1)}, bf16[256,640]{1,0:T(8,128)(2,1)S(1)}, u32[]{:S(2)}) copy-start(bf16[256,640]{1,0:T(8,128)(2,1)S(1)} %collective-permute-done.10.refs_3_) | copy-start | bytes 983044
  428.7 28.7 %collective-permute-start.15 = (bf16[2,528,256]{2,1,0:T(8,128)(2,1)}, bf16[2,528,256]{2,1,0:T(8,128)(2,1)S(1)}, u32[]{:S(2)}, u32[]{:S(2)}) collective-permute-start(bf16[2,528,256]{2,1,0:T(8,128)(2,1)} %fusion.8), channel_id=1, source_target_pairs={{0,16},{8,24},{16,0},{24,8},{1,17},{9,25},{17,1},{25,9},{2,18},{10... | collective-permute-start | bytes 1622024 | tf_op jit(solution)/shard_map/ppermute | solution.py:1062
  435.7 0.7 copy-start.30
  435.7 37.6 %collective-permute-start.18 = (bf16[2,2,2,2,320,128]{5,4,1,0,2,3:T(8,128)(2,1)}, bf16[2,2,2,2,320,128]{5,4,1,0,2,3:T(8,128)(2,1)}, u32[]{:S(2)}, u32[]{:S(2)}) collective-permute-start(bf16[2,2,2,2,320,128]{5,4,1,0,2,3:T(8,128)(2,1)} %bitcast.120), channel_id=1, source_target_pairs={{0,8},{8,0},{16,24},{24,16},{1,9},{9,1},{17,25},{25,17},{2,10},{10... | collective-permute-start | bytes 3932168 | tf_op jit(solution)/shard_map/ppermute | solution.py:1062
  442.2 16.6 %collective-permute-start.14 = (bf16[2,528,256]{2,1,0:T(8,128)(2,1)}, bf16[2,528,256]{2,1,0:T(8,128)(2,1)}, u32[]{:S(2)}, u32[]{:S(2)}) collective-permute-start(bf16[2,528,256]{2,1,0:T(8,128)(2,1)} %fusion.7), channel_id=1, source_target_pairs={{0,2},{1,3},{2,0},{3,1},{4,6},{5,7},{6,4},{7,5},{8,10},{9,11},{10,... | collective-permute-start | bytes 1622024 | tf_op jit(solution)/shard_map/ppermute | solution.py:1062
  454.1 1.7 copy-start.25
  455.7 1.7 copy-start.24
  455.7 16.2 %collective-permute-start.17 = (bf16[2,2,2,320,128]{4,3,1,0,2:T(8,128)(2,1)S(1)}, bf16[2,2,2,320,128]{4,3,1,0,2:T(8,128)(2,1)S(1)}, u32[]{:S(2)}, u32[]{:S(2)}) collective-permute-start(bf16[2,2,2,320,128]{4,3,1,0,2:T(8,128)(2,1)S(1)} %copy-done.25), channel_id=1, source_target_pairs={{0,1},{1,0},{2,3},{3,2},{4,5},{5,4},{6,7},{7,6},{8,9},{9,8},{10,11... | collective-permute-start | bytes 1966088 | tf_op jit(solution)/shard_map/ppermute | solution.py:1062
  457.3 1.4 copy-start.22

commit v5 on v4

--- a/solution.py
+++ b/solution.py
@@ -1343,7 +1343,8 @@
         )
         for k in range(1, halo + 1)
     ]
-    grad_normed = step_all(scatter_feed + [scatter_out] + scatter_near, grad_normed)
+    early = scatter_near[:-1] if by_part else scatter_near
+    grad_normed = step_all(scatter_feed + [scatter_out] + early, grad_normed)
     grad_tokens, grad_latent, grad_gain_one = finish(
         grad_window, got, tokens, normed, grad_normed, grad_hidden, gain_one, w_latent, w_key_rope.T, cos, sin,
         block, own, halo,

time: 541 us -> 547 us (1.011)
  Pallas kernels: 391 us -> 401 us
    pallas_call x1, Pallas kernels: 52.4 us -> 62.4 us  [scatter_rest(): pl.pallas_call(functools.partial(scatter_kernel, shape, orders), in_specs...]
    convert_element_type x9 -> x8, other arithmetic: 16.6 us -> 14.1 us  [total(): return sum((t.astype(f32) for t in terms)).astype(bf16)]
    ppermute x11 -> x10, waiting for transfers between devices: 25.5 us -> 23.9 us  [send(): lax.ppermute(sent, axis, bit_pairs(self.shape[axis], bit))]
    unnamed x66 -> x70, local copies, waits for them, and re-layouts: 14.2 us -> 14.4 us
    ppermute x11 -> x10, starting transfers between devices: 13.4 us -> 13.4 us  [send(): lax.ppermute(sent, axis, bit_pairs(self.shape[axis], bit))]
  transfers between devices with their start and end apart: 19 -> 18, of which waited for: 9 -> 9; matrix products, arithmetic and copies ran while one was open for 5% -> 5% of each run, Pallas kernels for 16% -> 16%
where the time goes in v5:
time: 547 us; the launch traced here: 542 us
  Pallas kernels  401 us (73%)
  waiting for transfers between devices  59.6 us (11%)
  local copies, waits for them, and re-layouts  36.8 us (7%)
  starting transfers between devices  23.3 us (4%)
  other arithmetic  20 us (4%)
    pallas_call x1, Pallas kernels, attend_gather(): pl.pallas_call(functools.partial(attend_gather_kernel, shape, plan, ready...  177 us
    pallas_call x2, Pallas kernels, attend_backward(): pl.pallas_call(functools.partial(attend_backward_kernel, groups, block, o...  64.6 us
    pallas_call x1, Pallas kernels, scatter_rest(): pl.pallas_call(functools.partial(scatter_kernel, shape, orders), in_specs...  62.4 us
    pallas_call x1, Pallas kernels, feed_forward_both(): pl.pallas_call(functools.partial(feed_kernel, cuts, shards, units), grid_...  49.9 us
    ppermute x7, waiting for transfers between devices, on_device(): lax.ppermute(grad_window[(halo - k) * block:(halo - k + 1) * block], 'hea...  35.6 us
    ppermute x10, waiting for transfers between devices, send(): lax.ppermute(sent, axis, bit_pairs(self.shape[axis], bit))  23.9 us
    pallas_call x2, Pallas kernels, fold(): pl.pallas_call(functools.partial(fold_kernel, [len(scatter.terms) for sca...  18.4 us
    unnamed x70, local copies, waits for them, and re-layouts  14.4 us
  transfers between devices with their start and end apart: 18, of which 9 were waited for; matrix products, arithmetic and copies ran while one was open for 5% of the time, Pallas kernels for 16%

profile of v5, /device:TPU:0, one launch (start us, length us, event | category | flops | bytes accessed | tf_op | source)
XLA Modules:
  0.0 542.3 jit_solution(15900692661318955760)
XLA Ops:
  0.7 0.8 reshape.213.gain_ref
  2.2 0.9 select_reduce_fusion.1
  3.1 0.9 broadcast_in_dim.3.token_ref.weight_ref
  4.0 1.4 multiply_sine_fusion
  5.5 1.7 copy-done.2
  7.2 0.8 copy-done.12
  8.0 1.8 prepare.1
  9.8 1.1 copy-done.4
  11.0 0.9 copy-done.11
  11.9 2.2 pack.1
  14.1 177.3 %attend_gather.1 = (bf16[2,512,768]{2,1,0:T(8,128)(2,1)}, f32[2,8,1,768]{3,2,1,0:T(1,128)}, bf16[2,768,1024]{2,1,0:T(8,128)(2,1)}, bf16[2,2,2,2,2,448,256]{6,5,4...) custom-call(bf16[768,1024]{1,0:T(8,128)(2,1)} %copy-done.4, ...), custom_call_target="tpu_custom_call" | custom-call | tf_op jit(solution)/shard_map/attend_gather/pallas_call | solution.py:877
  191.5 3.1 copy-done
  194.5 1.4 copy-done.1
  195.9 2.4 join.1
  198.4 1.7 copy-done.8
  200.0 1.1 copy-done.14
  201.2 49.9 %feed_forward_both.1 = (f32[768,1024]{1,0:T(8,128)}, f32[768,1024]{1,0:T(8,128)}, bf16[2,8,1056,256]{3,2,1,0:T(8,128)(2,1)}, bf16[2,8,1056,256]{3,2,1,0:T(8,128)(2,1)}) custom-call(s32[1]{0:T(128)} %bitcast.6.side_ref, bf16[768,1024]{1,0:T(8,128)(2,1)} %copy-done.14, bf16[768,1024]{1,0:T(8,128)(2,1)} %cotangent_ref.3, ...), custom_call_target="tpu_custom_call" | custom-call | flops 40000000000 | bytes 50000000 | tf_op jit(solution)/shard_map/feed_forward_both/pallas_call | solution.py:986
  251.4 11.0 %middle.1 = (bf16[768,1024]{1,0:T(8,128)(2,1)}, f32[768,1024]{1,0:T(8,128)}, bf16[4,8,128,256]{3,2,1,0:T(8,128)(2,1)}, f32[1,1024]{1,0:T(1,128)S(1)}, bf16[512,7...) custom-call(f32[768,1024]{1,0:T(8,128)} %copy-done.8, f32[768,1024]{1,0:T(8,128)} %get-tuple-element.82.feed_ref, ...), custom_call_target="tpu_custom_call" | custom-call | tf_op jit(solution)/shard_map/middle/pallas_call | solution.py:579
  264.1 2.4 copy_bitcast_fusion.1
  266.5 0.9 constant_dynamic-slice_fusion.1
  267.4 11.8 %fold.2 = (bf16[8,528,256]{2,1,0:T(8,128)(2,1)}, bf16[8,528,256]{2,1,0:T(8,128)(2,1)}, bf16[8,528,256]{2,1,0:T(8,128)(2,1)}, bf16[8,528,256]{2,1,0:T(8,128)(2,1)}) custom-call(s32[2]{0:T(128)} %pad_add_fusion.2.side_ref, bf16[1,2,8,1056,256]{4,3,2,1,0:T(8,128)(2,1)} %bitcast.128, bf16[1,2,8,1056,256]{4,3,2,1,0:T(8,128)(2,1)} %bitcast.14.refs_1_.refs_3_, ...), custom_call_target="tpu_custom_call" | custom-call | tf_op jit(solution)/shard_map/fold/pallas_call | solution.py:1101
  279.2 1.5 collective-permute-start.1
  280.7 3.1 collective-permute-start.2
  283.8 31.3 %attend_backward.2 = (bf16[2560,640]{1,0:T(8,128)(2,1)}, f32[768,1024]{1,0:T(8,128)}, bf16[4,8,320,128]{3,2,1,0:T(8,128)(2,1)}) custom-call(s32[2]{0:T(128)} %pad_add_fusion.place_ref, bf16[2,768,1024]{2,1,0:T(8,128)(2,1)} %get-tuple-element.85.q_ref, bf16[2560,640]{1,0:T(8,128)(2,1)} %get-tuple-element.86.window_ref, bf16[4,8,448,256]{3,2,1,0:T(8,128)(2,1)} %bitcast.116, ...), custom_call_target="tpu_custom_call" | custom-call | flops 40000000000 | bytes 30000000 | tf_op jit(solution)/shard_map/attend_backward/pallas_call | solution.py:421
  315.1 2.6 copy_bitcast_fusion
  317.8 0.9 constant_dynamic-slice_fusion
  318.7 9.9 %collective-permute-done.1 = bf16[2,2,2,528,256]{4,3,2,1,0:T(8,128)(2,1)} collective-permute-done((bf16[2,2,2,528,256]{4,3,2,1,0:T(8,128)(2,1)}, bf16[2,2,2,528,256]{4,3,2,1,0:T(8,128)(2,1)}, u32[]{:S(2)}, u32[]{:S(2)}) %collective-permute-start.1) | collective-permute-done | bytes 2162720 | tf_op jit(solution)/shard_map/ppermute | solution.py:1062
  328.6 2.9 collective-permute-done.2
  331.5 6.6 %fold.3 = (bf16[4,528,256]{2,1,0:T(8,128)(2,1)}, bf16[4,528,256]{2,1,0:T(8,128)(2,1)}, bf16[4,528,256]{2,1,0:T(8,128)(2,1)}, bf16[4,528,256]{2,1,0:T(8,128)(2,1)}) custom-call(s32[2]{0:T(128)} %pad_add_fusion.1.side_ref, bf16[4,2,1,528,256]{4,3,2,1,0:T(8,128)(2,1)} %bitcast.133, bf16[4,2,1,528,256]{4,3,2,1,0:T(8,128)(2,1)} %bitcast.20.refs_1_.refs_3_, ...), custom_call_target="tpu_custom_call" | custom-call | tf_op jit(solution)/shard_map/fold/pallas_call | solution.py:1101
  338.2 2.4 copy.63
  340.6 1.7 collective-permute-start.3
  342.3 5.4 collective-permute-start.4
  348.2 33.3 %attend_backward.3 = (bf16[2560,640]{1,0:T(8,128)(2,1)}, f32[768,1024]{1,0:T(8,128)}, bf16[4,8,320,128]{3,2,1,0:T(8,128)(2,1)}) custom-call(s32[2]{0:T(128)} %pad_add_fusion.place_ref, bf16[2,768,1024]{2,1,0:T(8,128)(2,1)} %get-tuple-element.85.q_ref, bf16[2560,640]{1,0:T(8,128)(2,1)} %get-tuple-element.86.window_ref, bf16[4,8,448,256]{3,2,1,0:T(8,128)(2,1)} %bitcast.118, ...), custom_call_target="tpu_custom_call" | custom-call | flops 40000000000 | bytes 30000000 | tf_op jit(solution)/shard_map/attend_backward/pallas_call | solution.py:421
  381.5 2.6 fusion.21
  384.1 1.4 collective-permute-start.7
  385.6 1.3 collective-permute-start.8
  386.9 2.1 fusion.5
  389.0 1.3 collective-permute-start.9
  390.3 2.1 fusion.7
  392.3 1.3 collective-permute-start.10
  393.6 2.1 fusion.6
  395.8 7.3 %collective-permute-done.7.refs_0_ = bf16[256,640]{1,0:T(8,128)(2,1)S(1)} collective-permute-done((bf16[256,640]{1,0:T(8,128)(2,1)S(1)}, bf16[256,640]{1,0:T(8,128)(2,1)S(1)}, u32[]{:S(2)}, u32[]{:S(2)}) %collective-permute-start.7) | collective-permute-done | bytes 327712 | tf_op jit(solution)/shard_map/ppermute | solution.py:1339
  403.0 1.3 collective-permute-start.11
  404.3 5.7 %collective-permute-done.8.refs_1_ = bf16[256,640]{1,0:T(8,128)(2,1)S(1)} collective-permute-done((bf16[256,640]{1,0:T(8,128)(2,1)S(1)}, bf16[256,640]{1,0:T(8,128)(2,1)S(1)}, u32[]{:S(2)}, u32[]{:S(2)}) %collective-permute-start.8) | collective-permute-done | bytes 327712 | tf_op jit(solution)/shard_map/ppermute | solution.py:1339
  410.1 0.7 copy-done.29
  410.8 1.3 collective-permute-start.12
  412.1 1.7 collective-permute-start.13
  413.8 2.1 fusion.1
  417.0 10.4 %collective-permute-done.10.refs_3_ = bf16[256,640]{1,0:T(8,128)(2,1)S(1)} collective-permute-done((bf16[256,640]{1,0:T(8,128)(2,1)S(1)}, bf16[256,640]{1,0:T(8,128)(2,1)S(1)}, u32[]{:S(2)}, u32[]{:S(2)}) %collective-permute-start.10) | collective-permute-done | bytes 327712 | tf_op jit(solution)/shard_map/ppermute | solution.py:1339
  428.3 1.7 copy.73
  429.9 4.6 collective-permute-done.11.refs_4_
  434.5 7.0 %collective-permute-done.12.refs_5_ = bf16[256,640]{1,0:T(8,128)(2,1)} collective-permute-done((bf16[256,640]{1,0:T(8,128)(2,1)}, bf16[256,640]{1,0:T(8,128)(2,1)}, u32[]{:S(2)}, u32[]{:S(2)}) %collective-permute-start.12) | collective-permute-done | bytes 327712 | tf_op jit(solution)/shard_map/ppermute | solution.py:1339
  441.6 11.0 %finish.1 = (f32[768,1024]{1,0:T(8,128)}, bf16[1024,640]{1,0:T(8,128)(2,1)}, f32[1,1024]{1,0:T(1,128)}) custom-call(bf16[2560,640]{1,0:T(8,128)(2,1)} %get-tuple-element.106.dwindow_ref, bf16[768,1024]{1,0:T(8,128)(2,1)} %tokens_ref.5, bf16[768,1024]{1,0:T(8,128)(2,1)} %copy-done.4, f32[768,1024]{1,0:T(8,128)} %get-tuple-element.114.dnormed_ref, ...), custom_call_target="tpu_custom_call" | custom-call | tf_op jit(solution)/shard_map/finish/pallas_call | solution.py:636
  453.5 1.6 copy.68
  455.3 1.5 add_convert_fusion.5
  456.8 1.5 fusion.2.refs_1_
  458.3 1.3 fusion.3.refs_0_
  459.6 11.1 %collective-permute-done.17 = bf16[2,2,2,320,128]{4,3,1,0,2:T(8,128)(2,1)S(1)} collective-permute-done((bf16[2,2,2,320,128]{4,3,1,0,2:T(8,128)(2,1)S(1)}, bf16[2,2,2,320,128]{4,3,1,0,2:T(8,128)(2,1)S(1)}, u32[]{:S(2)}, u32[]{:S(2)}) %collective-permute-start.17) | collective-permute-done | bytes 655392 | tf_op jit(solution)/shard_map/ppermute | solution.py:1062
  470.7 1.3 add_convert_fusion
  472.1 62.4 %scatter_rest.1 = (f32[528,256]{1,0:T(8,128)S(1)}, f32[528,256]{1,0:T(8,128)S(1)}, f32[128,256]{1,0:T(8,128)S(1)}, f32[32,640]{1,0:T(8,128)S(1)}, f32[16,128]{1,...) custom-call(bf16[2,528,256]{2,1,0:T(8,128)(2,1)S(1)} %fusion.3.refs_0_, ...), custom_call_target="tpu_custom_call" | custom-call | tf_op jit(solution)/shard_map/scatter_rest/pallas_call | solution.py:1180
  537.0 0.8 copy.76
  537.8 0.7 copy.75
  538.7 0.7 reshape.240
  540.1 1.0 fusion.22
  (102 shorter events, 10.5 us)
Async XLA Ops:
  0.6 4.8 copy-start.7
  2.1 7.7 %copy-start.13 = (bf16[1,1024]{1,0:T(2,128)(2,1)}, bf16[1,1024]{1,0:T(2,128)(2,1)S(1)}, u32[]{:S(2)}) copy-start(bf16[1,1024]{1,0:T(2,128)(2,1)S(1)} %reshape.214.gain_ref) | copy-start | bytes 6148
  5.5 4.3 copy-start.5
  5.5 4.3 copy-start.6
  5.5 1.7 copy-start.2
  7.2 0.8 copy-start.12
  9.8 1.2 copy-start.4
  11.0 0.9 copy-start.11
  14.1 177.3 %copy-start.3 = (bf16[768,1024]{1,0:T(8,128)(2,1)S(1)}, bf16[768,1024]{1,0:T(8,128)(2,1)}, u32[]{:S(2)}) copy-start(bf16[768,1024]{1,0:T(8,128)(2,1)} %tokens_ref.5) | copy-start | bytes 4718596
  191.5 3.1 copy-start
  194.5 1.4 copy-start.1
  198.3 1.7 copy-start.8
  200.0 1.1 copy-start.14
  201.2 50.2 %copy-start.9 = (f32[768,1]{1,0:T(8,128)S(1)}, f32[768,1]{1,0:T(8,128)}, u32[]{:S(2)}) copy-start(f32[768,1]{1,0:T(8,128)} %broadcast_in_dim.3.token_ref.weight_ref) | copy-start | bytes 9220
  201.2 50.2 %copy-start.10 = (bf16[768,1024]{1,0:T(8,128)(2,1)S(1)}, bf16[768,1024]{1,0:T(8,128)(2,1)}, u32[]{:S(2)}) copy-start(bf16[768,1024]{1,0:T(8,128)(2,1)} %cotangent_ref.3) | copy-start | bytes 4718596
  251.0 16.4 %collective-permute-start = (bf16[2,8,1056,256]{3,2,1,0:T(8,128)(2,1)}, bf16[2,8,1056,256]{3,2,1,0:T(8,128)(2,1)}, u32[]{:S(2)}, u32[]{:S(2)}) collective-permute-start(bf16[2,8,1056,256]{3,2,1,0:T(8,128)(2,1)} %get-tuple-element.89), channel_id=1, source_target_pairs={{0,8},{8,0},{16,24},{24,16},{1,9},{9,1},{17,25},{25,17},{2,10},{10... | collective-permute-start | bytes 25952264 | tf_op jit(solution)/shard_map/ppermute | solution.py:1308
  262.4 5.0 copy-start.15
  262.4 5.0 copy-start.16
  262.4 4.1 copy-start.20
  279.2 49.5 %collective-permute-start.1 = (bf16[2,2,2,528,256]{4,3,2,1,0:T(8,128)(2,1)}, bf16[2,2,2,528,256]{4,3,2,1,0:T(8,128)(2,1)}, u32[]{:S(2)}, u32[]{:S(2)}) collective-permute-start(bf16[2,2,2,528,256]{4,3,2,1,0:T(8,128)(2,1)} %bitcast.157), channel_id=1, source_target_pairs={{0,16},{8,24},{16,0},{24,8},{1,17},{9,25},{17,1},{25,9},{2,18},{10... | collective-permute-start | bytes 6488072 | tf_op jit(solution)/shard_map/ppermute | solution.py:1062
  280.7 50.8 %collective-permute-start.2 = (bf16[2,2,2,528,256]{4,3,2,1,0:T(8,128)(2,1)}, bf16[2,2,2,528,256]{4,3,2,1,0:T(8,128)(2,1)}, u32[]{:S(2)}, u32[]{:S(2)}) collective-permute-start(bf16[2,2,2,528,256]{4,3,2,1,0:T(8,128)(2,1)} %bitcast.156), channel_id=1, source_target_pairs={{0,1},{1,0},{2,3},{3,2},{4,5},{5,4},{6,7},{7,6},{8,9},{9,8},{10,11... | collective-permute-start | bytes 6488072 | tf_op jit(solution)/shard_map/ppermute | solution.py:1062
  315.1 2.6 copy-start.18
  338.2 4.2 copy-start.32
  340.6 51.7 %collective-permute-start.3 = (bf16[2,2,528,256]{3,2,0,1:T(8,128)(2,1)}, bf16[2,2,528,256]{3,2,0,1:T(8,128)(2,1)}, u32[]{:S(2)}, u32[]{:S(2)}) collective-permute-start(bf16[2,2,528,256]{3,2,0,1:T(8,128)(2,1)} %copy.63), channel_id=1, source_target_pairs={{0,1},{1,0},{2,3},{3,2},{4,5},{5,4},{6,7},{7,6},{8,9},{9,8},{10,11... | collective-permute-start | bytes 3244040 | tf_op jit(solution)/shard_map/ppermute | solution.py:1062
  342.3 46.6 %collective-permute-start.4 = (bf16[2,2,528,256]{3,2,1,0:T(8,128)(2,1)S(1)}, bf16[2,2,528,256]{3,2,1,0:T(8,128)(2,1)}, u32[]{:S(2)}, u32[]{:S(2)}) collective-permute-start(bf16[2,2,528,256]{3,2,1,0:T(8,128)(2,1)S(1)} %bitcast.158), channel_id=1, source_target_pairs={{0,2},{1,3},{2,0},{3,1},{4,6},{5,7},{6,4},{7,5},{8,10},{9,11},{10,... | collective-permute-start | bytes 3244040 | tf_op jit(solution)/shard_map/ppermute | solution.py:1062
  347.7 37.8 %collective-permute-start.5 = (bf16[2,2,2,2,128,256]{5,4,1,2,3,0:T(8,128)(2,1)}, bf16[2,2,2,2,128,256]{5,4,1,2,3,0:T(8,128)(2,1)}, u32[]{:S(2)}, u32[]{:S(2)}) collective-permute-start(bf16[2,2,2,2,128,256]{5,4,1,2,3,0:T(8,128)(2,1)} %copy_bitcast_fusion.1), channel_id=1, source_target_pairs={{0,8},{8,0},{16,24},{24,16},{1,9},{9,1},{17,25},{25,17},{2,10},{10... | collective-permute-start | bytes 3145736 | tf_op jit(solution)/shard_map/ppermute | solution.py:1062
  347.7 64.4 %collective-permute-start.6 = (bf16[2,2,2,2,320,128]{5,4,1,0,2,3:T(8,128)(2,1)}, bf16[2,2,2,2,320,128]{5,4,1,0,2,3:T(8,128)(2,1)}, u32[]{:S(2)}, u32[]{:S(2)}) collective-permute-start(bf16[2,2,2,2,320,128]{5,4,1,0,2,3:T(8,128)(2,1)} %copy_bitcast_fusion), channel_id=1, source_target_pairs={{0,8},{8,0},{16,24},{24,16},{1,9},{9,1},{17,25},{25,17},{2,10},{10... | collective-permute-start | bytes 3932168 | tf_op jit(solution)/shard_map/ppermute | solution.py:1062
  384.1 6.1 %copy-start.24 = (bf16[4,528,256]{2,1,0:T(8,128)(2,1)S(1)}, bf16[4,528,256]{2,1,0:T(8,128)(2,1)}, u32[]{:S(2)}) copy-start(bf16[4,528,256]{2,1,0:T(8,128)(2,1)} %get-tuple-element.109) | copy-start | bytes 3244036
  384.1 18.9 %collective-permute-start.7 = (bf16[256,640]{1,0:T(8,128)(2,1)S(1)}, bf16[256,640]{1,0:T(8,128)(2,1)S(1)}, u32[]{:S(2)}, u32[]{:S(2)}) collective-permute-start(bf16[256,640]{1,0:T(8,128)(2,1)S(1)} %get-tuple-element.166), channel_id=1, source_target_pairs={{1,0},{2,1},{3,2},{4,3},{5,4},{6,5},{7,6},{9,8},{10,9},{11,10},{12... | collective-permute-start | bytes 983048 | tf_op jit(solution)/shard_map/ppermute | solution.py:1339
  385.6 24.5 %collective-permute-start.8 = (bf16[256,640]{1,0:T(8,128)(2,1)S(1)}, bf16[256,640]{1,0:T(8,128)(2,1)S(1)}, u32[]{:S(2)}, u32[]{:S(2)}) collective-permute-start(bf16[256,640]{1,0:T(8,128)(2,1)S(1)} %get-tuple-element.165), channel_id=1, source_target_pairs={{1,0},{2,1},{4,3},{5,4},{6,5},{7,6},{9,8},{10,9},{12,11},{13,12},{... | collective-permute-start | bytes 983048 | tf_op jit(solution)/shard_map/ppermute | solution.py:1339
  386.9 6.8 %copy-start.22 = (bf16[4,528,256]{2,1,0:T(8,128)(2,1)S(1)}, bf16[4,528,256]{2,1,0:T(8,128)(2,1)}, u32[]{:S(2)}) copy-start(bf16[4,528,256]{2,1,0:T(8,128)(2,1)} %get-tuple-element.107) | copy-start | bytes 3244036
  389.0 27.5 %collective-permute-start.9 = (bf16[256,640]{1,0:T(8,128)(2,1)S(1)}, bf16[256,640]{1,0:T(8,128)(2,1)S(1)}, u32[]{:S(2)}, u32[]{:S(2)}) collective-permute-start(bf16[256,640]{1,0:T(8,128)(2,1)S(1)} %get-tuple-element.164), channel_id=1, source_target_pairs={{1,0},{2,1},{4,3},{5,4},{7,6},{9,8},{10,9},{12,11},{13,12},{15,14}... | collective-permute-start | bytes 983048 | tf_op jit(solution)/shard_map/ppermute | solution.py:1339
  392.3 35.1 %collective-permute-start.10 = (bf16[256,640]{1,0:T(8,128)(2,1)S(1)}, bf16[256,640]{1,0:T(8,128)(2,1)S(1)}, u32[]{:S(2)}, u32[]{:S(2)}) collective-permute-start(bf16[256,640]{1,0:T(8,128)(2,1)S(1)} %get-tuple-element.163), channel_id=1, source_target_pairs={{2,0},{4,2},{5,3},{7,5},{10,8},{12,10},{13,11},{15,13},{18,16},{20... | collective-permute-start | bytes 983048 | tf_op jit(solution)/shard_map/ppermute | solution.py:1339
  393.6 34.6 %copy-start.17 = (bf16[4,8,320,128]{3,2,1,0:T(8,128)(2,1)S(1)}, bf16[4,8,320,128]{3,2,1,0:T(8,128)(2,1)}, u32[]{:S(2)}) copy-start(bf16[4,8,320,128]{3,2,1,0:T(8,128)(2,1)} %get-tuple-element.124) | copy-start | bytes 7864324
  403.0 7.0 %copy-start.28 = (bf16[256,640]{1,0:T(8,128)(2,1)}, bf16[256,640]{1,0:T(8,128)(2,1)S(1)}, u32[]{:S(2)}) copy-start(bf16[256,640]{1,0:T(8,128)(2,1)S(1)} %collective-permute-done.7.refs_0_) | copy-start | bytes 983044
  403.0 31.5 %collective-permute-start.11 = (bf16[256,640]{1,0:T(8,128)(2,1)}, bf16[256,640]{1,0:T(8,128)(2,1)}, u32[]{:S(2)}, u32[]{:S(2)}) collective-permute-start(bf16[256,640]{1,0:T(8,128)(2,1)} %get-tuple-element.162), channel_id=1, source_target_pairs={{2,0},{5,3},{7,5},{10,8},{13,11},{15,13},{18,16},{21,19},{23,21},{... | collective-permute-start | bytes 983048 | tf_op jit(solution)/shard_map/ppermute | solution.py:1339
  410.1 0.7 copy-start.29
  410.8 30.8 %collective-permute-start.12 = (bf16[256,640]{1,0:T(8,128)(2,1)}, bf16[256,640]{1,0:T(8,128)(2,1)}, u32[]{:S(2)}, u32[]{:S(2)}) collective-permute-start(bf16[256,640]{1,0:T(8,128)(2,1)} %get-tuple-element.161), channel_id=1, source_target_pairs={{2,0},{5,3},{10,8},{13,11},{18,16},{21,19},{26,24},{29,27}} | collective-permute-start | bytes 983048 | tf_op jit(solution)/shard_map/ppermute | solution.py:1339
  412.1 29.5 %collective-permute-start.13 = (bf16[256,640]{1,0:T(8,128)(2,1)}, bf16[256,640]{1,0:T(8,128)(2,1)}, u32[]{:S(2)}, u32[]{:S(2)}) collective-permute-start(bf16[256,640]{1,0:T(8,128)(2,1)} %get-tuple-element.160), channel_id=1, source_target_pairs={{5,2},{13,10},{21,18},{29,26}} | collective-permute-start | bytes 983048 | tf_op jit(solution)/shard_map/ppermute | solution.py:1339
  416.4 11.0 %copy-start.30 = (bf16[256,640]{1,0:T(8,128)(2,1)}, bf16[256,640]{1,0:T(8,128)(2,1)S(1)}, u32[]{:S(2)}) copy-start(bf16[256,640]{1,0:T(8,128)(2,1)S(1)} %collective-permute-done.9.refs_2_) | copy-start | bytes 983044
  416.4 38.8 %collective-permute-start.16 = (bf16[2,2,2,128,256]{4,3,0,1,2:T(8,128)(2,1)}, bf16[2,2,2,128,256]{4,3,0,1,2:T(8,128)(2,1)}, u32[]{:S(2)}, u32[]{:S(2)}) collective-permute-start(bf16[2,2,2,128,256]{4,3,0,1,2:T(8,128)(2,1)} %fusion.5), channel_id=1, source_target_pairs={{0,16},{8,24},{16,0},{24,8},{1,17},{9,25},{17,1},{25,9},{2,18},{10... | collective-permute-start | bytes 1572872 | tf_op jit(solution)/shard_map/ppermute | solution.py:1062
  427.4 0.7 copy-start.31
  427.4 29.4 %collective-permute-start.15 = (bf16[2,528,256]{2,1,0:T(8,128)(2,1)}, bf16[2,528,256]{2,1,0:T(8,128)(2,1)}, u32[]{:S(2)}, u32[]{:S(2)}) collective-permute-start(bf16[2,528,256]{2,1,0:T(8,128)(2,1)} %fusion.7), channel_id=1, source_target_pairs={{0,16},{8,24},{16,0},{24,8},{1,17},{9,25},{17,1},{25,9},{2,18},{10... | collective-permute-start | bytes 1622024 | tf_op jit(solution)/shard_map/ppermute | solution.py:1062
  428.3 6.3 %copy-start.27 = (bf16[2,528,256]{2,1,0:T(8,128)(2,1)S(1)}, bf16[2,528,256]{2,1,0:T(8,128)(2,1)}, u32[]{:S(2)}) copy-start(bf16[2,528,256]{2,1,0:T(8,128)(2,1)} %fusion.6) | copy-start | bytes 1622020
  434.5 23.8 %collective-permute-start.14 = (bf16[2,528,256]{2,1,0:T(8,128)(2,1)S(1)}, bf16[2,528,256]{2,1,0:T(8,128)(2,1)S(1)}, u32[]{:S(2)}, u32[]{:S(2)}) collective-permute-start(bf16[2,528,256]{2,1,0:T(8,128)(2,1)S(1)} %copy-done.27), channel_id=1, source_target_pairs={{0,2},{1,3},{2,0},{3,1},{4,6},{5,7},{6,4},{7,5},{8,10},{9,11},{10,... | collective-permute-start | bytes 1622024 | tf_op jit(solution)/shard_map/ppermute | solution.py:1062
  453.5 1.7 copy-start.26
  453.5 1.8 copy-start.21
  455.1 1.7 copy-start.25
  455.2 15.6 %collective-permute-start.17 = (bf16[2,2,2,320,128]{4,3,1,0,2:T(8,128)(2,1)S(1)}, bf16[2,2,2,320,128]{4,3,1,0,2:T(8,128)(2,1)S(1)}, u32[]{:S(2)}, u32[]{:S(2)}) collective-permute-start(bf16[2,2,2,320,128]{4,3,1,0,2:T(8,128)(2,1)S(1)} %copy-done.26), channel_id=1, source_target_pairs={{0,1},{1,0},{2,3},{3,2},{4,5},{5,4},{6,7},{7,6},{8,9},{9,8},{10,11... | collective-permute-start | bytes 1966088 | tf_op jit(solution)/shard_map/ppermute | solution.py:1062
  456.8 1.6 copy-start.23
  458.3 12.4 %copy-start.19 = (bf16[2,1,2,2,1,320,128]{6,5,4,3,2,1,0:T(8,128)(2,1)S(1)}, bf16[2,1,2,2,1,320,128]{6,5,4,3,2,1,0:T(8,128)(2,1)}, u32[]{:S(2)}) copy-start(bf16[2,1,2,2,1,320,128]{6,5,4,3,2,1,0:T(8,128)(2,1)} %get-tuple-element.167) | copy-start | bytes 1966084
